TPU v7x, 32 devices: a whole 2x2x4 slice. The times are simulated.
32 devices in a mesh: dp: 16 (over z, y, x), outer: 2 (over core).
Axes of the slice: x: 2, y: 2, z: 4, core: 2. Of those that a mesh axis runs over, the one named last changes fastest.
Arguments:
- tokens: bfloat16 [64, 128, 2048], P(('dp', 'outer')), may hold values from -6 to 6
- starts: int32 [64, 128], P(('dp', 'outer')), may hold values 0 or 1
- w_query: bfloat16 [2048, 2048], P(('dp', 'outer')), may hold values from -0.125 to 0.125
- w_key: bfloat16 [2048, 2048], P(('dp', 'outer')), may hold values from -0.125 to 0.125
- w_value: bfloat16 [2048, 2048], P(('dp', 'outer')), may hold values from -0.125 to 0.125
- w_gate_out: bfloat16 [2048, 2048], P(('dp', 'outer')), may hold values from -0.125 to 0.125
- w_out: bfloat16 [2048, 2048], P(('dp', 'outer')), may hold values from -0.25 to 0.25
- w_forget_down: bfloat16 [2048, 16], P(('dp', 'outer')), may hold values from -0.125 to 0.125
- w_forget_up: bfloat16 [16, 256], P(None, ('dp', 'outer')), may hold values from -3 to 3
- norm_attn: bfloat16 [2048], P(('dp', 'outer')), may hold values from 0.5 to 1.5
- norm_head: bfloat16 [512], P(('dp', 'outer')), may hold values from 0.5 to 1.5
- norm_mlp: bfloat16 [2048], P(('dp', 'outer')), may hold values from 0.5 to 1.5
- w_gate: bfloat16 [2048, 5632], P(('dp', 'outer')), may hold values from -0.125 to 0.125
- w_up: bfloat16 [2048, 5632], P(('dp', 'outer')), may hold values from -0.125 to 0.125
- w_down: bfloat16 [5632, 2048], P(('dp', 'outer')), may hold values from -0.15625 to 0.15625
- cotangent: bfloat16 [64, 128, 2048], P(('dp', 'outer')), may hold values from -6 to 6
Outputs:
- mixed: bfloat16 [64, 128, 2048], P(('dp', 'outer'))
- tokens_grad: bfloat16 [64, 128, 2048], P(('dp', 'outer'))
- grad_query: float32 [2048, 2048], P(('dp', 'outer'))
- grad_key: float32 [2048, 2048], P(('dp', 'outer'))
- grad_value: float32 [2048, 2048], P(('dp', 'outer'))
- grad_gate_out: float32 [2048, 2048], P(('dp', 'outer'))
- grad_out: float32 [2048, 2048], P(('dp', 'outer'))
- grad_forget_down: float32 [2048, 16], P(('dp', 'outer'))
- grad_forget_up: float32 [16, 256], P(None, ('dp', 'outer'))
- grad_norm_attn: float32 [2048], P(('dp', 'outer'))
- grad_norm_head: float32 [512], P(('dp', 'outer'))
- grad_norm_mlp: float32 [2048], P(('dp', 'outer'))
- grad_gate: float32 [2048, 5632], P(('dp', 'outer'))
- grad_up: float32 [2048, 5632], P(('dp', 'outer'))
- grad_down: float32 [5632, 2048], P(('dp', 'outer'))
All inputs are finite; a program needn't handle non-finite values. No bound on the sum of `starts` on one device may be relied on, other than what follows from the above.
Results may differ from a plain program's by a relative error of at most 0.015.
Values may be sent and summed in bfloat16 or wider, within the bound.
A program may use at most 512 MiB of HBM per device.

v0:
```python
import functools

import jax
import jax.numpy as jnp
from jax import lax
from jax.experimental import pallas as pl
from jax.experimental.pallas import tpu as pltpu
from jax.sharding import Mesh, PartitionSpec as P

HEADS = 4
HEAD = 512
SLOTS = 64
TP = 4
ALL = ("z", "t", "c")
F32 = jnp.float32
BF16 = jnp.bfloat16
SPAN = 80.0


def mm(a, b, dims):
    return lax.dot_general(a, b, (dims, ((), ())), preferred_element_type=F32)


NN, NT, TN = ((1,), (0,)), ((1,), (1,)), ((0,), (0,))


def split(a):
    high = a.astype(BF16)
    return high, (a - high.astype(F32)).astype(BF16)


def mm3(a, b, dims):
    ah, al = split(a)
    bh, bl = split(b)
    return mm(ah, bh, dims) + (mm(ah, bl, dims) + mm(al, bh, dims))


def mm_exact(mask, b, dims):
    b1, rest = split(b)
    b2 = rest
    b3 = (b - b1.astype(F32) - b2.astype(F32)).astype(BF16)
    return mm(mask, b1, dims) + (mm(mask, b2, dims) + mm(mask, b3, dims))


def swish_parts(v):
    sig = 1.0 / (1.0 + jnp.exp(-v))
    return v * sig, sig * (1.0 + v * (1.0 - sig))


def gates(f_low, wfu):
    f_pre = mm(f_low, wfu, NN)
    soft = jnp.log(1.0 + jnp.exp(-jnp.abs(f_pre)))
    log_f = (jnp.minimum(f_pre, 0.0) - soft) * 0.125
    return f_pre, log_f


def lower_tri(n, kind=BF16):
    rows = lax.broadcasted_iota(jnp.int32, (n, n), 0)
    cols = lax.broadcasted_iota(jnp.int32, (n, n), 1)
    return rows >= cols


def column(a, j):
    picked = lax.broadcasted_iota(jnp.int32, a.shape, 1) == j
    return jnp.sum(jnp.where(picked, a, 0.0), axis=1, keepdims=True)


def row(a, j):
    picked = lax.broadcasted_iota(jnp.int32, a.shape, 0) == j
    return jnp.sum(jnp.where(picked, a, 0.0), axis=0, keepdims=True)


def gap(total, j):
    return jnp.exp(jnp.minimum(total - row(total, j), 0.0))


def softmax(scores):
    e = jnp.exp(scores - jnp.max(scores, axis=1, keepdims=True))
    return e / jnp.sum(e, axis=1, keepdims=True)


def far_near(total):
    mid = 0.5 * total[-1:]
    return jnp.exp(total - mid), jnp.exp(mid - total)


def sum_over_j(mats, total, unit, fast, dest):
    n = total.shape[0]

    @pl.when(fast)
    def _():
        near, far = far_near(total)
        got = mm3(jnp.concatenate(mats, axis=0), far * unit, NN)
        for i, d in enumerate(dest):
            d[...] = got[i * n:(i + 1) * n] * near

    @pl.when(jnp.logical_not(fast))
    def _():
        for d in dest:
            d[...] = jnp.zeros_like(total)

        def step(j, _):
            e = gap(total, j) * row(unit, j)
            for d, m in zip(dest, mats):
                d[...] += column(m, j) * e
            return 0

        lax.fori_loop(0, n, step, 0)


def sum_over_m(probs, total, unit, fast, dest):
    n = total.shape[0]

    @pl.when(fast)
    def _():
        near, far = far_near(total)
        got = mm3(jnp.concatenate([p * near for p in probs], axis=0), far * unit, NT)
        for i, d in enumerate(dest):
            d[...] = got[i * n:(i + 1) * n]

    @pl.when(jnp.logical_not(fast))
    def _():
        cols = lax.broadcasted_iota(jnp.int32, (n, n), 1)

        def step(j, _):
            e = gap(total, j) * row(unit, j)
            for d, p in zip(dest, probs):
                d[...] = jnp.where(cols == j, jnp.sum(p * e, axis=1, keepdims=True), d[...])
            return 0

        lax.fori_loop(0, n, step, 0)


def sum_over_t(mats, probs, total, fast, dest):
    n = total.shape[0]

    @pl.when(fast)
    def _():
        near, far = far_near(total)
        got = mm3(jnp.concatenate(mats, axis=0), jnp.concatenate([p * near for p in probs], axis=0), TN)
        dest[...] = got * far

    @pl.when(jnp.logical_not(fast))
    def _():
        rows = lax.broadcasted_iota(jnp.int32, total.shape, 0)

        def step(j, _):
            e = gap(total, j)
            s = sum(column(m, j) * p for m, p in zip(mats, probs))
            dest[...] = jnp.where(rows == j, jnp.sum(s * e, axis=0, keepdims=True), dest[...])
            return 0

        lax.fori_loop(0, n, step, 0)


def mixer_forward(pre_ref, f_low_ref, wfu_ref, doc_col_ref, doc_row_ref, score_ref, mix_ref):
    pre = pre_ref[...]
    q, q_slope = swish_parts(pre[:, :HEAD])
    k, k_slope = swish_parts(pre[:, HEAD:2 * HEAD])
    q, k, v = q.astype(BF16), k.astype(BF16), pre[:, 2 * HEAD:3 * HEAD].astype(BF16)
    n = q.shape[0]
    tri = lower_tri(n)
    keep = tri & (doc_col_ref[0] == doc_row_ref[0])
    inner = jnp.where(keep, mm(q, k, NT) * HEAD ** -0.5, 0.0)
    f_pre, log_f = gates(f_low_ref[...], wfu_ref[...])
    total = mm_exact(tri.astype(BF16), log_f, NN)
    unit = 1.0 - jnp.exp(log_f)
    fast = jnp.min(total[-1:]) > -SPAN
    return q, k, v, q_slope, k_slope, keep, inner, f_pre, log_f, total, unit, fast


def forward_kernel(pre_ref, f_low_ref, wfu_ref, gain_ref, doc_col_ref, doc_row_ref, act_ref, score_ref, mix_ref):
    q, k, v, _, _, keep, inner, _, _, total, unit, fast = mixer_forward(
        pre_ref, f_low_ref, wfu_ref, doc_col_ref, doc_row_ref, score_ref, mix_ref)
    sum_over_j([inner], total, unit, fast, [score_ref])
    probs = softmax(score_ref[...])
    sum_over_m([probs], total, unit, fast, [mix_ref])
    mixing = jnp.where(keep, mix_ref[...], 0.0).astype(BF16)
    out = mm(mixing, v, NN)
    scale = lax.rsqrt(jnp.mean(out * out, axis=1, keepdims=True) + 1e-06)
    gate, _ = swish_parts(pre_ref[:, 3 * HEAD:])
    act_ref[...] = (out * scale * gain_ref[...] * gate).astype(BF16)


def backward_kernel(pre_ref, f_low_ref, wfu_ref, gain_ref, doc_col_ref, doc_row_ref, d_act_ref, *refs):
    d_pre_ref, d_f_ref, d_low_ref, g_gain_ref, score_ref, d_p_ref, mix_ref, d_inner_ref, k_ref = refs[-9:]
    q, k, v, q_slope, k_slope, keep, inner, f_pre, log_f, total, unit, fast = mixer_forward(
        pre_ref, f_low_ref, wfu_ref, doc_col_ref, doc_row_ref, score_ref, mix_ref)
    sum_over_j([inner], total, unit, fast, [score_ref])
    scores = score_ref[...]
    probs = softmax(scores)
    sum_over_m([probs], total, unit, fast, [mix_ref])
    mixing = jnp.where(keep, mix_ref[...], 0.0).astype(BF16)
    out = mm(mixing, v, NN)

    scale = lax.rsqrt(jnp.mean(out * out, axis=1, keepdims=True) + 1e-06)
    gain = gain_ref[...]
    gate, gate_slope = swish_parts(pre_ref[:, 3 * HEAD:])
    d_act = d_act_ref[...].astype(F32)
    d_gate = d_act * out * scale * gain * gate_slope
    d_norm = d_act * gate
    g_gain = jnp.sum(d_norm * out * scale, axis=0, keepdims=True)

    @pl.when(pl.program_id(0) == 0)
    def _():
        g_gain_ref[...] = jnp.zeros_like(g_gain_ref)

    g_gain_ref[...] += g_gain
    d_norm = d_norm * gain
    d_out = scale * (d_norm - out * (scale * scale) * jnp.mean(d_norm * out, axis=1, keepdims=True))
    d_out = d_out.astype(BF16)

    d_mix = jnp.where(keep, mm(d_out, v, NT), 0.0)
    d_v = mm(mixing, d_out, TN)
    sum_over_j([d_mix], total, unit, fast, [d_p_ref])
    d_p = d_p_ref[...]
    d_score = probs * (d_p - jnp.sum(probs * d_p, axis=1, keepdims=True))
    sum_over_m([d_score], total, unit, fast, [d_inner_ref])
    d_inner = jnp.where(keep, d_inner_ref[...], 0.0).astype(BF16)
    sum_over_t([d_mix, inner], [probs, d_score], total, fast, k_ref)
    k_sum = k_ref[...]
    d_total = probs * d_p + d_score * scores - unit * k_sum
    n = q.shape[0]
    tri = lower_tri(n).astype(BF16)
    d_log = mm_exact(tri, d_total, TN) - jnp.exp(log_f) * k_sum
    d_f = (d_log * (0.125 / (1.0 + jnp.exp(f_pre)))).astype(BF16)
    d_f_ref[...] = d_f
    d_low_ref[...] = mm(d_f, wfu_ref[...], NT).astype(BF16)
    d_q = mm(d_inner, k, NN) * HEAD ** -0.5
    d_k = mm(d_inner, q, TN) * HEAD ** -0.5
    d_pre_ref[:, :HEAD] = (d_q * q_slope).astype(BF16)
    d_pre_ref[:, HEAD:2 * HEAD] = (d_k * k_slope).astype(BF16)
    d_pre_ref[:, 2 * HEAD:3 * HEAD] = d_v.astype(BF16)
    d_pre_ref[:, 3 * HEAD:] = d_gate.astype(BF16)


def mixer_specs(length, rank, first=0):
    return [
        pl.BlockSpec((length, 4 * HEAD), lambda i: (i + first, 0)),
        pl.BlockSpec((length, rank), lambda i: (i + first, 0)),
        pl.BlockSpec((rank, SLOTS), lambda i: (0, 0)),
        pl.BlockSpec((1, HEAD), lambda i: (0, 0)),
        pl.BlockSpec((1, length, 1), lambda i: (i + first, 0, 0)),
        pl.BlockSpec((1, 1, length), lambda i: (i + first, 0, 0)),
    ]


def slots_forward(pre, f_low, wfu, gain, docs):
    count, length = docs.shape
    tm = pltpu.VMEM((length, SLOTS), F32)
    tj = pltpu.VMEM((length, length), F32)
    return pl.pallas_call(
        forward_kernel,
        out_shape=jax.ShapeDtypeStruct((count * length, HEAD), BF16),
        grid=(count,),
        in_specs=mixer_specs(length, f_low.shape[1]),
        out_specs=pl.BlockSpec((length, HEAD), lambda i: (i, 0)),
        scratch_shapes=[tm, tj],
        compiler_params=pltpu.CompilerParams(vmem_limit_bytes=32 << 20),
        name="slots_forward",
    )(pre, f_low, wfu, gain, docs[:, :, None], docs[:, None, :])


def slots_backward(pre, f_low, wfu, gain, docs, d_act, first, steps, begun=()):
    count, length = docs.shape
    rank = f_low.shape[1]
    tm = pltpu.VMEM((length, SLOTS), F32)
    tj = pltpu.VMEM((length, length), F32)
    block = lambda width: pl.BlockSpec((length, width), lambda i: (i + first, 0))
    return pl.pallas_call(
        backward_kernel,
        out_shape=(
            jax.ShapeDtypeStruct((count * length, 4 * HEAD), BF16),
            jax.ShapeDtypeStruct((count * length, SLOTS), BF16),
            jax.ShapeDtypeStruct((count * length, rank), BF16),
            jax.ShapeDtypeStruct((1, HEAD), F32),
        ),
        grid=(steps,),
        in_specs=mixer_specs(length, rank, first) + [block(HEAD)] + [pl.BlockSpec(memory_space=pl.ANY)] * len(begun),
        out_specs=(block(4 * HEAD), block(SLOTS), block(rank), pl.BlockSpec((1, HEAD), lambda i: (0, 0))),
        scratch_shapes=[tm, tm, tj, tj, tm],
        input_output_aliases={7 + i: i for i in range(len(begun))},
        compiler_params=pltpu.CompilerParams(vmem_limit_bytes=32 << 20),
        name="slots_backward",
    )(pre, f_low, wfu, gain, docs[:, :, None], docs[:, None, :], d_act, *begun)


def place(index, cs):
    return (index // (TP * cs), (index // cs) % TP, index % cs)


def greet_all(n, cs, me):
    barrier = pltpu.get_barrier_semaphore()

    def greet(step, _):
        pl.semaphore_signal(barrier, inc=1, device_id=place((me + step) % n, cs), device_id_type=pl.DeviceIdType.MESH)
        return 0

    lax.fori_loop(1, n, greet, 0)
    pl.semaphore_wait(barrier, n - 1)


def my_index(cs):
    return (lax.axis_index("z") * TP + lax.axis_index("t")) * cs + lax.axis_index("c")


def chip_peer(t, step):
    high, low = t // 2, t % 2
    return (high + step // 2) % 2 * 2 + (low + step % 2) % 2


def share_kernel(n, cs, x_ref, o_ref, send_sem, recv_sem):
    me = my_index(cs)
    greet_all(n, cs, me)

    def send(step, _):
        pltpu.make_async_remote_copy(
            src_ref=x_ref, dst_ref=o_ref.at[me], send_sem=send_sem, recv_sem=recv_sem,
            device_id=place((me + step) % n, cs), device_id_type=pl.DeviceIdType.MESH).start()
        return 0

    lax.fori_loop(1, n, send, 0)
    o_ref[me] = x_ref[...]
    others = o_ref.at[pl.ds(0, n - 1)]
    pltpu.make_async_copy(others, others, recv_sem).wait()
    pltpu.make_async_copy(others, others, send_sem).wait()


def share(x, n, cs, ident):
    return pl.pallas_call(
        functools.partial(share_kernel, n, cs),
        out_shape=jax.ShapeDtypeStruct((n,) + x.shape, x.dtype),
        in_specs=[pl.BlockSpec(memory_space=pltpu.VMEM)],
        out_specs=pl.BlockSpec(memory_space=pltpu.VMEM),
        scratch_shapes=[pltpu.SemaphoreType.DMA, pltpu.SemaphoreType.DMA],
        compiler_params=pltpu.CompilerParams(collective_id=ident, has_side_effects=True, vmem_limit_bytes=32 << 20),
        name="share_small",
    )(x)


def spread_kernel(count, *refs):
    srcs, (out, own_sem, send_sem, recv_sem) = refs[:count], refs[count:]
    z, t, c = (lax.axis_index(a) for a in ALL)
    greet_plane(z, t, c)
    width = srcs[0].shape[1] // TP

    def block(i, to, at):
        src = srcs[i].at[:, pl.ds(pl.multiple_of(to * width, 128), width)]
        return src, out.at[at, :, pl.ds(i * width, width)]

    copies = []
    for step in (3, 1, 2):
        peer = chip_peer(t, step)
        for i in range(count):
            src, dst = block(i, peer, t)
            copies.append(pltpu.make_async_remote_copy(
                src_ref=src, dst_ref=dst, send_sem=send_sem.at[step - 1, i], recv_sem=recv_sem.at[step - 1, i],
                device_id=(z, peer, c), device_id_type=pl.DeviceIdType.MESH))
            copies[-1].start()
    for i in range(count):
        src, dst = block(i, t, t)
        copies.append(pltpu.make_async_copy(src, dst, own_sem.at[i]))
        copies[-1].start()
    for copy in copies:
        copy.wait()


def spread(weights, ident):
    rows, columns = weights[0].shape
    anywhere = pl.BlockSpec(memory_space=pl.ANY)
    return pl.pallas_call(
        functools.partial(spread_kernel, len(weights)),
        out_shape=jax.ShapeDtypeStruct((TP, rows, len(weights) * columns // TP), weights[0].dtype),
        in_specs=[anywhere] * len(weights),
        out_specs=anywhere,
        scratch_shapes=block_sems(len(weights)),
        compiler_params=pltpu.CompilerParams(collective_id=ident, has_side_effects=True),
        name="spread",
    )(*weights)


def greet_plane(z, t, c):
    barrier = pltpu.get_barrier_semaphore()
    for step in (1, 2, 3):
        pl.semaphore_signal(barrier, inc=1, device_id=(z, chip_peer(t, step), c), device_id_type=pl.DeviceIdType.MESH)
    pl.semaphore_wait(barrier, TP - 1)


LANES = 128


def unit_runs(piece, units):
    cuts = sorted(set(range(0, units, piece)) | set(range(0, units, LANES)) | {units})
    return [(low, high - low) for low, high in zip(cuts, cuts[1:])]


def packed_at(unit, up):
    return unit // LANES * 2 * LANES + up * LANES + unit % LANES


def natural_at(unit, piece, chip):
    return (unit // piece * TP + chip) * piece + unit % piece


def spread_ff_kernel(piece, parts, wg_ref, wu_ref, *refs):
    outs, (packed, own_sem, send_sem, recv_sem) = refs[:len(parts)], refs[len(parts):]
    z, t, c = (lax.axis_index(a) for a in ALL)
    greet_plane(z, t, c)
    for j in range(TP):
        for up, w in enumerate((wg_ref, wu_ref)):
            for unit, count in unit_runs(piece, packed.shape[2] // 2):
                at, source = packed_at(unit, up), natural_at(unit, piece, j)
                packed[j, :, at:at + count] = w[:, source:source + count]
    copies = []
    for step in (3, 1, 2):
        peer = chip_peer(t, step)
        for i, ((low, high), out) in enumerate(zip(parts, outs)):
            copies.append(pltpu.make_async_remote_copy(
                src_ref=packed.at[peer, :, low:high], dst_ref=out.at[t], send_sem=send_sem.at[step - 1, i],
                recv_sem=recv_sem.at[step - 1, i], device_id=(z, peer, c), device_id_type=pl.DeviceIdType.MESH))
            copies[-1].start()
    for i, ((low, high), out) in enumerate(zip(parts, outs)):
        copies.append(pltpu.make_async_copy(packed.at[t, :, low:high], out.at[t], own_sem.at[i]))
        copies[-1].start()
    for copy in copies:
        copy.wait()


def spread_ff(w_gate, w_up, piece, parts, ident):
    rows, units = w_gate.shape
    fast = pl.BlockSpec(memory_space=pltpu.VMEM)
    anywhere = pl.BlockSpec(memory_space=pl.ANY)
    return pl.pallas_call(
        functools.partial(spread_ff_kernel, piece, parts),
        out_shape=tuple(jax.ShapeDtypeStruct((TP, rows, high - low), w_gate.dtype) for low, high in parts),
        in_specs=[fast, fast],
        out_specs=(anywhere,) * len(parts),
        scratch_shapes=[pltpu.VMEM((TP, rows, 2 * units // TP), w_gate.dtype)] + block_sems(len(parts)),
        compiler_params=pltpu.CompilerParams(collective_id=ident, has_side_effects=True, vmem_limit_bytes=32 << 20),
        name="spread_ff",
    )(w_gate, w_up)


def send_blocks(sources, targets, own_sem, send_sem, recv_sem):
    z, t, c = (lax.axis_index(a) for a in ALL)
    copies = []
    for step in (3, 1, 2):
        peer = chip_peer(t, step)
        for i, (source, target) in enumerate(zip(sources, targets)):
            copies.append(pltpu.make_async_remote_copy(
                src_ref=source.at[peer], dst_ref=target.at[t], send_sem=send_sem.at[step - 1, i],
                recv_sem=recv_sem.at[step - 1, i], device_id=(z, peer, c), device_id_type=pl.DeviceIdType.MESH))
            copies[-1].start()
    for i, (source, target) in enumerate(zip(sources, targets)):
        copies.append(pltpu.make_async_copy(source.at[t], target.at[t], own_sem.at[i]))
        copies[-1].start()
    return copies


def block_sems(count):
    return [pltpu.SemaphoreType.DMA((count,))] + [pltpu.SemaphoreType.DMA((TP - 1, count))] * 2


def ff_moves(piece, units, parts):
    moves = []
    for j in range(TP):
        for up in (0, 1):
            for unit, count in unit_runs(piece, units):
                at = packed_at(unit, up)
                source = [i for i, (low, high) in enumerate(parts) if low <= at < high][0]
                moves.append((up, natural_at(unit, piece, j), source, j, at - parts[source][0], count))
    return moves


def widen_kernel(moves, sources, *refs):
    for out, at, source, j, start, width in moves:
        refs[sources + out][:, at:at + width] = refs[source][j, :, start:start + width].astype(F32)


def widen(xs, moves, count, columns):
    fast = pl.BlockSpec(memory_space=pltpu.VMEM)
    return pl.pallas_call(
        functools.partial(widen_kernel, moves, len(xs)),
        out_shape=tuple(jax.ShapeDtypeStruct((xs[0].shape[1], columns), F32) for _ in range(count)),
        in_specs=[fast] * len(xs),
        out_specs=tuple(fast for _ in range(count)),
        compiler_params=pltpu.CompilerParams(vmem_limit_bytes=32 << 20),
        name="widen",
    )(*xs)


def finish_kernel(n, cs, x_ref, blocks_ref, o_ref, back_ref, got_ref, send_sem, recv_sem, *block_sem):
    me = my_index(cs)
    greet_all(n, cs, me)

    def send(step, _):
        peer = (me + step) % n
        pltpu.make_async_remote_copy(
            src_ref=x_ref.at[peer], dst_ref=got_ref.at[me], send_sem=send_sem, recv_sem=recv_sem,
            device_id=place(peer, cs), device_id_type=pl.DeviceIdType.MESH).start()
        return 0

    lax.fori_loop(1, n, send, 0)
    copies = send_blocks([blocks_ref], [back_ref], *block_sem)
    got_ref[me] = x_ref[me]
    others = got_ref.at[pl.ds(0, n - 1)]
    pltpu.make_async_copy(others, others, recv_sem).wait()
    pltpu.make_async_copy(others, others, send_sem).wait()
    o_ref[...] = jnp.sum(got_ref[...], axis=0)
    for copy in copies:
        copy.wait()


def finish(x, blocks, n, cs):
    anywhere = pl.BlockSpec(memory_space=pl.ANY)
    fast = pl.BlockSpec(memory_space=pltpu.VMEM)
    return pl.pallas_call(
        functools.partial(finish_kernel, n, cs),
        out_shape=(jax.ShapeDtypeStruct(x.shape[1:], x.dtype), jax.ShapeDtypeStruct(blocks.shape, blocks.dtype)),
        in_specs=[fast, anywhere],
        out_specs=(fast, anywhere),
        scratch_shapes=[pltpu.VMEM(x.shape, x.dtype), pltpu.SemaphoreType.DMA, pltpu.SemaphoreType.DMA] + block_sems(1),
        compiler_params=pltpu.CompilerParams(collective_id=1, has_side_effects=True, vmem_limit_bytes=32 << 20),
        name="finish",
    )(x, blocks)


def pack_rows(parts, unit):
    flat = jnp.concatenate(parts, axis=-1)
    size = flat.shape[-1]
    padded = -(-size // (unit * 128)) * unit * 128
    flat = jnp.pad(flat, [(0, 0)] * (flat.ndim - 1) + [(0, padded - size)])
    return flat.reshape(flat.shape[:-1] + (padded // 128, 128))


def cut(flat, sizes):
    at, pieces = 0, []
    for size in sizes:
        pieces.append(flat[..., at:at + size])
        at += size
    return pieces


def relay(p_ref, o_ref, got1, pass2, got2, sems, subs, middle, shared=True, beside=None, plane=False, cores=False):
    z, t, c = (lax.axis_index(a) for a in ALL)
    peers = {step: (z, chip_peer(t, step), c) for step in (1, 2)}
    barrier = pltpu.get_barrier_semaphore()
    met = [peers[1], peers[2]] + [(z, chip_peer(t, 3), c)] * plane + [(z, t, 1 - c)] * cores
    for device in met:
        pl.semaphore_signal(barrier, inc=1, device_id=device, device_id_type=pl.DeviceIdType.MESH)
    pl.semaphore_wait(barrier, len(met))
    send_sem, recv_sem = sems
    half = p_ref.shape[1] // 2
    size = half // subs
    ways = ((1, 2), (2, 1))
    copies = []

    def start(src, dst, step, slot, i):
        copy = pltpu.make_async_remote_copy(
            src_ref=src, dst_ref=dst, send_sem=send_sem.at[slot, i], recv_sem=recv_sem.at[slot, i],
            device_id=peers[step], device_id_type=pl.DeviceIdType.MESH)
        copy.start()
        copies.append(copy)
        return copy

    def part(w, i):
        return pl.ds(w * half + i * size, size)

    def local(i):
        return pl.ds(i * size, size)

    first = [[[start(p_ref.at[near if j == 0 else 3, part(w, i)], got1.at[w, j, local(i)], near, 2 * w + j, i)
               for j in (0, 1)] for w, (near, far) in enumerate(ways)] for i in range(subs)]
    second, third, fourth = [None] * subs, [None] * subs, []
    for i in range(subs + 2):
        if i < subs:
            second[i] = []
            for w, (near, far) in enumerate(ways):
                first[i][w][1].wait_recv()
                both = p_ref[far, part(w, i)].astype(F32) + got1[w, 1, local(i)].astype(F32)
                pass2[w, local(i)] = both.astype(BF16)
                second[i].append(start(pass2.at[w, local(i)], got2.at[w, local(i)], far, 4 + w, i))
        if 1 <= i <= subs:
            k = i - 1
            third[k] = []
            for w in (0, 1):
                first[k][w][0].wait_recv()
                second[k][w].wait_recv()
                total = p_ref[0, part(w, k)].astype(F32) + got1[w, 0, local(k)].astype(F32)
                total = total + got2[w, local(k)].astype(F32)
                rows = middle(w * half + k * size, size, total)
                if not shared:
                    o_ref[part(w, k)] = rows
                    continue
                o_ref[0, part(w, k)] = rows
                third[k].append([start(o_ref.at[0, part(w, k)], o_ref.at[step, part(w, k)], step, 5 + 2 * w + step, k)
                                 for step in (1, 2)])
        if beside is not None:
            beside(i)
        if i >= 2 and shared:
            k = i - 2
            for w, (near, far) in enumerate(ways):
                third[k][w][far - 1].wait_recv()
                fourth.append(start(o_ref.at[far, part(w, k)], o_ref.at[3, part(w, k)], near, 10 + w, k))
    for copy in copies:
        copy.wait_send()
    for k in range(subs if shared else 0):
        for w, (near, far) in enumerate(ways):
            third[k][w][near - 1].wait_recv()
    for copy in fourth:
        copy.wait_recv()


def forward_relay_kernel(unit, subs, p_ref, x_ref, gain_ref, o_ref, resid_ref, got1, pass2, got2, ordered, *sems):
    def middle(at, size, total):
        rows = pl.ds(at, size)
        resid = total + x_ref[rows].astype(F32)
        resid_ref[rows] = resid
        normed = resid * lax.rsqrt(jnp.mean(resid * resid, axis=1, keepdims=True) + 1e-06) * gain_ref[...]
        half = normed.shape[1] // 2
        for j in range(half // unit):
            for k in (0, 1):
                ordered[:, k * half + j * unit:k * half + (j + 1) * unit] = normed[:, (2 * j + k) * unit:(2 * j + k + 1) * unit]
        return ordered[...].astype(BF16)

    relay(p_ref, o_ref, got1, pass2, got2, sems, subs, middle)


def norm_backward(unit, resid_ref, gain_ref, g_gain_ref, ordered, finish):
    g_gain_ref[...] = jnp.zeros_like(g_gain_ref)

    def middle(at, size, total):
        rows = pl.ds(at, size)
        half = total.shape[1] // 2
        for j in range(half // unit):
            for k in (0, 1):
                ordered[:, (2 * j + k) * unit:(2 * j + k + 1) * unit] = total[:, k * half + j * unit:k * half + (j + 1) * unit]
        d = ordered[...]
        resid = resid_ref[rows].astype(F32)
        scale = lax.rsqrt(jnp.mean(resid * resid, axis=1, keepdims=True) + 1e-06)
        unit_resid = resid * scale
        g_gain_ref[...] += jnp.sum(d * unit_resid, axis=0, keepdims=True)
        d = d * gain_ref[...]
        d = scale * (d - unit_resid * jnp.mean(d * unit_resid, axis=1, keepdims=True))
        return finish(rows, d)

    return middle


def backward_relay_kernel(unit, subs, parts, p_ref, resid_ref, cot_ref, gain_ref, *refs):
    hidden_hbm, (branch_hbm, down_hbm, o_ref, d_resid_ref, g_gain_ref, g_down_hbm, terms_hbm, *refs) = refs[:parts], refs[parts:]
    (got1, pass2, got2, ordered, send_sem, recv_sem, hidden, branch, down, g_down, g_other, terms,
     in_sem, out_sem, core_send, core_recv) = refs
    z, t, c = (lax.axis_index(a) for a in ALL)
    loads, at = [], 0
    for source in hidden_hbm:
        loads.append((source, hidden.at[:, at:at + source.shape[1]]))
        at += source.shape[1]
    loads += [(branch_hbm, branch), (down_hbm, down)]
    loads = [pltpu.make_async_copy(src, dst, in_sem.at[i]) for i, (src, dst) in enumerate(loads)]
    for copy in loads:
        copy.start()
    width = branch.shape[1] // subs
    _, zs, cs, count, _ = g_down.shape
    stores, crossings = [], []

    def beside(i):
        if i == 0:
            for copy in loads:
                copy.wait()
        cols = slice(i * width, (i + 1) * width)
        if i < subs:
            g = mm(hidden[...], branch[:, cols], TN).astype(BF16)
            for j in range(zs):
                for k in range(cs):
                    at = (j * cs + k) * count
                    g_down[i, j, k] = g[at:at + count]
            crossings.append(pltpu.make_async_remote_copy(
                src_ref=g_down.at[i, :, 1 - c], dst_ref=g_other.at[i], send_sem=core_send.at[i], recv_sem=core_recv.at[i],
                device_id=(z, t, 1 - c), device_id_type=pl.DeviceIdType.MESH))
            crossings[i].start()
            terms[i] = mm(hidden[...], down[:, cols], NN).astype(BF16)
            stores.append(pltpu.make_async_copy(terms.at[i], terms_hbm.at[:, cols], out_sem.at[0, i]))
            stores[-1].start()
        if 1 <= i <= subs:
            k = i - 1
            crossings[k].wait()
            g_other[k] = (g_other[k].astype(F32) + g_down[k, :, c].astype(F32)).astype(BF16)
            stores.append(pltpu.make_async_copy(
                g_other.at[k], g_down_hbm.at[:, :, slice(k * width, (k + 1) * width)], out_sem.at[1, k]))
            stores[-1].start()

    def finish(rows, d):
        d = d + cot_ref[rows].astype(F32)
        d_resid_ref[rows] = d
        return d.astype(BF16)

    middle = norm_backward(unit, resid_ref, gain_ref, g_gain_ref, ordered, finish)
    relay(p_ref, o_ref, got1, pass2, got2, (send_sem, recv_sem), subs, middle, beside=beside, cores=True)
    for copy in stores:
        copy.wait()


def settle_kernel(unit, count, subs, p_ref, x_ref, d_resid_ref, gain_ref, d_low_ref, f_low_ref, d_f_ref, g_head_ref,
                  g_mlp_ref, act_hbm, d_attn_hbm, h_hbm, *refs):
    blocks, refs = refs[:count], refs[count:]
    o_ref, flat_ref, g_out_hbm, refs = refs[0], refs[1], refs[2], refs[3:]
    returned, refs = refs[:count], refs[count:]
    (got1, pass2, got2, ordered, send_sem, recv_sem, own_sem, back_send, back_recv,
     act, d_attn, h, g_out, g_sum, g_gain_ref, in_sem, core_send, core_recv, swap_own, swap_send, swap_recv) = refs
    z, t, c = (lax.axis_index(a) for a in ALL)
    loads = [pltpu.make_async_copy(src, dst, in_sem.at[i])
             for i, (src, dst) in enumerate([(act_hbm, act), (d_attn_hbm, d_attn), (h_hbm, h)])]
    for copy in loads:
        copy.start()
    crossing = pltpu.make_async_remote_copy(
        src_ref=g_out.at[:, :, 1 - c], dst_ref=g_sum, send_sem=core_send, recv_sem=core_recv,
        device_id=(z, t, 1 - c), device_id_type=pl.DeviceIdType.MESH)
    copies = []
    n = flat_ref.shape[0]
    deep, _, cs, rows, D = g_out.shape
    rank = f_low_ref.shape[1]

    def beside(i):
        if i == 0:
            copies.extend(send_blocks(blocks, returned, own_sem, back_send, back_recv))
            for copy in loads:
                copy.wait()
            for low in range(0, D, D // 4):
                cols = slice(low, low + D // 4)
                g = mm(act[...], d_attn[:, cols], TN).astype(BF16)
                for j in range(deep):
                    for k in range(TP):
                        for m in range(cs):
                            at = ((j * TP + k) * cs + m) * rows
                            g_out[j, k, m, :, cols] = g[at:at + rows]
            crossing.start()
        if i == 1:
            crossing.wait()
            g_sum[...] = (g_sum[...].astype(F32) + g_out[:, :, c].astype(F32)).astype(BF16)
            for step in (3, 1, 2):
                peer = chip_peer(t, step)
                copies.append(pltpu.make_async_remote_copy(
                    src_ref=g_sum.at[:, peer], dst_ref=g_out_hbm.at[t], send_sem=swap_send.at[step - 1],
                    recv_sem=swap_recv.at[step - 1], device_id=(z, peer, c), device_id_type=pl.DeviceIdType.MESH))
                copies[-1].start()
            copies.append(pltpu.make_async_copy(g_sum.at[:, t], g_out_hbm.at[t], swap_own))
            copies[-1].start()
        if i == 2:
            flat_ref[...] = jnp.zeros_like(flat_ref)
            g_fd = mm(d_low_ref[...], h[...], TN)
            g_fu = mm(f_low_ref[...], d_f_ref[...], TN)
            zs = n // (TP * cs)
            each, wide = n // TP, g_fu.shape[1] * TP // n
            heads = g_head_ref.shape[1] // n
            for j in range(n):
                at = ((j % cs) * zs + j // (TP * cs)) * TP + j // cs % TP
                flat_ref[j, :rank, :unit] = g_fd[:, at * unit:(at + 1) * unit]
                flat_ref[j, rank:rank + 1, unit:unit + heads] = g_head_ref[:, j * heads:(j + 1) * heads]
                flat_ref[j, rank + 1:rank + 2, :unit] = g_mlp_ref[:, j * unit:(j + 1) * unit]
            for j in range(each):
                flat_ref[t * each + j, :rank, unit:unit + wide] = g_fu[:, j * wide:(j + 1) * wide]

    def finish(at, d):
        return (d + d_resid_ref[at]).astype(BF16)

    middle = norm_backward(unit, x_ref, gain_ref, g_gain_ref, ordered, finish)
    relay(p_ref, o_ref, got1, pass2, got2, (send_sem, recv_sem), subs, middle, False, beside, True, True)
    for j in range(n):
        flat_ref[j, rank:rank + 1, :unit] = g_gain_ref[:, j * unit:(j + 1) * unit]
    for copy in copies:
        copy.wait()


def relay_scratch(count, D, subs):
    half, size = count // 2, count // 2 // subs
    return [
        pltpu.VMEM((2, 2, half, D), BF16),
        pltpu.VMEM((2, half, D), BF16),
        pltpu.VMEM((2, half, D), BF16),
        pltpu.VMEM((size, D), F32),
        pltpu.SemaphoreType.DMA((12, subs)),
        pltpu.SemaphoreType.DMA((12, subs)),
    ]


SUBS = 4


def relay_forward(p, x, gain, unit, ident):
    _, count, D = p.shape
    fast = pl.BlockSpec(memory_space=pltpu.VMEM)
    return pl.pallas_call(
        functools.partial(forward_relay_kernel, unit, SUBS),
        out_shape=(jax.ShapeDtypeStruct(p.shape, BF16), jax.ShapeDtypeStruct(x.shape, F32)),
        in_specs=[fast] * 3,
        out_specs=(fast,) * 2,
        scratch_shapes=relay_scratch(count, D, SUBS),
        compiler_params=pltpu.CompilerParams(collective_id=ident, has_side_effects=True, vmem_limit_bytes=40 << 20),
        name="relay_forward",
    )(p, x, gain)


def relay_backward(p, resid, cot, gain, hidden, branch, down, unit, zs, cs, ident):
    _, count, D = p.shape
    tokens = hidden[0].shape[0]
    units = down.shape[0]
    width = D // SUBS
    each = units // (zs * cs)
    fast = pl.BlockSpec(memory_space=pltpu.VMEM)
    anywhere = pl.BlockSpec(memory_space=pl.ANY)
    return pl.pallas_call(
        functools.partial(backward_relay_kernel, unit, SUBS, len(hidden)),
        out_shape=(
            jax.ShapeDtypeStruct(p.shape, BF16),
            jax.ShapeDtypeStruct(resid.shape, F32),
            jax.ShapeDtypeStruct((1, D), F32),
            jax.ShapeDtypeStruct((zs, each, D), BF16),
            jax.ShapeDtypeStruct((tokens, D), BF16),
        ),
        in_specs=[fast] * 4 + [anywhere] * (len(hidden) + 2),
        out_specs=(fast,) * 3 + (anywhere,) * 2,
        scratch_shapes=relay_scratch(count, D, SUBS) + [
            pltpu.VMEM((tokens, units), BF16),
            pltpu.VMEM(branch.shape, BF16),
            pltpu.VMEM(down.shape, BF16),
            pltpu.VMEM((SUBS, zs, cs, each, width), BF16),
            pltpu.VMEM((SUBS, zs, each, width), BF16),
            pltpu.VMEM((SUBS, tokens, width), BF16),
            pltpu.SemaphoreType.DMA((len(hidden) + 2,)),
            pltpu.SemaphoreType.DMA((2, SUBS)),
            pltpu.SemaphoreType.DMA((SUBS,)),
            pltpu.SemaphoreType.DMA((SUBS,)),
        ],
        compiler_params=pltpu.CompilerParams(collective_id=ident, has_side_effects=True, vmem_limit_bytes=60 << 20),
        name="relay_backward",
    )(p, resid, cot, gain, *hidden, branch, down)


def settle(p, x, d_resid, gain, d_low, f_low, d_f, g_head, g_mlp, act, d_attn, h, blocks, unit, zs, cs, ident):
    _, count, D = p.shape
    fast = pl.BlockSpec(memory_space=pltpu.VMEM)
    anywhere = pl.BlockSpec(memory_space=pl.ANY)
    number = len(blocks)
    deep = zs // TP
    rank = f_low.shape[1]
    return pl.pallas_call(
        functools.partial(settle_kernel, unit, number, SUBS),
        out_shape=(
            jax.ShapeDtypeStruct(p.shape[1:], BF16),
            jax.ShapeDtypeStruct((zs * TP * cs, rank + 8, LANES), F32),
            jax.ShapeDtypeStruct((TP, deep, unit, D), BF16),
        ) + tuple(jax.ShapeDtypeStruct(b.shape, b.dtype) for b in blocks),
        in_specs=[fast] * 9 + [anywhere] * (3 + number),
        out_specs=(fast,) * 2 + (anywhere,) * (1 + number),
        scratch_shapes=relay_scratch(count, D, SUBS) + block_sems(number) + [
            pltpu.VMEM(act.shape, BF16),
            pltpu.VMEM(d_attn.shape, BF16),
            pltpu.VMEM(h.shape, BF16),
            pltpu.VMEM((deep, TP, cs, unit, D), BF16),
            pltpu.VMEM((deep, TP, unit, D), BF16),
            pltpu.VMEM((1, D), F32),
            pltpu.SemaphoreType.DMA((3,)),
            pltpu.SemaphoreType.DMA,
            pltpu.SemaphoreType.DMA,
            pltpu.SemaphoreType.DMA,
            pltpu.SemaphoreType.DMA((TP - 1,)),
            pltpu.SemaphoreType.DMA((TP - 1,)),
        ],
        compiler_params=pltpu.CompilerParams(collective_id=ident, has_side_effects=True, vmem_limit_bytes=56 << 20),
        name="settle",
    )(p, x, d_resid, gain, d_low, f_low, d_f, g_head, g_mlp, act, d_attn, h, *blocks)


def ff_kernel(tile, hm_ref, gu_ref, d_hidden_ref, hidden_ref, d_gu_ref):
    for at in range(0, hm_ref.shape[0], tile):
        rows = slice(at, at + tile)
        pre = mm(hm_ref[rows, :], gu_ref[...], NN)
        gate, up = pre[:, :LANES], pre[:, LANES:]
        sig = 0.5 * jnp.tanh(0.5 * gate) + 0.5
        act = gate * sig
        d_hidden = d_hidden_ref[rows, :]
        hidden_ref[rows, :] = (act * up).astype(BF16)
        d_gu_ref[rows, :LANES] = (d_hidden * up * (sig + act * (1.0 - sig))).astype(BF16)
        d_gu_ref[rows, LANES:] = (d_hidden * act).astype(BF16)


def ff_forward(hm, gu, d_hidden, first):
    tokens, D = hm.shape
    columns = gu.shape[1]
    wide = pl.BlockSpec((tokens, 2 * LANES), lambda j: (0, j))
    return pl.pallas_call(
        functools.partial(ff_kernel, 256),
        out_shape=(jax.ShapeDtypeStruct((tokens, columns // 2), BF16), jax.ShapeDtypeStruct((tokens, columns), BF16)),
        grid=(columns // (2 * LANES),),
        in_specs=[
            pl.BlockSpec((tokens, D), lambda j: (0, 0)),
            pl.BlockSpec((D, 2 * LANES), lambda j: (0, j)),
            pl.BlockSpec((tokens, LANES), lambda j: (0, j + first)),
        ],
        out_specs=(pl.BlockSpec((tokens, LANES), lambda j: (0, j)), wide),
        compiler_params=pltpu.CompilerParams(vmem_limit_bytes=48 << 20),
        name="feed_forward",
    )(hm, gu, d_hidden)


def d_hm_kernel(tile, count, *refs):
    grads, weights, o_ref = refs[:count], refs[count:2 * count], refs[2 * count]
    for at in range(0, o_ref.shape[0], tile):
        rows = slice(at, at + tile)
        o_ref[rows, :] = sum(mm(g[rows, :], w[...], NT) for g, w in zip(grads, weights)).astype(BF16)


def d_hm_product(grads, weights):
    tokens, D = grads[0].shape[0], weights[0].shape[0]
    width = 256
    return pl.pallas_call(
        functools.partial(d_hm_kernel, 256, len(grads)),
        out_shape=jax.ShapeDtypeStruct((tokens, D), BF16),
        grid=(D // width,),
        in_specs=[pl.BlockSpec(g.shape, lambda j: (0, 0)) for g in grads]
        + [pl.BlockSpec((width, w.shape[1]), lambda j: (j, 0)) for w in weights],
        out_specs=pl.BlockSpec((tokens, width), lambda j: (0, j)),
        compiler_params=pltpu.CompilerParams(vmem_limit_bytes=48 << 20),
        name="d_hm",
    )(*grads, *weights)


def send_t(x, step):
    return lax.ppermute(x, "t", [(i, i ^ step) for i in range(TP)])


def send_c(x):
    return lax.ppermute(x, "c", [(0, 1), (1, 0)])


def gather_t_begin(x):
    return send_t(x, 1), send_t(x, 2)


def gather_t_end(x, one, two):
    half = x.shape[0] // 2
    return jnp.concatenate([x, one, two, send_t(two[:half], 1), send_t(one[half:], 2)], axis=0)


def scatter_t_send(x):
    count = x.shape[0] // TP
    half = count // 2
    p = [(x[k * count:k * count + half], x[k * count + half:(k + 1) * count]) for k in range(TP)]
    return send_t(jnp.concatenate([p[1][0], p[3][0]], axis=0), 1), send_t(jnp.concatenate([p[2][1], p[3][1]], axis=0), 2)


def scatter_t_middle(x, got):
    count = x.shape[0] // TP
    half = count // 2
    first, second = got

    def add(low, v):
        return x[low:low + half].astype(F32) + v.astype(F32)

    on_a = add(2 * count, first[half:]).astype(BF16)
    on_b = add(count + half, second[half:]).astype(BF16)
    part = jnp.concatenate([add(0, first[:half]), add(half, second[:half])], axis=0)
    return part, (on_a, on_b)


def scatter_t_pass(passed):
    return send_t(passed[0], 2), send_t(passed[1], 1)


def swap_t(x):
    t = lax.axis_index("t")

    def block(a, j):
        return lax.dynamic_index_in_dim(a, j, 0, keepdims=False)

    got = jnp.stack([block(x, t)] + [send_t(block(x, t ^ k), k) for k in (1, 2, 3)])
    return jnp.stack([block(got, t ^ j) for j in range(TP)])


def dot(left, right):
    return mm(left, right, NN)


def dot_nt(left, right):
    return mm(left, right, NT)


def dot_tn(left, right):
    return mm(left, right, TN)


def after(x, *others):
    return lax.optimization_barrier((x,) + others)[:2]


def rms_norm(v, gain):
    return v * lax.rsqrt(jnp.mean(v * v, axis=-1, keepdims=True) + 1e-06) * gain


def swiglu(gate_val, up_val):
    return jax.nn.silu(gate_val) * up_val


def per_device(zs, cs, tokens, starts, w_query, w_key, w_value, w_gate_out, w_out, w_forget_down,
               w_forget_up, norm_attn, norm_head, norm_mlp, w_gate, w_up, w_down, cotangent):
    seqs, seq_len, D = tokens.shape
    n = zs * TP * cs
    rows = w_query.shape[0]
    ff_rows = w_down.shape[0]
    rank = w_forget_down.shape[1]
    fu_cols = w_forget_up.shape[1]
    mine = seqs * seq_len
    half = D // cs
    t_idx, c_idx = lax.axis_index("t"), lax.axis_index("c")

    def to_k(v):
        return v.reshape(-1, zs, TP, cs, rows).transpose(0, 3, 1, 2, 4).reshape(-1, D)

    def from_k(v):
        return v.reshape(-1, cs, zs, TP, rows).transpose(0, 2, 3, 1, 4).reshape(-1, D)

    def sum_z(v):
        return lax.psum_scatter(v, "z", scatter_dimension=0, tiled=True)

    def core_half(v, core):
        return lax.dynamic_slice_in_dim(v, core * half, half, axis=1)

    def other_term(left, right):
        return dot_tn(left, right).astype(BF16)

    def own_term(left, right, other):
        return (dot_tn(left, right) + send_c(other).astype(F32)).astype(BF16)

    docs = jnp.cumsum(starts, axis=1).astype(BF16)
    small = pack_rows([w_forget_down.reshape(-1), w_forget_up.reshape(-1), norm_attn, norm_head, norm_mlp,
                       docs.reshape(-1)], 16)
    sizes = [rows * rank, rank * fu_cols, norm_attn.shape[0], norm_head.shape[0], norm_mlp.shape[0]]
    by_rows = lax.all_gather(jnp.concatenate([w_out, w_down], axis=0), ("z", "c"), axis=0, tiled=True)
    by_rows = by_rows.reshape(zs, cs, rows + ff_rows, D)
    cot = cotangent.reshape(mine, D)
    w4 = spread([w_query, w_key, w_value, w_gate_out], 0)
    small, w4 = after(small, w4)
    small = share(small, n, cs, 9)
    piece = cs * ff_rows
    units = zs * piece
    middle = (units // LANES + 1) // 2 * 2 * LANES
    parts = ((0, middle), (middle, 2 * units))
    w_gate, small = after(w_gate, small)
    gus = spread_ff(w_gate, w_up, piece, parts, 2)
    pieces = cut(small.reshape(n, -1), sizes + [mine])
    wfd = to_k(pieces[0].reshape(D, rank).T).T
    wfu = pieces[1].reshape(n, rank, fu_cols).transpose(1, 0, 2).reshape(rank, n * fu_cols)
    wfu = lax.dynamic_slice_in_dim(wfu, t_idx * SLOTS, SLOTS, axis=1)
    gain_attn = pieces[2].reshape(-1).astype(F32)
    gain_head = pieces[3].reshape(1, -1).astype(F32)
    gain_mlp = pieces[4].reshape(1, -1).astype(F32)
    all_docs = pieces[5].reshape(zs, TP, cs, mine)
    all_docs = lax.dynamic_index_in_dim(all_docs, lax.axis_index("z"), 0, keepdims=False)
    all_docs = lax.dynamic_index_in_dim(all_docs, lax.axis_index("c"), 1, keepdims=False)
    docs = jnp.concatenate([lax.dynamic_index_in_dim(all_docs, t_idx ^ k, 0) for k in range(TP)], axis=0)
    docs = docs.astype(F32).reshape(TP * seqs, seq_len)

    def by_columns(w):
        return lax.all_gather(w.reshape(TP * rows, -1), ("c", "z"), axis=0, tiled=True)

    w4 = by_columns(w4)
    gus = [by_columns(gu) for gu in gus]
    down = by_rows[:, :, rows:].reshape(-1, D)
    wo = swap_t(by_rows[:, :, :rows].reshape(TP, -1, rows, D)).reshape(TP, zs // TP, cs, rows, D)
    wo = wo.transpose(1, 0, 2, 3, 4).reshape(HEAD, D)

    x = tokens.reshape(mine, D).astype(F32)
    normed_in, norm_in_back = jax.vjp(rms_norm, x, gain_attn)
    h = to_k(normed_in.astype(BF16))
    h = gather_t_end(h, *gather_t_begin(h))
    d_branch = gather_t_end(cot, *gather_t_begin(cot))
    d_hidden = dot_nt(d_branch, down)
    h, d_hidden = after(h, d_hidden)
    h, wo = after(h, wo)
    h_own, h_other = after(core_half(h, c_idx), core_half(h, 1 - c_idx))
    h, h_own = after(h, h_own)
    pre = dot(h, w4)
    f_low = dot(h, wfd).astype(BF16)
    act = slots_forward(pre, f_low, wfu, gain_head, docs)
    terms = dot(act, wo).astype(BF16)
    tokens_flat = tokens.reshape(mine, D)
    hm, resid = relay_forward(terms.reshape(TP, mine, D), tokens_flat, gain_mlp, rows, 6)
    hm = hm.reshape(TP * mine, D)

    hidden, d_gus, g_gus = [], [], []
    for gu, (low, _) in zip(gus, parts):
        part, d_gu = ff_forward(hm, gu, d_hidden, low // (2 * LANES))
        g_gu = own_term(core_half(hm, c_idx), d_gu, other_term(core_half(hm, 1 - c_idx), d_gu))
        hm, g_gu = after(hm, g_gu)
        hidden.append(part)
        d_gus.append(d_gu)
        g_gus.append(sum_z(g_gu).reshape(TP, rows, -1))
        last = g_gu
    d_gus[-1], _ = after(d_gus[-1], last)
    d_hm = d_hm_product(d_gus, gus)
    d_attn, d_resid, g_norm_mlp, g_down, branch = relay_backward(
        d_hm.reshape(TP, mine, D), resid, cot, gain_mlp, hidden, d_branch, down, rows, zs, cs, 7)
    d_attn = d_attn.reshape(TP * mine, D)
    g_down = sum_z(g_down.reshape(-1, D))

    d_attn, g_gus[0] = after(d_attn, g_gus[0])
    d_attn, g_gus[1] = after(d_attn, g_gus[1])
    first = scatter_t_send(branch)
    d_act = dot_nt(d_attn, wo)
    count = TP * seqs
    *begun, g_norm_head = slots_backward(pre, f_low, wfu, gain_head, docs, d_act, 0, count // 2)
    first, begun = after(first, begun)
    part, passed = scatter_t_middle(branch, first)
    d_act, passed = after(d_act, passed)
    second = scatter_t_pass(passed)
    d_pre, d_f, d_low, g_more = slots_backward(
        pre, f_low, wfu, gain_head, docs, d_act, count // 2, count - count // 2, begun)
    g_norm_head = g_norm_head + g_more
    g4 = other_term(h_other, d_pre)
    d_pre, g4 = after(d_pre, g4)
    d_h = (dot_nt(d_pre, w4) + dot_nt(d_low, wfd)).astype(BF16)
    d_pre, d_h = after(d_pre, d_h)
    d_pre, g_down = after(d_pre, g_down)
    d_pre, second = after(d_pre, second)
    g4 = own_term(h_own, d_pre, g4)
    d_h, _ = after(d_h, g4)
    g4 = sum_z(g4)
    tokens_grad, flat, g_out, *g_gus = settle(
        d_h.reshape(TP, mine, D), tokens_flat, d_resid, gain_attn.reshape(1, D), d_low, f_low, d_f, g_norm_head,
        g_norm_mlp, act, d_attn, h, g_gus, rows, zs, cs, 8)
    g_out = sum_z(g_out.reshape(-1, D))
    second, tokens_grad = after(second, tokens_grad)
    mixed = (resid + part + jnp.concatenate(second, axis=0).astype(F32)).astype(BF16)

    g_gate, g_up = widen(g_gus, ff_moves(piece, units, parts), 2, n * ff_rows)
    g_down = g_down.astype(F32)
    g4, mixed, tokens_grad, g_gate, g_up, g_down = lax.optimization_barrier(
        (g4, mixed, tokens_grad, g_gate, g_up, g_down))
    small, g4 = finish(flat, g4.reshape(TP, rows, -1), n, cs)
    heads = norm_head.shape[0]
    head_moves = [(i, j * HEAD, 0, j, i * HEAD, HEAD) for i in range(4) for j in range(TP)]
    g_heads, g_out = after(widen([g4], head_moves, 4, D), g_out)
    g_query, g_key, g_value, g_gate_out = g_heads
    g_out = g_out.astype(F32)
    return (
        mixed.reshape(tokens.shape),
        tokens_grad.reshape(tokens.shape),
        g_query, g_key, g_value, g_gate_out,
        g_out,
        small[:rank, :rows].T,
        small[:rank, rows:rows + fu_cols],
        small[rank, :rows],
        small[rank, rows:rows + heads],
        small[rank + 1, :rows],
        g_gate, g_up,
        g_down,
    )


def solution(mesh):
    cs = mesh.shape["outer"]
    zs = mesh.shape["dp"] // TP
    grid = Mesh(mesh.devices.reshape(zs, TP, cs), ALL)
    whole, row, vec = P(ALL, None, None), P(ALL, None), P(ALL)
    cols = P(None, ALL)

    def body(*args):
        return per_device(zs, cs, *args)

    return jax.shard_map(
        body,
        mesh=grid,
        in_specs=(whole, row, row, row, row, row, row, row, cols, vec, vec, vec, row, row, row, whole),
        out_specs=(whole, whole, row, row, row, row, row, row, cols, vec, vec, vec, row, row, row),
        check_vma=False,
    )
```

profile of v0, /device:TPU:0, one launch (start us, length us, event | category | flops | bytes accessed | tf_op | source)
XLA Modules:
  0.0 622.5 jit_solution(14909722744895115444)
XLA Ops:
  12.4 16.7 %spread.1 = bf16[4,64,2048]{2,1,0:T(8,128)(2,1)} custom-call(bf16[64,2048]{1,0:T(8,128)(2,1)} %refs_0_.1, bf16[64,2048]{1,0:T(8,128)(2,1)} %refs_1_.1, bf16[64,2048]{1,0:T(8,128)(2,1)} %refs_2_.1, bf16[64,2048]{1,0:T(8,128)(2,1)} %refs_3_.1), custom_call_target="tpu_custom_call" | custom-call | tf_op jit(solution)/shard_map/spread/pallas_call | solution.py:371
  29.4 10.4 %share_small.1 = bf16[32,16,128]{2,1,0:T(8,128)(2,1)S(1)} custom-call(bf16[16,128]{1,0:T(8,128)(2,1)S(1)} %pad_bitcast_fusion.x_ref), custom_call_target="tpu_custom_call" | custom-call | tf_op jit(solution)/shard_map/share_small/pallas_call | solution.py:330
  39.9 22.3 %spread_ff.1 = (bf16[4,64,1536]{2,1,0:T(8,128)(2,1)}, bf16[4,64,1280]{2,1,0:T(8,128)(2,1)}) custom-call(bf16[64,5632]{1,0:T(8,128)(2,1)S(1)} %copy-done.20, bf16[64,5632]{1,0:T(8,128)(2,1)S(1)} %copy-done.21), custom_call_target="tpu_custom_call" | custom-call | tf_op jit(solution)/shard_map/spread_ff/pallas_call | solution.py:433
  81.2 7.5 %collective-permute-done.5 = bf16[256,2048]{1,0:T(8,128)(2,1)} collective-permute-done((bf16[256,2048]{1,0:T(8,128)(2,1)}, bf16[256,2048]{1,0:T(8,128)(2,1)}, u32[]{:S(2)}, u32[]{:S(2)}) %collective-permute-start.5) | collective-permute-done | bytes 1048608 | tf_op jit(solution)/shard_map/ppermute | solution.py:930
  93.0 18.2 %collective-permute-done.1 = bf16[256,2048]{1,0:T(8,128)(2,1)} collective-permute-done((bf16[256,2048]{1,0:T(8,128)(2,1)}, bf16[256,2048]{1,0:T(8,128)(2,1)}, u32[]{:S(2)}, u32[]{:S(2)}) %collective-permute-start.1) | collective-permute-done | bytes 1048608 | tf_op jit(solution)/shard_map/ppermute | solution.py:930
  124.7 8.2 %collective-permute-done.2 = bf16[128,2048]{1,0:T(8,128)(2,1)S(1)} collective-permute-done((bf16[128,2048]{1,0:T(8,128)(2,1)S(1)}, bf16[128,2048]{1,0:T(8,128)(2,1)S(1)}, u32[]{:S(2)}, u32[]{:S(2)}) %collective-permute-start.2) | collective-permute-done | bytes 524320 | tf_op jit(solution)/shard_map/ppermute | solution.py:930
  145.0 10.8 %fusion.22.d_hidden_ref = f32[1024,1408]{1,0:T(8,128)} fusion(bf16[1024,2048]{1,0:T(8,128)(2,1)} %constant_dynamic-update-slice_fusion.5.refs_2_, bf16[1408,2048]{1,0:T(8,128)(2,1)S(1)} %bitcast.104), kind=kOutput, calls=%fused_computation.76 | convolution fusion | flops 5905580032 | bytes 15728640 | tf_op jit(solution)/shard_map/dot_general | solution.py:21
  157.3 8.3 %collective-permute-done.9 = bf16[2,64,2048]{2,1,0:T(8,128)(2,1)S(1)} collective-permute-done((bf16[2,64,2048]{2,1,0:T(8,128)(2,1)S(1)}, bf16[2,64,2048]{2,1,0:T(8,128)(2,1)S(1)}, u32[]{:S(2)}, u32[]{:S(2)}) %collective-permute-start.9) | collective-permute-done | bytes 524320 | tf_op jit(solution)/shard_map/ppermute | solution.py:930
  167.6 4.6 constant_dynamic-slice_fusion.5
  175.7 12.5 %fusion.23.pre_ref = f32[1024,2048]{1,0:T(8,128)S(1)} fusion(bf16[1024,2048]{1,0:T(8,128)(2,1)} %constant_dynamic-update-slice_fusion.h_hbm, bf16[2048,2048]{1,0:T(8,128)(2,1)} %all-gather.7.cloned.1.call-done), kind=kOutput, calls=%fused_computation.77 | convolution fusion | flops 8589934592 | bytes 20971520 | tf_op jit(solution)/shard_map/dot_general | solution.py:21
  188.3 10.7 %slots_forward.1.act_hbm = bf16[1024,512]{1,0:T(8,128)(2,1)S(1)} custom-call(f32[1024,2048]{1,0:T(8,128)S(1)} %fusion.23.pre_ref, bf16[1024,16]{1,0:T(8,128)(2,1)S(1)} %convolution_convert_fusion.4.f_low_ref, bf16[16,64]{1,0:T(8,128)(2,1)S(1)} %copy.58.wfu_ref, f32[1,512]{1,0:T(1,128)S(1)} %reshape.264.gain_ref, f32[8,128,1]{2,1,0:T(8,128)S(1)} %reshape.269.doc_col_ref, ...), custom_call_target="tpu_custom_call" | custom-call | tf_op jit(solution)/shard_map/slots_forward/pallas_call | solution.py:252
  201.4 72.0 %relay_forward.1 = (bf16[4,256,2048]{2,1,0:T(8,128)(2,1)S(1)}, f32[256,2048]{1,0:T(8,128)S(1)}) custom-call(bf16[4,256,2048]{2,1,0:T(8,128)(2,1)S(1)} %bitcast.101, bf16[256,2048]{1,0:T(8,128)(2,1)S(1)} %bitcast.94, f32[1,2048]{1,0:T(1,128)S(1)} %reshape.267.gain_ref), custom_call_target="tpu_custom_call" | custom-call | tf_op jit(solution)/shard_map/relay_forward/pallas_call | solution.py:793
  276.7 12.1 %feed_forward.2 = (bf16[1024,768]{1,0:T(8,128)(2,1)S(1)}, bf16[1024,1536]{1,0:T(8,128)(2,1)S(1)}) custom-call(bf16[1024,2048]{1,0:T(8,128)(2,1)} %bitcast.95, bf16[2048,1536]{1,0:T(8,128)(2,1)} %all-gather.9.cloned.1.call-done.gu_ref.refs_2_, f32[1024,1408]{1,0:T(8,128)} %fusion.22.d_hidden_ref), custom_call_target="tpu_custom_call" | custom-call | tf_op jit(solution)/shard_map/feed_forward/pallas_call | solution.py:892
  288.8 3.7 convolution_convert_fusion.2
  292.6 5.6 collective-permute-done.11
  298.2 4.8 add_convert_fusion.2
  303.1 10.9 %feed_forward.3 = (bf16[1024,640]{1,0:T(8,128)(2,1)S(1)}, bf16[1024,1280]{1,0:T(8,128)(2,1)S(1)}) custom-call(bf16[1024,2048]{1,0:T(8,128)(2,1)} %bitcast.96, bf16[2048,1280]{1,0:T(8,128)(2,1)} %all-gather.11.cloned.1.call-done.gu_ref.refs_3_, f32[1024,1408]{1,0:T(8,128)} %fusion.22.d_hidden_ref), custom_call_target="tpu_custom_call" | custom-call | tf_op jit(solution)/shard_map/feed_forward/pallas_call | solution.py:892
  317.6 4.7 collective-permute-done.12
  322.3 4.2 add_convert_fusion.3
  330.2 16.0 %d_hm.1 = bf16[1024,2048]{1,0:T(8,128)(2,1)} custom-call(bf16[1024,1536]{1,0:T(8,128)(2,1)S(1)} %copy-done.11, bf16[1024,1280]{1,0:T(8,128)(2,1)S(1)} %copy-done.13, bf16[2048,1536]{1,0:T(8,128)(2,1)} %all-gather.9.cloned.1.call-done.gu_ref.refs_2_, bf16[2048,1280]{1,0:T(8,128)(2,1)} %all-gather.11.cloned.1.call-done.gu_ref.refs_3_), custom_call_target="tpu_custom_call" | custom-call | tf_op jit(solution)/shard_map/d_hm/pallas_call | solution.py:917
  346.2 77.1 %relay_backward.1 = (bf16[4,256,2048]{2,1,0:T(8,128)(2,1)}, f32[256,2048]{1,0:T(8,128)}, f32[1,2048]{1,0:T(1,128)}, bf16[4,176,2048]{2,1,0:T(8,128)(2,1)}, bf16[1024,2048]{1,0:T(8,128)(2,1)}) custom-call(bf16[4,256,2048]{2,1,0:T(8,128)(2,1)} %bitcast.107, f32[256,2048]{1,0:T(8,128)} %copy-done.5, bf16[256,2048]{1,0:T(8,128)(2,1)} %bitcast.112, ...), custom_call_target="tpu_custom_call" | custom-call | tf_op jit(solution)/shard_map/relay_backward/pallas_call | solution.py:812
  429.7 5.4 fusion.24.d_act_ref
  435.4 11.6 %slots_backward.2 = (bf16[1024,2048]{1,0:T(8,128)(2,1)S(1)}, bf16[1024,64]{1,0:T(8,128)(2,1)S(1)}, bf16[1024,16]{1,0:T(8,128)(2,1)S(1)}, f32[1,512]{1,0:T(1,128)S(1)}) custom-call(f32[1024,2048]{1,0:T(8,128)S(1)} %bitcast.92, bf16[1024,16]{1,0:T(8,128)(2,1)S(1)} %convolution_convert_fusion.4.f_low_ref, bf16[16,64]{1,0:T(8,128)(2,1)S(1)} %copy.58.wfu_ref, ...), custom_call_target="tpu_custom_call" | custom-call | tf_op jit(solution)/shard_map/slots_backward/pallas_call | solution.py:270
  447.0 4.2 collective-permute-done.13
  452.4 3.5 convert_add_fusion.1
  455.9 11.6 %slots_backward.3 = (bf16[1024,2048]{1,0:T(8,128)(2,1)S(1)}, bf16[1024,64]{1,0:T(8,128)(2,1)S(1)}, bf16[1024,16]{1,0:T(8,128)(2,1)S(1)}, f32[1,512]{1,0:T(1,128)S(1)}) custom-call(f32[1024,2048]{1,0:T(8,128)S(1)} %bitcast.92, bf16[1024,16]{1,0:T(8,128)(2,1)S(1)} %convolution_convert_fusion.4.f_low_ref, ...), custom_call_target="tpu_custom_call", output_to_operand_aliasing={{0}: (7, {}), {1}: (8, {}), {2}: (9, {})} | custom-call | tf_op jit(solution)/shard_map/slots_backward/pallas_call | solution.py:270
  467.5 6.3 %convolution_convert_fusion.3 = bf16[1024,2048]{1,0:T(8,128)(2,1)} fusion(bf16[1024,1024]{1,0:T(8,128)(2,1)S(1)} %copy-done.29, bf16[1024,2048]{1,0:T(8,128)(2,1)S(1)} %get-tuple-element.146), kind=kOutput, calls=%fused_computation.7 | convolution fusion | flops 4297064448 | bytes 10485760 | tf_op jit(solution)/shard_map/dot_general | solution.py:21
  476.1 8.8 %fusion.25 = f32[1024,2048]{1,0:T(8,128)S(1)} fusion(bf16[1024,2048]{1,0:T(8,128)(2,1)S(1)} %get-tuple-element.146, bf16[2048,2048]{1,0:T(8,128)(2,1)S(1)} %bitcast.140), kind=kOutput, calls=%fused_computation.79 | convolution fusion | flops 8589934592 | bytes 20971520 | tf_op jit(solution)/shard_map/dot_general | solution.py:21
  490.1 9.0 %add_convert_fusion = bf16[1024,2048]{1,0:T(8,128)(2,1)} fusion(bf16[1024,2048]{1,0:T(8,128)(2,1)} %collective-permute-done.17, bf16[1024,1024]{1,0:T(8,128)(2,1)S(1)} %copy-done.28, bf16[1024,2048]{1,0:T(8,128)(2,1)} %copy-done.9), kind=kOutput, calls=%fused_computation | convolution fusion | flops 4301258752 | bytes 14680064 | tf_op jit(solution)/shard_map/dot_general | solution.py:21
  501.1 69.0 %settle.1 = (bf16[256,2048]{1,0:T(8,128)(2,1)}, f32[32,24,128]{2,1,0:T(8,128)}, bf16[4,1,64,2048]{3,2,1,0:T(8,128)(2,1)}, bf16[4,64,1536]{2,1,0:T(8,128)(2,1)}, bf16[4,64,1280]{2,1,0:T(8,128)(2,1)}) custom-call(bf16[4,256,2048]{2,1,0:T(8,128)(2,1)} %bitcast.106, bf16[256,2048]{1,0:T(8,128)(2,1)} %bitcast.93, f32[256,2048]{1,0:T(8,128)} %get-tuple-element.152.d_resid_ref, ...), custom_call_target="tpu_custom_call" | custom-call | tf_op jit(solution)/shard_map/settle/pallas_call | solution.py:847
  581.4 22.2 %finish.1 = (f32[24,128]{1,0:T(8,128)S(1)}, bf16[4,64,2048]{2,1,0:T(8,128)(2,1)S(1)}) custom-call(f32[32,24,128]{2,1,0:T(8,128)S(1)} %copy-done.23, bf16[4,64,2048]{2,1,0:T(8,128)(2,1)S(1)} %bitcast.102), custom_call_target="tpu_custom_call" | custom-call | tf_op jit(solution)/shard_map/finish/pallas_call | solution.py:517
  607.4 4.2 reduce-scatter.14.cloned.1.call-done
  (215 shorter events, 110.5 us)
Async XLA Ops:
  7.2 32.6 %copy-start.20 = (bf16[64,5632]{1,0:T(8,128)(2,1)S(1)}, bf16[64,5632]{1,0:T(8,128)(2,1)}, u32[]{:S(2)}) copy-start(bf16[64,5632]{1,0:T(8,128)(2,1)} %wg_ref) | copy-start | bytes 2162692
  7.2 32.6 %copy-start.21 = (bf16[64,5632]{1,0:T(8,128)(2,1)S(1)}, bf16[64,5632]{1,0:T(8,128)(2,1)}, u32[]{:S(2)}) copy-start(bf16[64,5632]{1,0:T(8,128)(2,1)} %wu_ref.1) | copy-start | bytes 2162692
  7.2 57.1 %copy-start.1 = (bf16[2,128,2048]{2,1,0:T(8,128)(2,1)S(1)}, bf16[2,128,2048]{2,1,0:T(8,128)(2,1)}, u32[]{:S(2)}) copy-start(bf16[2,128,2048]{2,1,0:T(8,128)(2,1)} %param.16) | copy-start | bytes 3145732
  7.2 129.1 %all-gather.5.cloned.1.call-start = ((), (), s32[]{:S(2)}) async-start(), calls=%async_computation.5 | async-start | bytes 8847360 | tf_op jit(solution)/shard_map/all_gather | solution.py:1039
  9.7 166.0 %all-gather.7.cloned.1.call-start = ((), (), s32[]{:S(2)}) async-start(), calls=%async_computation.6 | async-start | bytes 9437184 | tf_op jit(solution)/shard_map/all_gather | solution.py:1065
  29.3 247.3 %all-gather.9.cloned.1.call-start = ((), (), s32[]{:S(2)}) async-start(), calls=%async_computation.7 | async-start | bytes 7077888 | tf_op jit(solution)/shard_map/all_gather | solution.py:1065
  62.2 241.0 %all-gather.11.cloned.1.call-start = ((), (), s32[]{:S(2)}) async-start(), calls=%async_computation.8 | async-start | bytes 5898240 | tf_op jit(solution)/shard_map/all_gather | solution.py:1065
  62.2 26.5 %collective-permute-start.5 = (bf16[256,2048]{1,0:T(8,128)(2,1)}, bf16[256,2048]{1,0:T(8,128)(2,1)}, u32[]{:S(2)}, u32[]{:S(2)}) collective-permute-start(bf16[256,2048]{1,0:T(8,128)(2,1)} %bitcast.110), channel_id=1, source_target_pairs={{0,4},{2,6},{4,0},{6,2},{1,5},{3,7},{5,1},{7,3},{8,12},{10,14},{12... | collective-permute-start | bytes 3145736 | tf_op jit(solution)/shard_map/ppermute | solution.py:930
  63.3 27.6 %collective-permute-start.4 = (bf16[256,2048]{1,0:T(8,128)(2,1)}, bf16[256,2048]{1,0:T(8,128)(2,1)}, u32[]{:S(2)}, u32[]{:S(2)}) collective-permute-start(bf16[256,2048]{1,0:T(8,128)(2,1)} %bitcast.111), channel_id=1, source_target_pairs={{0,2},{2,0},{4,6},{6,4},{1,3},{3,1},{5,7},{7,5},{8,10},{10,8},{12,... | collective-permute-start | bytes 3145736 | tf_op jit(solution)/shard_map/ppermute | solution.py:930
  73.6 37.6 %collective-permute-start.1 = (bf16[256,2048]{1,0:T(8,128)(2,1)}, bf16[256,2048]{1,0:T(8,128)(2,1)}, u32[]{:S(2)}, u32[]{:S(2)}) collective-permute-start(bf16[256,2048]{1,0:T(8,128)(2,1)} %copy.46), channel_id=1, source_target_pairs={{0,4},{2,6},{4,0},{6,2},{1,5},{3,7},{5,1},{7,3},{8,12},{10,14},{12... | collective-permute-start | bytes 3145736 | tf_op jit(solution)/shard_map/ppermute | solution.py:930
  74.7 38.7 %collective-permute-start = (bf16[256,2048]{1,0:T(8,128)(2,1)}, bf16[256,2048]{1,0:T(8,128)(2,1)}, u32[]{:S(2)}, u32[]{:S(2)}) collective-permute-start(bf16[256,2048]{1,0:T(8,128)(2,1)} %copy.46), channel_id=1, source_target_pairs={{0,2},{2,0},{4,6},{6,4},{1,3},{3,1},{5,7},{7,5},{8,10},{10,8},{12,... | collective-permute-start | bytes 3145736 | tf_op jit(solution)/shard_map/ppermute | solution.py:930
  75.7 354.0 %reduce-scatter.6.cloned.1.call-start = ((), (), s32[]{:S(2)}) async-start(), calls=%async_computation.9 | async-start | bytes 3932160 | tf_op jit(solution)/shard_map/reduce_scatter | solution.py:1024
  76.9 124.4 %copy-start.24 = (f32[1,2048]{1,0:T(1,128)}, f32[1,2048]{1,0:T(1,128)S(1)}, u32[]{:S(2)}) copy-start(f32[1,2048]{1,0:T(1,128)S(1)} %reshape.267.gain_ref) | copy-start | bytes 24580
  89.8 44.9 %collective-permute-start.6 = (bf16[128,2048]{1,0:T(8,128)(2,1)S(1)}, bf16[128,2048]{1,0:T(8,128)(2,1)S(1)}, u32[]{:S(2)}, u32[]{:S(2)}) collective-permute-start(bf16[128,2048]{1,0:T(8,128)(2,1)S(1)} %slice.119), channel_id=1, source_target_pairs={{0,2},{2,0},{4,6},{6,4},{1,3},{3,1},{5,7},{7,5},{8,10},{10,8},{12,... | collective-permute-start | bytes 1572872 | tf_op jit(solution)/shard_map/ppermute | solution.py:930
  92.0 43.5 %collective-permute-start.7 = (bf16[128,2048]{1,0:T(8,128)(2,1)S(1)}, bf16[128,2048]{1,0:T(8,128)(2,1)S(1)}, u32[]{:S(2)}, u32[]{:S(2)}) collective-permute-start(bf16[128,2048]{1,0:T(8,128)(2,1)S(1)} %slice.120), channel_id=1, source_target_pairs={{0,4},{2,6},{4,0},{6,2},{1,5},{3,7},{5,1},{7,3},{8,12},{10,14},{12... | collective-permute-start | bytes 1572872 | tf_op jit(solution)/shard_map/ppermute | solution.py:930
  112.2 20.7 %collective-permute-start.2 = (bf16[128,2048]{1,0:T(8,128)(2,1)S(1)}, bf16[128,2048]{1,0:T(8,128)(2,1)S(1)}, u32[]{:S(2)}, u32[]{:S(2)}) collective-permute-start(bf16[128,2048]{1,0:T(8,128)(2,1)S(1)} %slice.117), channel_id=1, source_target_pairs={{0,2},{2,0},{4,6},{6,4},{1,3},{3,1},{5,7},{7,5},{8,10},{10,8},{12,... | collective-permute-start | bytes 1572872 | tf_op jit(solution)/shard_map/ppermute | solution.py:930
  114.5 19.3 %collective-permute-start.3 = (bf16[128,2048]{1,0:T(8,128)(2,1)S(1)}, bf16[128,2048]{1,0:T(8,128)(2,1)S(1)}, u32[]{:S(2)}, u32[]{:S(2)}) collective-permute-start(bf16[128,2048]{1,0:T(8,128)(2,1)S(1)} %slice.118), channel_id=1, source_target_pairs={{0,4},{2,6},{4,0},{6,2},{1,5},{3,7},{5,1},{7,3},{8,12},{10,14},{12... | collective-permute-start | bytes 1572872 | tf_op jit(solution)/shard_map/ppermute | solution.py:930
  141.4 15.8 %collective-permute-start.10 = (bf16[2,64,2048]{2,1,0:T(8,128)(2,1)S(1)}, bf16[2,64,2048]{2,1,0:T(8,128)(2,1)S(1)}, u32[]{:S(2)}, u32[]{:S(2)}) collective-permute-start(bf16[2,64,2048]{2,1,0:T(8,128)(2,1)S(1)} %get-tuple-element.234), channel_id=1, source_target_pairs={{0,6},{2,4},{4,2},{6,0},{1,7},{3,5},{5,3},{7,1},{8,14},{10,12},{12... | collective-permute-start | bytes 1572872 | tf_op jit(solution)/shard_map/ppermute | solution.py:930
  142.6 22.9 %collective-permute-start.9 = (bf16[2,64,2048]{2,1,0:T(8,128)(2,1)S(1)}, bf16[2,64,2048]{2,1,0:T(8,128)(2,1)S(1)}, u32[]{:S(2)}, u32[]{:S(2)}) collective-permute-start(bf16[2,64,2048]{2,1,0:T(8,128)(2,1)S(1)} %get-tuple-element.235), channel_id=1, source_target_pairs={{0,4},{2,6},{4,0},{6,2},{1,5},{3,7},{5,1},{7,3},{8,12},{10,14},{12... | collective-permute-start | bytes 1572872 | tf_op jit(solution)/shard_map/ppermute | solution.py:930
  143.7 21.8 %collective-permute-start.8 = (bf16[2,64,2048]{2,1,0:T(8,128)(2,1)S(1)}, bf16[2,64,2048]{2,1,0:T(8,128)(2,1)S(1)}, u32[]{:S(2)}, u32[]{:S(2)}) collective-permute-start(bf16[2,64,2048]{2,1,0:T(8,128)(2,1)S(1)} %get-tuple-element.236), channel_id=1, source_target_pairs={{0,2},{2,0},{4,6},{6,4},{1,3},{3,1},{5,7},{7,5},{8,10},{10,8},{12,... | collective-permute-start | bytes 1572872 | tf_op jit(solution)/shard_map/ppermute | solution.py:930
  175.7 280.2 %copy-start.7 = (bf16[1024,16]{1,0:T(8,128)(2,1)}, bf16[1024,16]{1,0:T(8,128)(2,1)S(1)}, u32[]{:S(2)}) copy-start(bf16[1024,16]{1,0:T(8,128)(2,1)S(1)} %convolution_convert_fusion.4.f_low_ref) | copy-start | bytes 98308
  292.5 5.7 collective-permute-start.11
  303.1 126.6 %reduce-scatter.8.cloned.1.call-start = ((), (), s32[]{:S(2)}) async-start(), calls=%async_computation.10 | async-start | bytes 3276800 | tf_op jit(solution)/shard_map/reduce_scatter | solution.py:1024
  317.3 5.0 collective-permute-start.12
  326.5 161.7 %reduce-scatter.10.cloned.1.call-start = ((), (), s32[]{:S(2)}) async-start(), calls=%async_computation.11 | async-start | bytes 3604480 | tf_op jit(solution)/shard_map/reduce_scatter | solution.py:1024
  426.5 24.7 %collective-permute-start.13 = (bf16[256,2048]{1,0:T(8,128)(2,1)}, bf16[256,2048]{1,0:T(8,128)(2,1)S(1)}, u32[]{:S(2)}, u32[]{:S(2)}) collective-permute-start(bf16[256,2048]{1,0:T(8,128)(2,1)} %pad_maximum_fusion.2), channel_id=1, source_target_pairs={{0,2},{2,0},{4,6},{6,4},{1,3},{3,1},{5,7},{7,5},{8,10},{10,8},{12,... | collective-permute-start | bytes 3145736 | tf_op jit(solution)/shard_map/ppermute | solution.py:930
  428.1 24.3 %collective-permute-start.14 = (bf16[256,2048]{1,0:T(8,128)(2,1)}, bf16[256,2048]{1,0:T(8,128)(2,1)}, u32[]{:S(2)}, u32[]{:S(2)}) collective-permute-start(bf16[256,2048]{1,0:T(8,128)(2,1)} %pad_maximum_fusion.3), channel_id=1, source_target_pairs={{0,4},{2,6},{4,0},{6,2},{1,5},{3,7},{5,1},{7,3},{8,12},{10,14},{12... | collective-permute-start | bytes 3145736 | tf_op jit(solution)/shard_map/ppermute | solution.py:930
  429.6 150.6 %reduce-scatter.12.cloned.1.call-start = ((), (), s32[]{:S(2)}) async-start(), calls=%async_computation.12 | async-start | bytes 5242880 | tf_op jit(solution)/shard_map/reduce_scatter | solution.py:1024
  473.9 16.2 %collective-permute-start.17 = (bf16[1024,2048]{1,0:T(8,128)(2,1)}, bf16[1024,2048]{1,0:T(8,128)(2,1)}, u32[]{:S(2)}, u32[]{:S(2)}) collective-permute-start(bf16[1024,2048]{1,0:T(8,128)(2,1)} %convolution_convert_fusion.3), channel_id=1, source_target_pairs={{0,1},{1,0},{2,3},{3,2},{4,5},{5,4},{6,7},{7,6},{8,9},{9,8},{10,11... | collective-permute-start | bytes 12582920 | tf_op jit(solution)/shard_map/ppermute | solution.py:934
  474.0 14.5 %collective-permute-start.15 = (bf16[128,2048]{1,0:T(8,128)(2,1)}, bf16[128,2048]{1,0:T(8,128)(2,1)S(1)}, u32[]{:S(2)}, u32[]{:S(2)}) collective-permute-start(bf16[128,2048]{1,0:T(8,128)(2,1)} %get-tuple-element.144), channel_id=1, source_target_pairs={{0,4},{2,6},{4,0},{6,2},{1,5},{3,7},{5,1},{7,3},{8,12},{10,14},{12... | collective-permute-start | bytes 1572872 | tf_op jit(solution)/shard_map/ppermute | solution.py:930
  475.8 14.3 %collective-permute-start.16 = (bf16[128,2048]{1,0:T(8,128)(2,1)}, bf16[128,2048]{1,0:T(8,128)(2,1)}, u32[]{:S(2)}, u32[]{:S(2)}) collective-permute-start(bf16[128,2048]{1,0:T(8,128)(2,1)} %get-tuple-element.145), channel_id=1, source_target_pairs={{0,2},{2,0},{4,6},{6,4},{1,3},{3,1},{5,7},{7,5},{8,10},{10,8},{12,... | collective-permute-start | bytes 1572872 | tf_op jit(solution)/shard_map/ppermute | solution.py:930
  499.1 112.5 %reduce-scatter.14.cloned.1.call-start = ((), (), s32[]{:S(2)}) async-start(), calls=%async_computation.13 | async-start | bytes 1310720 | tf_op jit(solution)/shard_map/reduce_scatter | solution.py:1024
  (36 other events, 322.0 us)
Sparse Core Ops, SparseCore 0:
  10.3 83.1 all-gather.4
  95.1 80.5 all-gather.6
  177.3 63.2 all-gather.8
  242.0 56.4 all-gather.10
  303.2 59.0 reduce-scatter.5
  364.5 52.1 reduce-scatter.7
  429.7 55.1 reduce-scatter.9
  499.3 75.4 reduce-scatter.11
  577.2 34.4 reduce-scatter.13
where the time goes:
time: 629 us; the launch traced here: 623 us
  Pallas kernels  366 us (58%)
  matrix products  77.8 us (12%)
  waiting for transfers between devices  65.8 us (10%)
  local copies, waits for them, and re-layouts  60.9 us (10%)
  other arithmetic  20.2 us (3%)
  starting transfers between devices  17 us (3%)
  between operations  14.9 us (2%)
    dot_general x13, matrix products, mm(): return lax.dot_general(a, b, (dims, ((), ())), preferred_element_type=F32)  77.8 us
    pallas_call x1, Pallas kernels, relay_backward(): pl.pallas_call(functools.partial(backward_relay_kernel, unit, SUBS, len(h...  77.1 us
    pallas_call x1, Pallas kernels, relay_forward(): pl.pallas_call(functools.partial(forward_relay_kernel, unit, SUBS), out_s...  72 us
    pallas_call x1, Pallas kernels, settle(): pl.pallas_call(functools.partial(settle_kernel, unit, number, SUBS), out_...  69 us
    ppermute x15, waiting for transfers between devices, send_t(): return lax.ppermute(x, 't', [(i, i ^ step) for i in range(TP)])  50.9 us
    unnamed x97, local copies, waits for them, and re-layouts  30.4 us
    pallas_call x2, Pallas kernels, slots_backward(): pl.pallas_call(backward_kernel, out_shape=(jax.ShapeDtypeStruct((count *...  23.2 us
    pallas_call x2, Pallas kernels, ff_forward(): pl.pallas_call(functools.partial(ff_kernel, 256), out_shape=(jax.ShapeDty...  22.9 us
  transfers between devices with their start and end apart: 27, of which 12 were waited for; matrix products, arithmetic and copies ran while one was open for 21% of the time, Pallas kernels for 59%

commit v1 on v0

--- a/solution.py
+++ b/solution.py
@@ -701,13 +701,10 @@
         copy.wait()
 
 
-def settle_kernel(unit, count, subs, p_ref, x_ref, d_resid_ref, gain_ref, d_low_ref, f_low_ref, d_f_ref, g_head_ref,
-                  g_mlp_ref, act_hbm, d_attn_hbm, h_hbm, *refs):
-    blocks, refs = refs[:count], refs[count:]
-    o_ref, flat_ref, g_out_hbm, refs = refs[0], refs[1], refs[2], refs[3:]
-    returned, refs = refs[:count], refs[count:]
-    (got1, pass2, got2, ordered, send_sem, recv_sem, own_sem, back_send, back_recv,
-     act, d_attn, h, g_out, g_sum, g_gain_ref, in_sem, core_send, core_recv, swap_own, swap_send, swap_recv) = refs
+def settle_kernel(unit, subs, p_ref, x_ref, d_resid_ref, gain_ref, d_low_ref, f_low_ref, d_f_ref, g_head_ref,
+                  g_mlp_ref, act_hbm, d_attn_hbm, h_hbm, o_ref, flat_ref, g_out_hbm,
+                  got1, pass2, got2, ordered, send_sem, recv_sem,
+                  act, d_attn, h, g_out, g_sum, g_gain_ref, in_sem, core_send, core_recv, swap_own, swap_send, swap_recv):
     z, t, c = (lax.axis_index(a) for a in ALL)
     loads = [pltpu.make_async_copy(src, dst, in_sem.at[i])
              for i, (src, dst) in enumerate([(act_hbm, act), (d_attn_hbm, d_attn), (h_hbm, h)])]
@@ -723,7 +720,6 @@
 
     def beside(i):
         if i == 0:
-            copies.extend(send_blocks(blocks, returned, own_sem, back_send, back_recv))
             for copy in loads:
                 copy.wait()
             for low in range(0, D, D // 4):
@@ -837,23 +833,22 @@
     )(p, resid, cot, gain, *hidden, branch, down)
 
 
-def settle(p, x, d_resid, gain, d_low, f_low, d_f, g_head, g_mlp, act, d_attn, h, blocks, unit, zs, cs, ident):
+def settle(p, x, d_resid, gain, d_low, f_low, d_f, g_head, g_mlp, act, d_attn, h, unit, zs, cs, ident):
     _, count, D = p.shape
     fast = pl.BlockSpec(memory_space=pltpu.VMEM)
     anywhere = pl.BlockSpec(memory_space=pl.ANY)
-    number = len(blocks)
     deep = zs // TP
     rank = f_low.shape[1]
     return pl.pallas_call(
-        functools.partial(settle_kernel, unit, number, SUBS),
+        functools.partial(settle_kernel, unit, SUBS),
         out_shape=(
             jax.ShapeDtypeStruct(p.shape[1:], BF16),
             jax.ShapeDtypeStruct((zs * TP * cs, rank + 8, LANES), F32),
             jax.ShapeDtypeStruct((TP, deep, unit, D), BF16),
-        ) + tuple(jax.ShapeDtypeStruct(b.shape, b.dtype) for b in blocks),
-        in_specs=[fast] * 9 + [anywhere] * (3 + number),
-        out_specs=(fast,) * 2 + (anywhere,) * (1 + number),
-        scratch_shapes=relay_scratch(count, D, SUBS) + block_sems(number) + [
+        ),
+        in_specs=[fast] * 9 + [anywhere] * 3,
+        out_specs=(fast,) * 2 + (anywhere,),
+        scratch_shapes=relay_scratch(count, D, SUBS) + [
             pltpu.VMEM(act.shape, BF16),
             pltpu.VMEM(d_attn.shape, BF16),
             pltpu.VMEM(h.shape, BF16),
@@ -869,7 +864,7 @@
         ],
         compiler_params=pltpu.CompilerParams(collective_id=ident, has_side_effects=True, vmem_limit_bytes=56 << 20),
         name="settle",
-    )(p, x, d_resid, gain, d_low, f_low, d_f, g_head, g_mlp, act, d_attn, h, *blocks)
+    )(p, x, d_resid, gain, d_low, f_low, d_f, g_head, g_mlp, act, d_attn, h)
 
 
 def ff_kernel(tile, hm_ref, gu_ref, d_hidden_ref, hidden_ref, d_gu_ref):
@@ -924,6 +919,75 @@
         compiler_params=pltpu.CompilerParams(vmem_limit_bytes=48 << 20),
         name="d_hm",
     )(*grads, *weights)
+
+
+def heads_kernel(steps, count, own_hbm, other_hbm, d_pre_hbm, *refs):
+    blocks, (o_hbm, *refs) = refs[:count], refs[count:]
+    returned, refs = refs[:count], refs[count:]
+    (own, other, d_pre, sent, got, own_sem, back_send, back_recv, in_sem, out_sem, core_send, core_recv) = refs
+    z, t, c = (lax.axis_index(a) for a in ALL)
+    width = d_pre.shape[2]
+    cols = [slice(i * width, (i + 1) * width) for i in range(steps)]
+    loads = [pltpu.make_async_copy(other_hbm, other, in_sem.at[0])]
+    loads += [pltpu.make_async_copy(d_pre_hbm.at[:, cols[i]], d_pre.at[i], in_sem.at[2 + i]) for i in range(steps)]
+    loads += [pltpu.make_async_copy(own_hbm, own, in_sem.at[1])]
+    for copy in loads:
+        copy.start()
+    barrier = pltpu.get_barrier_semaphore()
+    for device in [(z, chip_peer(t, step), c) for step in (1, 2, 3)] + [(z, t, 1 - c)]:
+        pl.semaphore_signal(barrier, inc=1, device_id=device, device_id_type=pl.DeviceIdType.MESH)
+    pl.semaphore_wait(barrier, TP)
+    copies = send_blocks(blocks, returned, own_sem, back_send, back_recv)
+    crossings = []
+    loads[0].wait()
+    for i in range(steps):
+        loads[1 + i].wait()
+        sent[i] = mm(other[...], d_pre[i], TN).astype(BF16)
+        crossings.append(pltpu.make_async_remote_copy(
+            src_ref=sent.at[i], dst_ref=got.at[i], send_sem=core_send.at[i], recv_sem=core_recv.at[i],
+            device_id=(z, t, 1 - c), device_id_type=pl.DeviceIdType.MESH))
+        crossings[i].start()
+    loads[-1].wait()
+    for i in range(steps):
+        g = mm(own[...], d_pre[i], TN)
+        crossings[i].wait_recv()
+        got[i] = (g + got[i].astype(F32)).astype(BF16)
+        copies.append(pltpu.make_async_copy(got.at[i], o_hbm.at[:, cols[i]], out_sem.at[i]))
+        copies[-1].start()
+    for copy in crossings:
+        copy.wait_send()
+    for copy in copies:
+        copy.wait()
+
+
+def heads_gradient(own, other, d_pre, blocks, ident):
+    tokens, half = own.shape
+    columns = d_pre.shape[1]
+    steps = 4
+    width = columns // steps
+    count = len(blocks)
+    anywhere = pl.BlockSpec(memory_space=pl.ANY)
+    return pl.pallas_call(
+        functools.partial(heads_kernel, steps, count),
+        out_shape=(jax.ShapeDtypeStruct((half, columns), BF16),)
+        + tuple(jax.ShapeDtypeStruct(b.shape, b.dtype) for b in blocks),
+        in_specs=[anywhere] * (3 + count),
+        out_specs=(anywhere,) * (1 + count),
+        scratch_shapes=[
+            pltpu.VMEM((tokens, half), BF16),
+            pltpu.VMEM((tokens, half), BF16),
+            pltpu.VMEM((steps, tokens, width), BF16),
+            pltpu.VMEM((steps, half, width), BF16),
+            pltpu.VMEM((steps, half, width), BF16),
+        ] + block_sems(count) + [
+            pltpu.SemaphoreType.DMA((2 + steps,)),
+            pltpu.SemaphoreType.DMA((steps,)),
+            pltpu.SemaphoreType.DMA((steps,)),
+            pltpu.SemaphoreType.DMA((steps,)),
+        ],
+        compiler_params=pltpu.CompilerParams(collective_id=ident, has_side_effects=True, vmem_limit_bytes=56 << 20),
+        name="heads_gradient",
+    )(own, other, d_pre, *blocks)
 
 
 def send_t(x, step):
@@ -1089,16 +1153,19 @@
     hm = hm.reshape(TP * mine, D)
 
     hidden, d_gus, g_gus = [], [], []
-    for gu, (low, _) in zip(gus, parts):
+    for gu, (low, high) in zip(gus, parts):
         part, d_gu = ff_forward(hm, gu, d_hidden, low // (2 * LANES))
-        g_gu = own_term(core_half(hm, c_idx), d_gu, other_term(core_half(hm, 1 - c_idx), d_gu))
-        hm, g_gu = after(hm, g_gu)
         hidden.append(part)
         d_gus.append(d_gu)
+        g_gu = other_term(core_half(hm, 1 - c_idx), d_gu)
+        if high == 2 * units:
+            d_gus[-1], _ = after(d_gu, g_gu)
+            d_hm = d_hm_product(d_gus, gus)
+            hm, _ = after(hm, d_hm)
+        g_gu = own_term(core_half(hm, c_idx), d_gu, g_gu)
+        hm, g_gu = after(hm, g_gu)
         g_gus.append(sum_z(g_gu).reshape(TP, rows, -1))
-        last = g_gu
-    d_gus[-1], _ = after(d_gus[-1], last)
-    d_hm = d_hm_product(d_gus, gus)
+    d_hm, _ = after(d_hm, g_gu)
     d_attn, d_resid, g_norm_mlp, g_down, branch = relay_backward(
         d_hm.reshape(TP, mine, D), resid, cot, gain_mlp, hidden, d_branch, down, rows, zs, cs, 7)
     d_attn = d_attn.reshape(TP * mine, D)
@@ -1117,22 +1184,19 @@
     d_pre, d_f, d_low, g_more = slots_backward(
         pre, f_low, wfu, gain_head, docs, d_act, count // 2, count - count // 2, begun)
     g_norm_head = g_norm_head + g_more
-    g4 = other_term(h_other, d_pre)
-    d_pre, g4 = after(d_pre, g4)
+    d_pre, second = after(d_pre, second)
+    g4, *g_gus = heads_gradient(h_own, h_other, d_pre, g_gus, 3)
+    d_pre, _ = after(d_pre, g4)
+    d_pre, g_down = after(d_pre, g_down)
+    g4 = sum_z(g4)
     d_h = (dot_nt(d_pre, w4) + dot_nt(d_low, wfd)).astype(BF16)
-    d_pre, d_h = after(d_pre, d_h)
-    d_pre, g_down = after(d_pre, g_down)
-    d_pre, second = after(d_pre, second)
-    g4 = own_term(h_own, d_pre, g4)
-    d_h, _ = after(d_h, g4)
-    g4 = sum_z(g4)
-    tokens_grad, flat, g_out, *g_gus = settle(
+    tokens_grad, flat, g_out = settle(
         d_h.reshape(TP, mine, D), tokens_flat, d_resid, gain_attn.reshape(1, D), d_low, f_low, d_f, g_norm_head,
-        g_norm_mlp, act, d_attn, h, g_gus, rows, zs, cs, 8)
+        g_norm_mlp, act, d_attn, h, rows, zs, cs, 8)
     g_out = sum_z(g_out.reshape(-1, D))
+
     second, tokens_grad = after(second, tokens_grad)
     mixed = (resid + part + jnp.concatenate(second, axis=0).astype(F32)).astype(BF16)
-
     g_gate, g_up = widen(g_gus, ff_moves(piece, units, parts), 2, n * ff_rows)
     g_down = g_down.astype(F32)
     g4, mixed, tokens_grad, g_gate, g_up, g_down = lax.optimization_barrier(

time: 629 us -> 610 us (0.970)
  matrix products: 77.8 us -> 67.4 us
  waiting for transfers between devices: 65.8 us -> 58.3 us
    dot_general x13 -> x11, matrix products: 77.8 us -> 67.4 us  [mm(): return lax.dot_general(a, b, (dims, ((), ())), preferred_element_type=F32)]
    pallas_call x1 -> x2, Pallas kernels: 69 us -> 72.7 us  [the longest x1 53.5 us: settle(): pl.pallas_call(functools.partial(settle_kernel, unit, SUBS), out_shape=(j...]
    unnamed x97 -> x87, local copies, waits for them, and re-layouts: 30.4 us -> 27.8 us
  transfers between devices with their start and end apart: 27 -> 26, of which waited for: 12 -> 9; matrix products, arithmetic and copies ran while one was open for 21% -> 21% of each run, Pallas kernels for 59% -> 61%
where the time goes in v1:
time: 610 us; the launch traced here: 603 us
  Pallas kernels  369 us (60%)
  matrix products  67.4 us (11%)
  waiting for transfers between devices  58.3 us (10%)
  local copies, waits for them, and re-layouts  56.5 us (9%)
  other arithmetic  19.1 us (3%)
  starting transfers between devices  17.2 us (3%)
  between operations  14.9 us (2%)
    pallas_call x1, Pallas kernels, relay_backward(): pl.pallas_call(functools.partial(backward_relay_kernel, unit, SUBS, len(h...  77.1 us
    pallas_call x1, Pallas kernels, relay_forward(): pl.pallas_call(functools.partial(forward_relay_kernel, unit, SUBS), out_s...  71.9 us
    dot_general x11, matrix products, mm(): return lax.dot_general(a, b, (dims, ((), ())), preferred_element_type=F32)  67.4 us
    pallas_call x1, Pallas kernels, settle(): pl.pallas_call(functools.partial(settle_kernel, unit, SUBS), out_shape=(j...  53.5 us
    ppermute x15, waiting for transfers between devices, send_t(): return lax.ppermute(x, 't', [(i, i ^ step) for i in range(TP)])  48.2 us
    unnamed x87, local copies, waits for them, and re-layouts  27.8 us
    pallas_call x2, Pallas kernels, slots_backward(): pl.pallas_call(backward_kernel, out_shape=(jax.ShapeDtypeStruct((count *...  23.4 us
    pallas_call x2, Pallas kernels, ff_forward(): pl.pallas_call(functools.partial(ff_kernel, 256), out_shape=(jax.ShapeDty...  22.9 us
  transfers between devices with their start and end apart: 26, of which 9 were waited for; matrix products, arithmetic and copies ran while one was open for 21% of the time, Pallas kernels for 61%

profile of v1, /device:TPU:0, one launch (start us, length us, event | category | flops | bytes accessed | tf_op | source)
XLA Modules:
  0.0 603.0 jit_solution(3742012532747231892)
XLA Ops:
  12.5 16.7 %spread.1 = bf16[4,64,2048]{2,1,0:T(8,128)(2,1)} custom-call(bf16[64,2048]{1,0:T(8,128)(2,1)} %refs_0_.1, bf16[64,2048]{1,0:T(8,128)(2,1)} %refs_1_.1, bf16[64,2048]{1,0:T(8,128)(2,1)} %refs_2_.1, bf16[64,2048]{1,0:T(8,128)(2,1)} %refs_3_.1), custom_call_target="tpu_custom_call" | custom-call | tf_op jit(solution)/shard_map/spread/pallas_call | solution.py:371
  29.4 10.5 %share_small.1 = bf16[32,16,128]{2,1,0:T(8,128)(2,1)S(1)} custom-call(bf16[16,128]{1,0:T(8,128)(2,1)S(1)} %pad_bitcast_fusion.x_ref), custom_call_target="tpu_custom_call" | custom-call | tf_op jit(solution)/shard_map/share_small/pallas_call | solution.py:330
  40.0 22.2 %spread_ff.1 = (bf16[4,64,1536]{2,1,0:T(8,128)(2,1)}, bf16[4,64,1280]{2,1,0:T(8,128)(2,1)}) custom-call(bf16[64,5632]{1,0:T(8,128)(2,1)S(1)} %copy-done.19, bf16[64,5632]{1,0:T(8,128)(2,1)S(1)} %copy-done.20), custom_call_target="tpu_custom_call" | custom-call | tf_op jit(solution)/shard_map/spread_ff/pallas_call | solution.py:433
  79.3 9.4 %collective-permute-done.5 = bf16[256,2048]{1,0:T(8,128)(2,1)} collective-permute-done((bf16[256,2048]{1,0:T(8,128)(2,1)}, bf16[256,2048]{1,0:T(8,128)(2,1)}, u32[]{:S(2)}, u32[]{:S(2)}) %collective-permute-start.5) | collective-permute-done | bytes 1048608 | tf_op jit(solution)/shard_map/ppermute | solution.py:994
  93.0 18.2 %collective-permute-done.1 = bf16[256,2048]{1,0:T(8,128)(2,1)} collective-permute-done((bf16[256,2048]{1,0:T(8,128)(2,1)}, bf16[256,2048]{1,0:T(8,128)(2,1)}, u32[]{:S(2)}, u32[]{:S(2)}) %collective-permute-start.1) | collective-permute-done | bytes 1048608 | tf_op jit(solution)/shard_map/ppermute | solution.py:994
  124.8 8.1 %collective-permute-done.2 = bf16[128,2048]{1,0:T(8,128)(2,1)S(1)} collective-permute-done((bf16[128,2048]{1,0:T(8,128)(2,1)S(1)}, bf16[128,2048]{1,0:T(8,128)(2,1)S(1)}, u32[]{:S(2)}, u32[]{:S(2)}) %collective-permute-start.2) | collective-permute-done | bytes 524320 | tf_op jit(solution)/shard_map/ppermute | solution.py:994
  145.0 10.4 %fusion.22.d_hidden_ref = f32[1024,1408]{1,0:T(8,128)} fusion(bf16[1024,2048]{1,0:T(8,128)(2,1)} %constant_dynamic-update-slice_fusion.5.refs_2_, bf16[1408,2048]{1,0:T(8,128)(2,1)S(1)} %bitcast.98), kind=kOutput, calls=%fused_computation.74 | convolution fusion | flops 5905580032 | bytes 15728640 | tf_op jit(solution)/shard_map/dot_general | solution.py:21
  157.3 8.3 %collective-permute-done.9 = bf16[2,64,2048]{2,1,0:T(8,128)(2,1)S(1)} collective-permute-done((bf16[2,64,2048]{2,1,0:T(8,128)(2,1)S(1)}, bf16[2,64,2048]{2,1,0:T(8,128)(2,1)S(1)}, u32[]{:S(2)}, u32[]{:S(2)}) %collective-permute-start.9) | collective-permute-done | bytes 524320 | tf_op jit(solution)/shard_map/ppermute | solution.py:994
  167.6 4.7 constant_dynamic-slice_fusion.5
  172.3 3.4 convolution_convert_fusion.3.f_low_ref
  175.7 12.5 %fusion.23.pre_ref = f32[1024,2048]{1,0:T(8,128)S(1)} fusion(bf16[1024,2048]{1,0:T(8,128)(2,1)} %constant_dynamic-update-slice_fusion.h_hbm, bf16[2048,2048]{1,0:T(8,128)(2,1)} %all-gather.7.cloned.1.call-done), kind=kOutput, calls=%fused_computation.75 | convolution fusion | flops 8589934592 | bytes 20971520 | tf_op jit(solution)/shard_map/dot_general | solution.py:21
  188.3 10.7 %slots_forward.1.act_hbm = bf16[1024,512]{1,0:T(8,128)(2,1)S(1)} custom-call(f32[1024,2048]{1,0:T(8,128)S(1)} %fusion.23.pre_ref, bf16[1024,16]{1,0:T(8,128)(2,1)S(1)} %convolution_convert_fusion.3.f_low_ref, bf16[16,64]{1,0:T(8,128)(2,1)S(1)} %copy.58.wfu_ref, f32[1,512]{1,0:T(1,128)S(1)} %reshape.264.gain_ref, f32[8,128,1]{2,1,0:T(8,128)S(1)} %reshape.269.doc_col_ref, ...), custom_call_target="tpu_custom_call" | custom-call | tf_op jit(solution)/shard_map/slots_forward/pallas_call | solution.py:252
  201.4 71.9 %relay_forward.1 = (bf16[4,256,2048]{2,1,0:T(8,128)(2,1)S(1)}, f32[256,2048]{1,0:T(8,128)S(1)}) custom-call(bf16[4,256,2048]{2,1,0:T(8,128)(2,1)S(1)} %bitcast.95, bf16[256,2048]{1,0:T(8,128)(2,1)S(1)} %bitcast.94, f32[1,2048]{1,0:T(1,128)S(1)} %reshape.267.gain_ref), custom_call_target="tpu_custom_call" | custom-call | tf_op jit(solution)/shard_map/relay_forward/pallas_call | solution.py:789
  276.6 12.1 %feed_forward.2 = (bf16[1024,768]{1,0:T(8,128)(2,1)S(1)}, bf16[1024,1536]{1,0:T(8,128)(2,1)S(1)}) custom-call(bf16[1024,2048]{1,0:T(8,128)(2,1)} %bitcast.87, bf16[2048,1536]{1,0:T(8,128)(2,1)} %all-gather.9.cloned.1.call-done.gu_ref.refs_2_, f32[1024,1408]{1,0:T(8,128)} %fusion.22.d_hidden_ref), custom_call_target="tpu_custom_call" | custom-call | tf_op jit(solution)/shard_map/feed_forward/pallas_call | solution.py:887
  288.8 3.7 convolution_convert_fusion.2
  292.6 5.6 collective-permute-done.11
  298.2 4.8 add_convert_fusion.1
  303.2 10.9 %feed_forward.3 = (bf16[1024,640]{1,0:T(8,128)(2,1)S(1)}, bf16[1024,1280]{1,0:T(8,128)(2,1)S(1)}) custom-call(bf16[1024,2048]{1,0:T(8,128)(2,1)} %bitcast.88, bf16[2048,1280]{1,0:T(8,128)(2,1)} %all-gather.11.cloned.1.call-done.gu_ref.refs_3_, f32[1024,1408]{1,0:T(8,128)} %fusion.22.d_hidden_ref), custom_call_target="tpu_custom_call" | custom-call | tf_op jit(solution)/shard_map/feed_forward/pallas_call | solution.py:887
  314.1 4.3 convolution_convert_fusion.1
  318.5 15.7 %d_hm.1 = bf16[1024,2048]{1,0:T(8,128)(2,1)} custom-call(bf16[1024,1536]{1,0:T(8,128)(2,1)S(1)} %copy-done.12, bf16[1024,1280]{1,0:T(8,128)(2,1)S(1)} %get-tuple-element.118.refs_1_, bf16[2048,1536]{1,0:T(8,128)(2,1)} %all-gather.9.cloned.1.call-done.gu_ref.refs_2_, bf16[2048,1280]{1,0:T(8,128)(2,1)} %all-gather.11.cloned.1.call-done.gu_ref.refs_3_), custom_call_target="tpu_custom_call" | custom-call | tf_op jit(solution)/shard_map/d_hm/pallas_call | solution.py:912
  334.3 4.2 add_convert_fusion.2
  339.0 77.1 %relay_backward.1 = (bf16[4,256,2048]{2,1,0:T(8,128)(2,1)}, f32[256,2048]{1,0:T(8,128)}, f32[1,2048]{1,0:T(1,128)}, bf16[4,176,2048]{2,1,0:T(8,128)(2,1)}, bf16[1024,2048]{1,0:T(8,128)(2,1)}) custom-call(bf16[4,256,2048]{2,1,0:T(8,128)(2,1)} %bitcast.101, f32[256,2048]{1,0:T(8,128)} %copy-done.7, bf16[256,2048]{1,0:T(8,128)(2,1)} %bitcast.106, ...), custom_call_target="tpu_custom_call" | custom-call | tf_op jit(solution)/shard_map/relay_backward/pallas_call | solution.py:808
  422.3 5.7 fusion.24.d_act_ref
  428.0 3.4 copy-done.1
  431.3 11.6 %slots_backward.2 = (bf16[1024,2048]{1,0:T(8,128)(2,1)S(1)}, bf16[1024,64]{1,0:T(8,128)(2,1)S(1)}, bf16[1024,16]{1,0:T(8,128)(2,1)S(1)}, f32[1,512]{1,0:T(1,128)S(1)}) custom-call(f32[1024,2048]{1,0:T(8,128)S(1)} %copy-done.1, bf16[1024,16]{1,0:T(8,128)(2,1)S(1)} %convolution_convert_fusion.3.f_low_ref, bf16[16,64]{1,0:T(8,128)(2,1)S(1)} %copy.58.wfu_ref, ...), custom_call_target="tpu_custom_call" | custom-call | tf_op jit(solution)/shard_map/slots_backward/pallas_call | solution.py:270
  445.2 3.3 convert_add_fusion.1
  450.5 11.8 %slots_backward.3 = (bf16[1024,2048]{1,0:T(8,128)(2,1)S(1)}, bf16[1024,64]{1,0:T(8,128)(2,1)S(1)}, bf16[1024,16]{1,0:T(8,128)(2,1)S(1)}, f32[1,512]{1,0:T(1,128)S(1)}) custom-call(f32[1024,2048]{1,0:T(8,128)S(1)} %copy-done.1, bf16[1024,16]{1,0:T(8,128)(2,1)S(1)} %convolution_convert_fusion.3.f_low_ref, ...), custom_call_target="tpu_custom_call", output_to_operand_aliasing={{0}: (7, {}), {1}: (8, {}), {2}: (9, {})} | custom-call | tf_op jit(solution)/shard_map/slots_backward/pallas_call | solution.py:270
  464.3 19.2 %heads_gradient.1 = (bf16[1024,2048]{1,0:T(8,128)(2,1)}, bf16[4,64,1536]{2,1,0:T(8,128)(2,1)}, bf16[4,64,1280]{2,1,0:T(8,128)(2,1)}) custom-call(bf16[1024,1024]{1,0:T(8,128)(2,1)} %get-tuple-element.105.own_hbm, bf16[1024,1024]{1,0:T(8,128)(2,1)} %get-tuple-element.106.other_hbm, bf16[1024,2048]{1,0:T(8,128)(2,1)} %copy-done.2, ...), custom_call_target="tpu_custom_call" | custom-call | tf_op jit(solution)/shard_map/heads_gradient/pallas_call | solution.py:970
  484.9 12.8 %fusion.25 = f32[1024,2048]{1,0:T(8,128)S(1)} fusion(bf16[1024,2048]{1,0:T(8,128)(2,1)} %copy-done.2, bf16[2048,2048]{1,0:T(8,128)(2,1)} %all-gather.7.cloned.1.call-done), kind=kOutput, calls=%fused_computation.77 | convolution fusion | flops 8589934592 | bytes 20971520 | tf_op jit(solution)/shard_map/dot_general | solution.py:21
  500.9 53.5 %settle.1 = (bf16[256,2048]{1,0:T(8,128)(2,1)}, f32[32,24,128]{2,1,0:T(8,128)}, bf16[4,1,64,2048]{3,2,1,0:T(8,128)(2,1)}) custom-call(bf16[4,256,2048]{2,1,0:T(8,128)(2,1)} %bitcast.100, bf16[256,2048]{1,0:T(8,128)(2,1)} %bitcast.93, f32[256,2048]{1,0:T(8,128)} %get-tuple-element.152.d_resid_ref, f32[1,2048]{1,0:T(1,128)} %reshape.268.gain_ref, ...), custom_call_target="tpu_custom_call" | custom-call | tf_op jit(solution)/shard_map/settle/pallas_call | solution.py:842
  563.2 22.1 %finish.1 = (f32[24,128]{1,0:T(8,128)S(1)}, bf16[4,64,2048]{2,1,0:T(8,128)(2,1)S(1)}) custom-call(f32[32,24,128]{2,1,0:T(8,128)S(1)} %copy-done.22, bf16[4,64,2048]{2,1,0:T(8,128)(2,1)S(1)} %bitcast.96), custom_call_target="tpu_custom_call" | custom-call | tf_op jit(solution)/shard_map/finish/pallas_call | solution.py:517
  589.1 4.3 reduce-scatter.14.cloned.1.call-done
  (200 shorter events, 94.8 us)
Async XLA Ops:
  7.2 129.0 %all-gather.5.cloned.1.call-start = ((), (), s32[]{:S(2)}) async-start(), calls=%async_computation.5 | async-start | bytes 8847360 | tf_op jit(solution)/shard_map/all_gather | solution.py:1103
  9.6 54.7 %copy-start.6 = (bf16[2,128,2048]{2,1,0:T(8,128)(2,1)S(1)}, bf16[2,128,2048]{2,1,0:T(8,128)(2,1)}, u32[]{:S(2)}) copy-start(bf16[2,128,2048]{2,1,0:T(8,128)(2,1)} %param.16) | copy-start | bytes 3145732
  9.6 166.1 %all-gather.7.cloned.1.call-start = ((), (), s32[]{:S(2)}) async-start(), calls=%async_computation.6 | async-start | bytes 9437184 | tf_op jit(solution)/shard_map/all_gather | solution.py:1129
  29.4 247.3 %all-gather.9.cloned.1.call-start = ((), (), s32[]{:S(2)}) async-start(), calls=%async_computation.7 | async-start | bytes 7077888 | tf_op jit(solution)/shard_map/all_gather | solution.py:1129
  62.2 241.0 %all-gather.11.cloned.1.call-start = ((), (), s32[]{:S(2)}) async-start(), calls=%async_computation.8 | async-start | bytes 5898240 | tf_op jit(solution)/shard_map/all_gather | solution.py:1129
  62.2 26.5 %collective-permute-start.5 = (bf16[256,2048]{1,0:T(8,128)(2,1)}, bf16[256,2048]{1,0:T(8,128)(2,1)}, u32[]{:S(2)}, u32[]{:S(2)}) collective-permute-start(bf16[256,2048]{1,0:T(8,128)(2,1)} %bitcast.104), channel_id=1, source_target_pairs={{0,4},{2,6},{4,0},{6,2},{1,5},{3,7},{5,1},{7,3},{8,12},{10,14},{12... | collective-permute-start | bytes 3145736 | tf_op jit(solution)/shard_map/ppermute | solution.py:994
  63.3 27.6 %collective-permute-start.4 = (bf16[256,2048]{1,0:T(8,128)(2,1)}, bf16[256,2048]{1,0:T(8,128)(2,1)}, u32[]{:S(2)}, u32[]{:S(2)}) collective-permute-start(bf16[256,2048]{1,0:T(8,128)(2,1)} %bitcast.105), channel_id=1, source_target_pairs={{0,2},{2,0},{4,6},{6,4},{1,3},{3,1},{5,7},{7,5},{8,10},{10,8},{12,... | collective-permute-start | bytes 3145736 | tf_op jit(solution)/shard_map/ppermute | solution.py:994
  71.7 39.4 %collective-permute-start.1 = (bf16[256,2048]{1,0:T(8,128)(2,1)}, bf16[256,2048]{1,0:T(8,128)(2,1)}, u32[]{:S(2)}, u32[]{:S(2)}) collective-permute-start(bf16[256,2048]{1,0:T(8,128)(2,1)} %copy.46), channel_id=1, source_target_pairs={{0,4},{2,6},{4,0},{6,2},{1,5},{3,7},{5,1},{7,3},{8,12},{10,14},{12... | collective-permute-start | bytes 3145736 | tf_op jit(solution)/shard_map/ppermute | solution.py:994
  72.9 40.5 %collective-permute-start = (bf16[256,2048]{1,0:T(8,128)(2,1)}, bf16[256,2048]{1,0:T(8,128)(2,1)}, u32[]{:S(2)}, u32[]{:S(2)}) collective-permute-start(bf16[256,2048]{1,0:T(8,128)(2,1)} %copy.46), channel_id=1, source_target_pairs={{0,2},{2,0},{4,6},{6,4},{1,3},{3,1},{5,7},{7,5},{8,10},{10,8},{12,... | collective-permute-start | bytes 3145736 | tf_op jit(solution)/shard_map/ppermute | solution.py:994
  73.8 348.4 %reduce-scatter.6.cloned.1.call-start = ((), (), s32[]{:S(2)}) async-start(), calls=%async_computation.9 | async-start | bytes 3932160 | tf_op jit(solution)/shard_map/reduce_scatter | solution.py:1088
  75.1 126.3 %copy-start.23 = (f32[1,2048]{1,0:T(1,128)}, f32[1,2048]{1,0:T(1,128)S(1)}, u32[]{:S(2)}) copy-start(f32[1,2048]{1,0:T(1,128)S(1)} %reshape.267.gain_ref) | copy-start | bytes 24580
  89.8 44.8 %collective-permute-start.6 = (bf16[128,2048]{1,0:T(8,128)(2,1)S(1)}, bf16[128,2048]{1,0:T(8,128)(2,1)S(1)}, u32[]{:S(2)}, u32[]{:S(2)}) collective-permute-start(bf16[128,2048]{1,0:T(8,128)(2,1)S(1)} %slice.119), channel_id=1, source_target_pairs={{0,2},{2,0},{4,6},{6,4},{1,3},{3,1},{5,7},{7,5},{8,10},{10,8},{12,... | collective-permute-start | bytes 1572872 | tf_op jit(solution)/shard_map/ppermute | solution.py:994
  92.0 43.4 %collective-permute-start.7 = (bf16[128,2048]{1,0:T(8,128)(2,1)S(1)}, bf16[128,2048]{1,0:T(8,128)(2,1)S(1)}, u32[]{:S(2)}, u32[]{:S(2)}) collective-permute-start(bf16[128,2048]{1,0:T(8,128)(2,1)S(1)} %slice.120), channel_id=1, source_target_pairs={{0,4},{2,6},{4,0},{6,2},{1,5},{3,7},{5,1},{7,3},{8,12},{10,14},{12... | collective-permute-start | bytes 1572872 | tf_op jit(solution)/shard_map/ppermute | solution.py:994
  112.3 20.7 %collective-permute-start.2 = (bf16[128,2048]{1,0:T(8,128)(2,1)S(1)}, bf16[128,2048]{1,0:T(8,128)(2,1)S(1)}, u32[]{:S(2)}, u32[]{:S(2)}) collective-permute-start(bf16[128,2048]{1,0:T(8,128)(2,1)S(1)} %slice.117), channel_id=1, source_target_pairs={{0,2},{2,0},{4,6},{6,4},{1,3},{3,1},{5,7},{7,5},{8,10},{10,8},{12,... | collective-permute-start | bytes 1572872 | tf_op jit(solution)/shard_map/ppermute | solution.py:994
  114.5 19.3 %collective-permute-start.3 = (bf16[128,2048]{1,0:T(8,128)(2,1)S(1)}, bf16[128,2048]{1,0:T(8,128)(2,1)S(1)}, u32[]{:S(2)}, u32[]{:S(2)}) collective-permute-start(bf16[128,2048]{1,0:T(8,128)(2,1)S(1)} %slice.118), channel_id=1, source_target_pairs={{0,4},{2,6},{4,0},{6,2},{1,5},{3,7},{5,1},{7,3},{8,12},{10,14},{12... | collective-permute-start | bytes 1572872 | tf_op jit(solution)/shard_map/ppermute | solution.py:994
  141.4 15.8 %collective-permute-start.10 = (bf16[2,64,2048]{2,1,0:T(8,128)(2,1)S(1)}, bf16[2,64,2048]{2,1,0:T(8,128)(2,1)S(1)}, u32[]{:S(2)}, u32[]{:S(2)}) collective-permute-start(bf16[2,64,2048]{2,1,0:T(8,128)(2,1)S(1)} %get-tuple-element.232), channel_id=1, source_target_pairs={{0,6},{2,4},{4,2},{6,0},{1,7},{3,5},{5,3},{7,1},{8,14},{10,12},{12... | collective-permute-start | bytes 1572872 | tf_op jit(solution)/shard_map/ppermute | solution.py:994
  142.6 22.9 %collective-permute-start.9 = (bf16[2,64,2048]{2,1,0:T(8,128)(2,1)S(1)}, bf16[2,64,2048]{2,1,0:T(8,128)(2,1)S(1)}, u32[]{:S(2)}, u32[]{:S(2)}) collective-permute-start(bf16[2,64,2048]{2,1,0:T(8,128)(2,1)S(1)} %get-tuple-element.233), channel_id=1, source_target_pairs={{0,4},{2,6},{4,0},{6,2},{1,5},{3,7},{5,1},{7,3},{8,12},{10,14},{12... | collective-permute-start | bytes 1572872 | tf_op jit(solution)/shard_map/ppermute | solution.py:994
  143.8 21.8 %collective-permute-start.8 = (bf16[2,64,2048]{2,1,0:T(8,128)(2,1)S(1)}, bf16[2,64,2048]{2,1,0:T(8,128)(2,1)S(1)}, u32[]{:S(2)}, u32[]{:S(2)}) collective-permute-start(bf16[2,64,2048]{2,1,0:T(8,128)(2,1)S(1)} %get-tuple-element.234), channel_id=1, source_target_pairs={{0,2},{2,0},{4,6},{6,4},{1,3},{3,1},{5,7},{7,5},{8,10},{10,8},{12,... | collective-permute-start | bytes 1572872 | tf_op jit(solution)/shard_map/ppermute | solution.py:994
  175.7 274.8 %copy-start.9 = (bf16[1024,16]{1,0:T(8,128)(2,1)}, bf16[1024,16]{1,0:T(8,128)(2,1)S(1)}, u32[]{:S(2)}) copy-start(bf16[1024,16]{1,0:T(8,128)(2,1)S(1)} %convolution_convert_fusion.3.f_low_ref) | copy-start | bytes 98308
  292.5 5.7 collective-permute-start.11
  303.1 119.2 %reduce-scatter.8.cloned.1.call-start = ((), (), s32[]{:S(2)}) async-start(), calls=%async_computation.10 | async-start | bytes 3276800 | tf_op jit(solution)/shard_map/reduce_scatter | solution.py:1088
  318.3 15.9 %collective-permute-start.12 = (bf16[1024,1280]{1,0:T(8,128)(2,1)}, bf16[1024,1280]{1,0:T(8,128)(2,1)S(1)}, u32[]{:S(2)}, u32[]{:S(2)}) collective-permute-start(bf16[1024,1280]{1,0:T(8,128)(2,1)} %convolution_convert_fusion.1), channel_id=1, source_target_pairs={{0,1},{1,0},{2,3},{3,2},{4,5},{5,4},{6,7},{7,6},{8,9},{9,8},{10,11... | collective-permute-start | bytes 7864328 | tf_op jit(solution)/shard_map/ppermute | solution.py:998
  338.5 146.4 %reduce-scatter.12.cloned.1.call-start = ((), (), s32[]{:S(2)}) async-start(), calls=%async_computation.12 | async-start | bytes 3604480 | tf_op jit(solution)/shard_map/reduce_scatter | solution.py:1088
  416.2 145.8 %reduce-scatter.10.cloned.1.call-start = ((), (), s32[]{:S(2)}) async-start(), calls=%async_computation.11 | async-start | bytes 5242880 | tf_op jit(solution)/shard_map/reduce_scatter | solution.py:1088
  419.1 25.0 %collective-permute-start.13 = (bf16[256,2048]{1,0:T(8,128)(2,1)}, bf16[256,2048]{1,0:T(8,128)(2,1)}, u32[]{:S(2)}, u32[]{:S(2)}) collective-permute-start(bf16[256,2048]{1,0:T(8,128)(2,1)} %pad_maximum_fusion.2), channel_id=1, source_target_pairs={{0,2},{2,0},{4,6},{6,4},{1,3},{3,1},{5,7},{7,5},{8,10},{10,8},{12,... | collective-permute-start | bytes 3145736 | tf_op jit(solution)/shard_map/ppermute | solution.py:994
  420.7 24.4 %collective-permute-start.14 = (bf16[256,2048]{1,0:T(8,128)(2,1)}, bf16[256,2048]{1,0:T(8,128)(2,1)S(1)}, u32[]{:S(2)}, u32[]{:S(2)}) collective-permute-start(bf16[256,2048]{1,0:T(8,128)(2,1)} %pad_maximum_fusion.3), channel_id=1, source_target_pairs={{0,4},{2,6},{4,0},{6,2},{1,5},{3,7},{5,1},{7,3},{8,12},{10,14},{12... | collective-permute-start | bytes 3145736 | tf_op jit(solution)/shard_map/ppermute | solution.py:994
  448.4 15.8 %collective-permute-start.15 = (bf16[128,2048]{1,0:T(8,128)(2,1)S(1)}, bf16[128,2048]{1,0:T(8,128)(2,1)S(1)}, u32[]{:S(2)}, u32[]{:S(2)}) collective-permute-start(bf16[128,2048]{1,0:T(8,128)(2,1)S(1)} %get-tuple-element.140), channel_id=1, source_target_pairs={{0,4},{2,6},{4,0},{6,2},{1,5},{3,7},{5,1},{7,3},{8,12},{10,14},{12... | collective-permute-start | bytes 1572872 | tf_op jit(solution)/shard_map/ppermute | solution.py:994
  450.2 14.1 %collective-permute-start.16 = (bf16[128,2048]{1,0:T(8,128)(2,1)S(1)}, bf16[128,2048]{1,0:T(8,128)(2,1)S(1)}, u32[]{:S(2)}, u32[]{:S(2)}) collective-permute-start(bf16[128,2048]{1,0:T(8,128)(2,1)S(1)} %get-tuple-element.141), channel_id=1, source_target_pairs={{0,2},{2,0},{4,6},{6,4},{1,3},{3,1},{5,7},{7,5},{8,10},{10,8},{12,... | collective-permute-start | bytes 1572872 | tf_op jit(solution)/shard_map/ppermute | solution.py:994
  464.2 33.5 %copy-start.13 = (bf16[1024,16]{1,0:T(8,128)(2,1)}, bf16[1024,16]{1,0:T(8,128)(2,1)S(1)}, u32[]{:S(2)}) copy-start(bf16[1024,16]{1,0:T(8,128)(2,1)S(1)} %get-tuple-element.151.d_low_ref) | copy-start | bytes 98308
  483.6 109.8 %reduce-scatter.14.cloned.1.call-start = ((), (), s32[]{:S(2)}) async-start(), calls=%async_computation.13 | async-start | bytes 1310720 | tf_op jit(solution)/shard_map/reduce_scatter | solution.py:1088
  500.9 56.1 %copy-start.21 = (bf16[4,64,1280]{2,1,0:T(8,128)(2,1)S(1)}, bf16[4,64,1280]{2,1,0:T(8,128)(2,1)}, u32[]{:S(2)}) copy-start(bf16[4,64,1280]{2,1,0:T(8,128)(2,1)} %get-tuple-element.162.refs_1_) | copy-start | bytes 1966084
  559.0 36.2 %copy-start.29 = (bf16[256,2048]{1,0:T(8,128)(2,1)S(1)}, bf16[256,2048]{1,0:T(8,128)(2,1)}, u32[]{:S(2)}) copy-start(bf16[256,2048]{1,0:T(8,128)(2,1)} %get-tuple-element.167) | copy-start | bytes 3145732
  (30 other events, 322.0 us)
Sparse Core Ops, SparseCore 0:
  10.3 83.1 all-gather.4
  95.1 80.5 all-gather.6
  177.3 63.2 all-gather.8
  242.0 56.4 all-gather.10
  303.2 58.9 reduce-scatter.5
  364.4 52.1 reduce-scatter.7
  418.9 55.8 reduce-scatter.11
  483.7 75.7 reduce-scatter.9
  561.9 31.4 reduce-scatter.13

commit v2 on v1

--- a/solution.py
+++ b/solution.py
@@ -648,7 +648,7 @@
 
 
 def backward_relay_kernel(unit, subs, parts, p_ref, resid_ref, cot_ref, gain_ref, *refs):
-    hidden_hbm, (branch_hbm, down_hbm, o_ref, d_resid_ref, g_gain_ref, g_down_hbm, terms_hbm, *refs) = refs[:parts], refs[parts:]
+    hidden_hbm, (branch_hbm, down_hbm, o_ref, d_resid_ref, g_gain_ref, g_down_hbm, kept_hbm, one_hbm, two_hbm, *refs) = refs[:parts], refs[parts:]
     (got1, pass2, got2, ordered, send_sem, recv_sem, hidden, branch, down, g_down, g_other, terms,
      in_sem, out_sem, core_send, core_recv) = refs
     z, t, c = (lax.axis_index(a) for a in ALL)
@@ -680,14 +680,19 @@
                 device_id=(z, t, 1 - c), device_id_type=pl.DeviceIdType.MESH))
             crossings[i].start()
             terms[i] = mm(hidden[...], down[:, cols], NN).astype(BF16)
-            stores.append(pltpu.make_async_copy(terms.at[i], terms_hbm.at[:, cols], out_sem.at[0, i]))
-            stores[-1].start()
+            half = terms.shape[1] // (2 * TP)
+            places = ((kept_hbm, 0, 0, 2), (kept_hbm, 2, 4, 1), (kept_hbm, 3, 3, 1),
+                      (one_hbm, 0, 2, 1), (one_hbm, 1, 6, 1), (two_hbm, 0, 5, 1), (two_hbm, 1, 7, 1))
+            for j, (target, at, low, size) in enumerate(places):
+                stores.append(pltpu.make_async_copy(
+                    terms.at[i, low * half:(low + size) * half], target.at[at * half:(at + size) * half, cols], out_sem.at[j, i]))
+                stores[-1].start()
         if 1 <= i <= subs:
             k = i - 1
             crossings[k].wait()
             g_other[k] = (g_other[k].astype(F32) + g_down[k, :, c].astype(F32)).astype(BF16)
             stores.append(pltpu.make_async_copy(
-                g_other.at[k], g_down_hbm.at[:, :, slice(k * width, (k + 1) * width)], out_sem.at[1, k]))
+                g_other.at[k], g_down_hbm.at[:, :, slice(k * width, (k + 1) * width)], out_sem.at[7, k]))
             stores[-1].start()
 
     def finish(rows, d):
@@ -812,10 +817,9 @@
             jax.ShapeDtypeStruct(resid.shape, F32),
             jax.ShapeDtypeStruct((1, D), F32),
             jax.ShapeDtypeStruct((zs, each, D), BF16),
-            jax.ShapeDtypeStruct((tokens, D), BF16),
-        ),
+        ) + tuple(jax.ShapeDtypeStruct((rows, D), BF16) for rows in (tokens // 2, tokens // 4, tokens // 4)),
         in_specs=[fast] * 4 + [anywhere] * (len(hidden) + 2),
-        out_specs=(fast,) * 3 + (anywhere,) * 2,
+        out_specs=(fast,) * 3 + (anywhere,) * 4,
         scratch_shapes=relay_scratch(count, D, SUBS) + [
             pltpu.VMEM((tokens, units), BF16),
             pltpu.VMEM(branch.shape, BF16),
@@ -824,7 +828,7 @@
             pltpu.VMEM((SUBS, zs, each, width), BF16),
             pltpu.VMEM((SUBS, tokens, width), BF16),
             pltpu.SemaphoreType.DMA((len(hidden) + 2,)),
-            pltpu.SemaphoreType.DMA((2, SUBS)),
+            pltpu.SemaphoreType.DMA((8, SUBS)),
             pltpu.SemaphoreType.DMA((SUBS,)),
             pltpu.SemaphoreType.DMA((SUBS,)),
         ],
@@ -1007,25 +1011,15 @@
     return jnp.concatenate([x, one, two, send_t(two[:half], 1), send_t(one[half:], 2)], axis=0)
 
 
-def scatter_t_send(x):
-    count = x.shape[0] // TP
-    half = count // 2
-    p = [(x[k * count:k * count + half], x[k * count + half:(k + 1) * count]) for k in range(TP)]
-    return send_t(jnp.concatenate([p[1][0], p[3][0]], axis=0), 1), send_t(jnp.concatenate([p[2][1], p[3][1]], axis=0), 2)
-
-
-def scatter_t_middle(x, got):
-    count = x.shape[0] // TP
-    half = count // 2
+def scatter_t_middle(kept, got):
+    half = kept.shape[0] // 4
     first, second = got
 
     def add(low, v):
-        return x[low:low + half].astype(F32) + v.astype(F32)
-
-    on_a = add(2 * count, first[half:]).astype(BF16)
-    on_b = add(count + half, second[half:]).astype(BF16)
+        return kept[low:low + half].astype(F32) + v.astype(F32)
+
     part = jnp.concatenate([add(0, first[:half]), add(half, second[:half])], axis=0)
-    return part, (on_a, on_b)
+    return part, (add(2 * half, first[half:]).astype(BF16), add(3 * half, second[half:]).astype(BF16))
 
 
 def scatter_t_pass(passed):
@@ -1166,23 +1160,24 @@
         hm, g_gu = after(hm, g_gu)
         g_gus.append(sum_z(g_gu).reshape(TP, rows, -1))
     d_hm, _ = after(d_hm, g_gu)
-    d_attn, d_resid, g_norm_mlp, g_down, branch = relay_backward(
+    d_attn, d_resid, g_norm_mlp, g_down, *branch = relay_backward(
         d_hm.reshape(TP, mine, D), resid, cot, gain_mlp, hidden, d_branch, down, rows, zs, cs, 7)
     d_attn = d_attn.reshape(TP * mine, D)
     g_down = sum_z(g_down.reshape(-1, D))
 
     d_attn, g_gus[0] = after(d_attn, g_gus[0])
     d_attn, g_gus[1] = after(d_attn, g_gus[1])
-    first = scatter_t_send(branch)
+    first = send_t(branch[1], 1), send_t(branch[2], 2)
     d_act = dot_nt(d_attn, wo)
     count = TP * seqs
-    *begun, g_norm_head = slots_backward(pre, f_low, wfu, gain_head, docs, d_act, 0, count // 2)
+    ahead = count * 5 // 8
+    *begun, g_norm_head = slots_backward(pre, f_low, wfu, gain_head, docs, d_act, 0, ahead)
     first, begun = after(first, begun)
-    part, passed = scatter_t_middle(branch, first)
+    part, passed = scatter_t_middle(branch[0], first)
     d_act, passed = after(d_act, passed)
     second = scatter_t_pass(passed)
     d_pre, d_f, d_low, g_more = slots_backward(
-        pre, f_low, wfu, gain_head, docs, d_act, count // 2, count - count // 2, begun)
+        pre, f_low, wfu, gain_head, docs, d_act, ahead, count - ahead, begun)
     g_norm_head = g_norm_head + g_more
     d_pre, second = after(d_pre, second)
     g4, *g_gus = heads_gradient(h_own, h_other, d_pre, g_gus, 3)

time: 610 us -> 604 us (level)
  transfers between devices with their start and end apart: 26 -> 26, of which waited for: 9 -> 8; matrix products, arithmetic and copies ran while one was open for 21% -> 21% of each run, Pallas kernels for 61% -> 62%
where the time goes in v2:
time: 604 us; the launch traced here: 597 us
  Pallas kernels  370 us (61%)
  matrix products  67 us (11%)
  waiting for transfers between devices  56.3 us (9%)
  local copies, waits for them, and re-layouts  55.2 us (9%)
  starting transfers between devices  17.4 us (3%)
  other arithmetic  17 us (3%)
  between operations  14.9 us (2%)
    pallas_call x1, Pallas kernels, relay_backward(): pl.pallas_call(functools.partial(backward_relay_kernel, unit, SUBS, len(h...  77.4 us
    pallas_call x1, Pallas kernels, relay_forward(): pl.pallas_call(functools.partial(forward_relay_kernel, unit, SUBS), out_s...  72 us
    dot_general x11, matrix products, mm(): return lax.dot_general(a, b, (dims, ((), ())), preferred_element_type=F32)  67 us
    pallas_call x1, Pallas kernels, settle(): pl.pallas_call(functools.partial(settle_kernel, unit, SUBS), out_shape=(j...  53.8 us
    ppermute x15, waiting for transfers between devices, send_t(): return lax.ppermute(x, 't', [(i, i ^ step) for i in range(TP)])  46 us
    unnamed x87, local copies, waits for them, and re-layouts  28.2 us
    pallas_call x2, Pallas kernels, slots_backward(): pl.pallas_call(backward_kernel, out_shape=(jax.ShapeDtypeStruct((count *...  23.4 us
    pallas_call x2, Pallas kernels, ff_forward(): pl.pallas_call(functools.partial(ff_kernel, 256), out_shape=(jax.ShapeDty...  23 us
  transfers between devices with their start and end apart: 26, of which 8 were waited for; matrix products, arithmetic and copies ran while one was open for 21% of the time, Pallas kernels for 62%

profile of v2, /device:TPU:0, one launch (start us, length us, event | category | flops | bytes accessed | tf_op | source)
XLA Modules:
  0.0 597.5 jit_solution(4745348680567309185)
XLA Ops:
  12.5 16.7 %spread.1 = bf16[4,64,2048]{2,1,0:T(8,128)(2,1)} custom-call(bf16[64,2048]{1,0:T(8,128)(2,1)} %refs_0_.1, bf16[64,2048]{1,0:T(8,128)(2,1)} %refs_1_.1, bf16[64,2048]{1,0:T(8,128)(2,1)} %refs_2_.1, bf16[64,2048]{1,0:T(8,128)(2,1)} %refs_3_.1), custom_call_target="tpu_custom_call" | custom-call | tf_op jit(solution)/shard_map/spread/pallas_call | solution.py:371
  29.4 10.5 %share_small.1 = bf16[32,16,128]{2,1,0:T(8,128)(2,1)S(1)} custom-call(bf16[16,128]{1,0:T(8,128)(2,1)S(1)} %pad_bitcast_fusion.x_ref), custom_call_target="tpu_custom_call" | custom-call | tf_op jit(solution)/shard_map/share_small/pallas_call | solution.py:330
  40.0 22.2 %spread_ff.1 = (bf16[4,64,1536]{2,1,0:T(8,128)(2,1)}, bf16[4,64,1280]{2,1,0:T(8,128)(2,1)}) custom-call(bf16[64,5632]{1,0:T(8,128)(2,1)S(1)} %copy-done.19, bf16[64,5632]{1,0:T(8,128)(2,1)S(1)} %copy-done.20), custom_call_target="tpu_custom_call" | custom-call | tf_op jit(solution)/shard_map/spread_ff/pallas_call | solution.py:433
  79.3 9.4 %collective-permute-done.5 = bf16[256,2048]{1,0:T(8,128)(2,1)} collective-permute-done((bf16[256,2048]{1,0:T(8,128)(2,1)}, bf16[256,2048]{1,0:T(8,128)(2,1)}, u32[]{:S(2)}, u32[]{:S(2)}) %collective-permute-start.5) | collective-permute-done | bytes 1048608 | tf_op jit(solution)/shard_map/ppermute | solution.py:998
  93.0 18.2 %collective-permute-done.1 = bf16[256,2048]{1,0:T(8,128)(2,1)} collective-permute-done((bf16[256,2048]{1,0:T(8,128)(2,1)}, bf16[256,2048]{1,0:T(8,128)(2,1)}, u32[]{:S(2)}, u32[]{:S(2)}) %collective-permute-start.1) | collective-permute-done | bytes 1048608 | tf_op jit(solution)/shard_map/ppermute | solution.py:998
  124.8 8.1 %collective-permute-done.2 = bf16[128,2048]{1,0:T(8,128)(2,1)S(1)} collective-permute-done((bf16[128,2048]{1,0:T(8,128)(2,1)S(1)}, bf16[128,2048]{1,0:T(8,128)(2,1)S(1)}, u32[]{:S(2)}, u32[]{:S(2)}) %collective-permute-start.2) | collective-permute-done | bytes 524320 | tf_op jit(solution)/shard_map/ppermute | solution.py:998
  145.0 10.4 %fusion.21.d_hidden_ref = f32[1024,1408]{1,0:T(8,128)} fusion(bf16[1024,2048]{1,0:T(8,128)(2,1)} %constant_dynamic-update-slice_fusion.5.refs_2_, bf16[1408,2048]{1,0:T(8,128)(2,1)S(1)} %bitcast.98), kind=kOutput, calls=%fused_computation.71 | convolution fusion | flops 5905580032 | bytes 15728640 | tf_op jit(solution)/shard_map/dot_general | solution.py:21
  157.3 8.3 %collective-permute-done.9 = bf16[2,64,2048]{2,1,0:T(8,128)(2,1)S(1)} collective-permute-done((bf16[2,64,2048]{2,1,0:T(8,128)(2,1)S(1)}, bf16[2,64,2048]{2,1,0:T(8,128)(2,1)S(1)}, u32[]{:S(2)}, u32[]{:S(2)}) %collective-permute-start.9) | collective-permute-done | bytes 524320 | tf_op jit(solution)/shard_map/ppermute | solution.py:998
  167.6 4.6 constant_dynamic-slice_fusion.5
  172.3 3.4 convolution_convert_fusion.3.f_low_ref
  175.7 12.5 %fusion.22.pre_ref = f32[1024,2048]{1,0:T(8,128)S(1)} fusion(bf16[1024,2048]{1,0:T(8,128)(2,1)} %constant_dynamic-update-slice_fusion.h_hbm, bf16[2048,2048]{1,0:T(8,128)(2,1)} %all-gather.7.cloned.1.call-done), kind=kOutput, calls=%fused_computation.72 | convolution fusion | flops 8589934592 | bytes 20971520 | tf_op jit(solution)/shard_map/dot_general | solution.py:21
  188.3 10.7 %slots_forward.1.act_hbm = bf16[1024,512]{1,0:T(8,128)(2,1)S(1)} custom-call(f32[1024,2048]{1,0:T(8,128)S(1)} %fusion.22.pre_ref, bf16[1024,16]{1,0:T(8,128)(2,1)S(1)} %convolution_convert_fusion.3.f_low_ref, bf16[16,64]{1,0:T(8,128)(2,1)S(1)} %copy.58.wfu_ref, f32[1,512]{1,0:T(1,128)S(1)} %reshape.264.gain_ref, f32[8,128,1]{2,1,0:T(8,128)S(1)} %reshape.269.doc_col_ref, ...), custom_call_target="tpu_custom_call" | custom-call | tf_op jit(solution)/shard_map/slots_forward/pallas_call | solution.py:252
  201.4 72.0 %relay_forward.1 = (bf16[4,256,2048]{2,1,0:T(8,128)(2,1)S(1)}, f32[256,2048]{1,0:T(8,128)S(1)}) custom-call(bf16[4,256,2048]{2,1,0:T(8,128)(2,1)S(1)} %bitcast.95, bf16[256,2048]{1,0:T(8,128)(2,1)S(1)} %bitcast.94, f32[1,2048]{1,0:T(1,128)S(1)} %reshape.267.gain_ref), custom_call_target="tpu_custom_call" | custom-call | tf_op jit(solution)/shard_map/relay_forward/pallas_call | solution.py:794
  276.6 12.1 %feed_forward.2 = (bf16[1024,768]{1,0:T(8,128)(2,1)S(1)}, bf16[1024,1536]{1,0:T(8,128)(2,1)S(1)}) custom-call(bf16[1024,2048]{1,0:T(8,128)(2,1)} %bitcast.87, bf16[2048,1536]{1,0:T(8,128)(2,1)} %all-gather.9.cloned.1.call-done.gu_ref.refs_2_, f32[1024,1408]{1,0:T(8,128)} %fusion.21.d_hidden_ref), custom_call_target="tpu_custom_call" | custom-call | tf_op jit(solution)/shard_map/feed_forward/pallas_call | solution.py:891
  288.7 3.7 convolution_convert_fusion.2
  292.5 5.6 collective-permute-done.11
  298.2 4.8 add_convert_fusion.1
  303.1 10.9 %feed_forward.3 = (bf16[1024,640]{1,0:T(8,128)(2,1)S(1)}, bf16[1024,1280]{1,0:T(8,128)(2,1)S(1)}) custom-call(bf16[1024,2048]{1,0:T(8,128)(2,1)} %bitcast.88, bf16[2048,1280]{1,0:T(8,128)(2,1)} %all-gather.11.cloned.1.call-done.gu_ref.refs_3_, f32[1024,1408]{1,0:T(8,128)} %fusion.21.d_hidden_ref), custom_call_target="tpu_custom_call" | custom-call | tf_op jit(solution)/shard_map/feed_forward/pallas_call | solution.py:891
  314.1 4.3 convolution_convert_fusion.1
  318.6 15.7 %d_hm.1 = bf16[1024,2048]{1,0:T(8,128)(2,1)} custom-call(bf16[1024,1536]{1,0:T(8,128)(2,1)S(1)} %copy-done.12, bf16[1024,1280]{1,0:T(8,128)(2,1)S(1)} %get-tuple-element.120.refs_1_, bf16[2048,1536]{1,0:T(8,128)(2,1)} %all-gather.9.cloned.1.call-done.gu_ref.refs_2_, bf16[2048,1280]{1,0:T(8,128)(2,1)} %all-gather.11.cloned.1.call-done.gu_ref.refs_3_), custom_call_target="tpu_custom_call" | custom-call | tf_op jit(solution)/shard_map/d_hm/pallas_call | solution.py:916
  334.3 4.2 add_convert_fusion.2
  339.0 77.4 %relay_backward.1 = (bf16[4,256,2048]{2,1,0:T(8,128)(2,1)}, f32[256,2048]{1,0:T(8,128)}, f32[1,2048]{1,0:T(1,128)}, bf16[4,176,2048]{2,1,0:T(8,128)(2,1)}, bf16[...) custom-call(bf16[4,256,2048]{2,1,0:T(8,128)(2,1)} %bitcast.101, f32[256,2048]{1,0:T(8,128)} %copy-done.7, ...), custom_call_target="tpu_custom_call" | custom-call | tf_op jit(solution)/shard_map/relay_backward/pallas_call | solution.py:813
  418.8 5.2 fusion.23.d_act_ref
  424.0 3.7 copy-done.1
  427.8 14.5 %slots_backward.2 = (bf16[1024,2048]{1,0:T(8,128)(2,1)S(1)}, bf16[1024,64]{1,0:T(8,128)(2,1)S(1)}, bf16[1024,16]{1,0:T(8,128)(2,1)S(1)}, f32[1,512]{1,0:T(1,128)S(1)}) custom-call(f32[1024,2048]{1,0:T(8,128)S(1)} %copy-done.1, bf16[1024,16]{1,0:T(8,128)(2,1)S(1)} %convolution_convert_fusion.3.f_low_ref, bf16[16,64]{1,0:T(8,128)(2,1)S(1)} %copy.58.wfu_ref, ...), custom_call_target="tpu_custom_call" | custom-call | tf_op jit(solution)/shard_map/slots_backward/pallas_call | solution.py:270
  442.3 3.3 convert_add_fusion.1
  447.8 8.9 %slots_backward.3 = (bf16[1024,2048]{1,0:T(8,128)(2,1)S(1)}, bf16[1024,64]{1,0:T(8,128)(2,1)S(1)}, bf16[1024,16]{1,0:T(8,128)(2,1)S(1)}, f32[1,512]{1,0:T(1,128)S(1)}) custom-call(f32[1024,2048]{1,0:T(8,128)S(1)} %copy-done.1, bf16[1024,16]{1,0:T(8,128)(2,1)S(1)} %convolution_convert_fusion.3.f_low_ref, ...), custom_call_target="tpu_custom_call", output_to_operand_aliasing={{0}: (7, {}), {1}: (8, {}), {2}: (9, {})} | custom-call | tf_op jit(solution)/shard_map/slots_backward/pallas_call | solution.py:270
  458.8 18.9 %heads_gradient.1 = (bf16[1024,2048]{1,0:T(8,128)(2,1)}, bf16[4,64,1536]{2,1,0:T(8,128)(2,1)}, bf16[4,64,1280]{2,1,0:T(8,128)(2,1)}) custom-call(bf16[1024,1024]{1,0:T(8,128)(2,1)} %get-tuple-element.107.own_hbm, bf16[1024,1024]{1,0:T(8,128)(2,1)} %get-tuple-element.108.other_hbm, bf16[1024,2048]{1,0:T(8,128)(2,1)} %copy-done.2, ...), custom_call_target="tpu_custom_call" | custom-call | tf_op jit(solution)/shard_map/heads_gradient/pallas_call | solution.py:974
  479.0 12.8 %fusion.24 = f32[1024,2048]{1,0:T(8,128)S(1)} fusion(bf16[1024,2048]{1,0:T(8,128)(2,1)} %copy-done.2, bf16[2048,2048]{1,0:T(8,128)(2,1)} %all-gather.7.cloned.1.call-done), kind=kOutput, calls=%fused_computation.74 | convolution fusion | flops 8589934592 | bytes 20971520 | tf_op jit(solution)/shard_map/dot_general | solution.py:21
  495.0 53.8 %settle.1 = (bf16[256,2048]{1,0:T(8,128)(2,1)}, f32[32,24,128]{2,1,0:T(8,128)}, bf16[4,1,64,2048]{3,2,1,0:T(8,128)(2,1)}) custom-call(bf16[4,256,2048]{2,1,0:T(8,128)(2,1)} %bitcast.100, bf16[256,2048]{1,0:T(8,128)(2,1)} %bitcast.93, f32[256,2048]{1,0:T(8,128)} %get-tuple-element.156.d_resid_ref, f32[1,2048]{1,0:T(1,128)} %reshape.268.gain_ref, ...), custom_call_target="tpu_custom_call" | custom-call | tf_op jit(solution)/shard_map/settle/pallas_call | solution.py:846
  557.7 21.9 %finish.1 = (f32[24,128]{1,0:T(8,128)S(1)}, bf16[4,64,2048]{2,1,0:T(8,128)(2,1)S(1)}) custom-call(f32[32,24,128]{2,1,0:T(8,128)S(1)} %copy-done.22, bf16[4,64,2048]{2,1,0:T(8,128)(2,1)S(1)} %bitcast.96), custom_call_target="tpu_custom_call" | custom-call | tf_op jit(solution)/shard_map/finish/pallas_call | solution.py:517
  583.5 4.5 reduce-scatter.14.cloned.1.call-done
  (197 shorter events, 89.1 us)
Async XLA Ops:
  7.2 129.0 %all-gather.5.cloned.1.call-start = ((), (), s32[]{:S(2)}) async-start(), calls=%async_computation.5 | async-start | bytes 8847360 | tf_op jit(solution)/shard_map/all_gather | solution.py:1097
  9.6 54.7 %copy-start.6 = (bf16[2,128,2048]{2,1,0:T(8,128)(2,1)S(1)}, bf16[2,128,2048]{2,1,0:T(8,128)(2,1)}, u32[]{:S(2)}) copy-start(bf16[2,128,2048]{2,1,0:T(8,128)(2,1)} %param.16) | copy-start | bytes 3145732
  9.6 166.1 %all-gather.7.cloned.1.call-start = ((), (), s32[]{:S(2)}) async-start(), calls=%async_computation.6 | async-start | bytes 9437184 | tf_op jit(solution)/shard_map/all_gather | solution.py:1123
  29.4 247.3 %all-gather.9.cloned.1.call-start = ((), (), s32[]{:S(2)}) async-start(), calls=%async_computation.7 | async-start | bytes 7077888 | tf_op jit(solution)/shard_map/all_gather | solution.py:1123
  62.2 240.9 %all-gather.11.cloned.1.call-start = ((), (), s32[]{:S(2)}) async-start(), calls=%async_computation.8 | async-start | bytes 5898240 | tf_op jit(solution)/shard_map/all_gather | solution.py:1123
  62.2 26.5 %collective-permute-start.5 = (bf16[256,2048]{1,0:T(8,128)(2,1)}, bf16[256,2048]{1,0:T(8,128)(2,1)}, u32[]{:S(2)}, u32[]{:S(2)}) collective-permute-start(bf16[256,2048]{1,0:T(8,128)(2,1)} %bitcast.104), channel_id=1, source_target_pairs={{0,4},{2,6},{4,0},{6,2},{1,5},{3,7},{5,1},{7,3},{8,12},{10,14},{12... | collective-permute-start | bytes 3145736 | tf_op jit(solution)/shard_map/ppermute | solution.py:998
  63.3 27.6 %collective-permute-start.4 = (bf16[256,2048]{1,0:T(8,128)(2,1)}, bf16[256,2048]{1,0:T(8,128)(2,1)}, u32[]{:S(2)}, u32[]{:S(2)}) collective-permute-start(bf16[256,2048]{1,0:T(8,128)(2,1)} %bitcast.105), channel_id=1, source_target_pairs={{0,2},{2,0},{4,6},{6,4},{1,3},{3,1},{5,7},{7,5},{8,10},{10,8},{12,... | collective-permute-start | bytes 3145736 | tf_op jit(solution)/shard_map/ppermute | solution.py:998
  71.8 39.4 %collective-permute-start.1 = (bf16[256,2048]{1,0:T(8,128)(2,1)}, bf16[256,2048]{1,0:T(8,128)(2,1)}, u32[]{:S(2)}, u32[]{:S(2)}) collective-permute-start(bf16[256,2048]{1,0:T(8,128)(2,1)} %copy.46), channel_id=1, source_target_pairs={{0,4},{2,6},{4,0},{6,2},{1,5},{3,7},{5,1},{7,3},{8,12},{10,14},{12... | collective-permute-start | bytes 3145736 | tf_op jit(solution)/shard_map/ppermute | solution.py:998
  72.9 40.5 %collective-permute-start = (bf16[256,2048]{1,0:T(8,128)(2,1)}, bf16[256,2048]{1,0:T(8,128)(2,1)}, u32[]{:S(2)}, u32[]{:S(2)}) collective-permute-start(bf16[256,2048]{1,0:T(8,128)(2,1)} %copy.46), channel_id=1, source_target_pairs={{0,2},{2,0},{4,6},{6,4},{1,3},{3,1},{5,7},{7,5},{8,10},{10,8},{12,... | collective-permute-start | bytes 3145736 | tf_op jit(solution)/shard_map/ppermute | solution.py:998
  73.9 344.9 %reduce-scatter.6.cloned.1.call-start = ((), (), s32[]{:S(2)}) async-start(), calls=%async_computation.9 | async-start | bytes 3932160 | tf_op jit(solution)/shard_map/reduce_scatter | solution.py:1082
  75.1 126.3 %copy-start.23 = (f32[1,2048]{1,0:T(1,128)}, f32[1,2048]{1,0:T(1,128)S(1)}, u32[]{:S(2)}) copy-start(f32[1,2048]{1,0:T(1,128)S(1)} %reshape.267.gain_ref) | copy-start | bytes 24580
  89.8 44.8 %collective-permute-start.6 = (bf16[128,2048]{1,0:T(8,128)(2,1)S(1)}, bf16[128,2048]{1,0:T(8,128)(2,1)S(1)}, u32[]{:S(2)}, u32[]{:S(2)}) collective-permute-start(bf16[128,2048]{1,0:T(8,128)(2,1)S(1)} %slice.103), channel_id=1, source_target_pairs={{0,2},{2,0},{4,6},{6,4},{1,3},{3,1},{5,7},{7,5},{8,10},{10,8},{12,... | collective-permute-start | bytes 1572872 | tf_op jit(solution)/shard_map/ppermute | solution.py:998
  92.0 43.4 %collective-permute-start.7 = (bf16[128,2048]{1,0:T(8,128)(2,1)S(1)}, bf16[128,2048]{1,0:T(8,128)(2,1)S(1)}, u32[]{:S(2)}, u32[]{:S(2)}) collective-permute-start(bf16[128,2048]{1,0:T(8,128)(2,1)S(1)} %slice.104), channel_id=1, source_target_pairs={{0,4},{2,6},{4,0},{6,2},{1,5},{3,7},{5,1},{7,3},{8,12},{10,14},{12... | collective-permute-start | bytes 1572872 | tf_op jit(solution)/shard_map/ppermute | solution.py:998
  112.3 20.7 %collective-permute-start.2 = (bf16[128,2048]{1,0:T(8,128)(2,1)S(1)}, bf16[128,2048]{1,0:T(8,128)(2,1)S(1)}, u32[]{:S(2)}, u32[]{:S(2)}) collective-permute-start(bf16[128,2048]{1,0:T(8,128)(2,1)S(1)} %slice.101), channel_id=1, source_target_pairs={{0,2},{2,0},{4,6},{6,4},{1,3},{3,1},{5,7},{7,5},{8,10},{10,8},{12,... | collective-permute-start | bytes 1572872 | tf_op jit(solution)/shard_map/ppermute | solution.py:998
  114.5 19.3 %collective-permute-start.3 = (bf16[128,2048]{1,0:T(8,128)(2,1)S(1)}, bf16[128,2048]{1,0:T(8,128)(2,1)S(1)}, u32[]{:S(2)}, u32[]{:S(2)}) collective-permute-start(bf16[128,2048]{1,0:T(8,128)(2,1)S(1)} %slice.102), channel_id=1, source_target_pairs={{0,4},{2,6},{4,0},{6,2},{1,5},{3,7},{5,1},{7,3},{8,12},{10,14},{12... | collective-permute-start | bytes 1572872 | tf_op jit(solution)/shard_map/ppermute | solution.py:998
  141.4 15.8 %collective-permute-start.10 = (bf16[2,64,2048]{2,1,0:T(8,128)(2,1)S(1)}, bf16[2,64,2048]{2,1,0:T(8,128)(2,1)S(1)}, u32[]{:S(2)}, u32[]{:S(2)}) collective-permute-start(bf16[2,64,2048]{2,1,0:T(8,128)(2,1)S(1)} %get-tuple-element.232), channel_id=1, source_target_pairs={{0,6},{2,4},{4,2},{6,0},{1,7},{3,5},{5,3},{7,1},{8,14},{10,12},{12... | collective-permute-start | bytes 1572872 | tf_op jit(solution)/shard_map/ppermute | solution.py:998
  142.6 22.9 %collective-permute-start.9 = (bf16[2,64,2048]{2,1,0:T(8,128)(2,1)S(1)}, bf16[2,64,2048]{2,1,0:T(8,128)(2,1)S(1)}, u32[]{:S(2)}, u32[]{:S(2)}) collective-permute-start(bf16[2,64,2048]{2,1,0:T(8,128)(2,1)S(1)} %get-tuple-element.233), channel_id=1, source_target_pairs={{0,4},{2,6},{4,0},{6,2},{1,5},{3,7},{5,1},{7,3},{8,12},{10,14},{12... | collective-permute-start | bytes 1572872 | tf_op jit(solution)/shard_map/ppermute | solution.py:998
  143.8 21.8 %collective-permute-start.8 = (bf16[2,64,2048]{2,1,0:T(8,128)(2,1)S(1)}, bf16[2,64,2048]{2,1,0:T(8,128)(2,1)S(1)}, u32[]{:S(2)}, u32[]{:S(2)}) collective-permute-start(bf16[2,64,2048]{2,1,0:T(8,128)(2,1)S(1)} %get-tuple-element.234), channel_id=1, source_target_pairs={{0,2},{2,0},{4,6},{6,4},{1,3},{3,1},{5,7},{7,5},{8,10},{10,8},{12,... | collective-permute-start | bytes 1572872 | tf_op jit(solution)/shard_map/ppermute | solution.py:998
  175.7 272.1 %copy-start.9 = (bf16[1024,16]{1,0:T(8,128)(2,1)}, bf16[1024,16]{1,0:T(8,128)(2,1)S(1)}, u32[]{:S(2)}) copy-start(bf16[1024,16]{1,0:T(8,128)(2,1)S(1)} %convolution_convert_fusion.3.f_low_ref) | copy-start | bytes 98308
  292.5 5.7 collective-permute-start.11
  303.1 115.7 %reduce-scatter.8.cloned.1.call-start = ((), (), s32[]{:S(2)}) async-start(), calls=%async_computation.10 | async-start | bytes 3276800 | tf_op jit(solution)/shard_map/reduce_scatter | solution.py:1082
  318.3 16.0 %collective-permute-start.12 = (bf16[1024,1280]{1,0:T(8,128)(2,1)}, bf16[1024,1280]{1,0:T(8,128)(2,1)S(1)}, u32[]{:S(2)}, u32[]{:S(2)}) collective-permute-start(bf16[1024,1280]{1,0:T(8,128)(2,1)} %convolution_convert_fusion.1), channel_id=1, source_target_pairs={{0,1},{1,0},{2,3},{3,2},{4,5},{5,4},{6,7},{7,6},{8,9},{9,8},{10,11... | collective-permute-start | bytes 7864328 | tf_op jit(solution)/shard_map/ppermute | solution.py:1002
  338.6 140.5 %reduce-scatter.12.cloned.1.call-start = ((), (), s32[]{:S(2)}) async-start(), calls=%async_computation.12 | async-start | bytes 3604480 | tf_op jit(solution)/shard_map/reduce_scatter | solution.py:1082
  416.5 140.0 %reduce-scatter.10.cloned.1.call-start = ((), (), s32[]{:S(2)}) async-start(), calls=%async_computation.11 | async-start | bytes 5242880 | tf_op jit(solution)/shard_map/reduce_scatter | solution.py:1082
  416.7 25.6 %collective-permute-start.13 = (bf16[256,2048]{1,0:T(8,128)(2,1)}, bf16[256,2048]{1,0:T(8,128)(2,1)S(1)}, u32[]{:S(2)}, u32[]{:S(2)}) collective-permute-start(bf16[256,2048]{1,0:T(8,128)(2,1)} %get-tuple-element.132), channel_id=1, source_target_pairs={{0,2},{2,0},{4,6},{6,4},{1,3},{3,1},{5,7},{7,5},{8,10},{10,8},{12,... | collective-permute-start | bytes 3145736 | tf_op jit(solution)/shard_map/ppermute | solution.py:998
  417.3 25.0 %collective-permute-start.14 = (bf16[256,2048]{1,0:T(8,128)(2,1)}, bf16[256,2048]{1,0:T(8,128)(2,1)}, u32[]{:S(2)}, u32[]{:S(2)}) collective-permute-start(bf16[256,2048]{1,0:T(8,128)(2,1)} %get-tuple-element.133), channel_id=1, source_target_pairs={{0,4},{2,6},{4,0},{6,2},{1,5},{3,7},{5,1},{7,3},{8,12},{10,14},{12... | collective-permute-start | bytes 3145736 | tf_op jit(solution)/shard_map/ppermute | solution.py:998
  445.6 13.1 %collective-permute-start.15 = (bf16[128,2048]{1,0:T(8,128)(2,1)S(1)}, bf16[128,2048]{1,0:T(8,128)(2,1)S(1)}, u32[]{:S(2)}, u32[]{:S(2)}) collective-permute-start(bf16[128,2048]{1,0:T(8,128)(2,1)S(1)} %get-tuple-element.144), channel_id=1, source_target_pairs={{0,4},{2,6},{4,0},{6,2},{1,5},{3,7},{5,1},{7,3},{8,12},{10,14},{12... | collective-permute-start | bytes 1572872 | tf_op jit(solution)/shard_map/ppermute | solution.py:998
  446.8 12.0 %collective-permute-start.16 = (bf16[128,2048]{1,0:T(8,128)(2,1)S(1)}, bf16[128,2048]{1,0:T(8,128)(2,1)S(1)}, u32[]{:S(2)}, u32[]{:S(2)}) collective-permute-start(bf16[128,2048]{1,0:T(8,128)(2,1)S(1)} %get-tuple-element.145), channel_id=1, source_target_pairs={{0,2},{2,0},{4,6},{6,4},{1,3},{3,1},{5,7},{7,5},{8,10},{10,8},{12,... | collective-permute-start | bytes 1572872 | tf_op jit(solution)/shard_map/ppermute | solution.py:998
  458.6 33.2 %copy-start.13 = (bf16[1024,16]{1,0:T(8,128)(2,1)}, bf16[1024,16]{1,0:T(8,128)(2,1)S(1)}, u32[]{:S(2)}) copy-start(bf16[1024,16]{1,0:T(8,128)(2,1)S(1)} %get-tuple-element.155.d_low_ref) | copy-start | bytes 98308
  477.7 110.2 %reduce-scatter.14.cloned.1.call-start = ((), (), s32[]{:S(2)}) async-start(), calls=%async_computation.13 | async-start | bytes 1310720 | tf_op jit(solution)/shard_map/reduce_scatter | solution.py:1082
  495.0 56.4 %copy-start.21 = (bf16[4,64,1280]{2,1,0:T(8,128)(2,1)S(1)}, bf16[4,64,1280]{2,1,0:T(8,128)(2,1)}, u32[]{:S(2)}) copy-start(bf16[4,64,1280]{2,1,0:T(8,128)(2,1)} %get-tuple-element.166.refs_1_) | copy-start | bytes 1966084
  553.5 36.2 %copy-start.29 = (bf16[256,2048]{1,0:T(8,128)(2,1)S(1)}, bf16[256,2048]{1,0:T(8,128)(2,1)}, u32[]{:S(2)}) copy-start(bf16[256,2048]{1,0:T(8,128)(2,1)} %get-tuple-element.171) | copy-start | bytes 3145732
  (30 other events, 322.2 us)
Sparse Core Ops, SparseCore 0:
  10.3 83.1 all-gather.4
  95.1 80.5 all-gather.6
  177.3 63.2 all-gather.8
  242.0 56.3 all-gather.10
  303.2 59.0 reduce-scatter.5
  364.5 52.1 reduce-scatter.7
  418.9 55.8 reduce-scatter.11
  477.8 76.0 reduce-scatter.9
  556.3 31.5 reduce-scatter.13

commit v3 on v2

--- a/solution.py
+++ b/solution.py
@@ -541,7 +541,8 @@
     return pieces
 
 
-def relay(p_ref, o_ref, got1, pass2, got2, sems, subs, middle, shared=True, beside=None, plane=False, cores=False):
+def relay(p_ref, o_ref, got1, pass2, got2, sems, subs, middle, shared=True, beside=None, plane=False, cores=False,
+          source=None, ready=None, landed=None):
     z, t, c = (lax.axis_index(a) for a in ALL)
     peers = {step: (z, chip_peer(t, step), c) for step in (1, 2)}
     barrier = pltpu.get_barrier_semaphore()
@@ -569,9 +570,13 @@
     def local(i):
         return pl.ds(i * size, size)
 
-    first = [[[start(p_ref.at[near if j == 0 else 3, part(w, i)], got1.at[w, j, local(i)], near, 2 * w + j, i)
+    source = p_ref if source is None else source
+    landed = landed or (lambda block, w, i: None)
+    first = [[[start(source.at[near if j == 0 else 3, part(w, i)], got1.at[w, j, local(i)], near, 2 * w + j, i)
                for j in (0, 1)] for w, (near, far) in enumerate(ways)] for i in range(subs)]
     second, third, fourth = [None] * subs, [None] * subs, []
+    if ready is not None:
+        ready()
     for i in range(subs + 2):
         if i < subs:
             second[i] = []
@@ -595,20 +600,24 @@
                 o_ref[0, part(w, k)] = rows
                 third[k].append([start(o_ref.at[0, part(w, k)], o_ref.at[step, part(w, k)], step, 5 + 2 * w + step, k)
                                  for step in (1, 2)])
-        if beside is not None:
-            beside(i)
+                landed(0, w, k)
         if i >= 2 and shared:
             k = i - 2
             for w, (near, far) in enumerate(ways):
                 third[k][w][far - 1].wait_recv()
                 fourth.append(start(o_ref.at[far, part(w, k)], o_ref.at[3, part(w, k)], near, 10 + w, k))
+                landed(far, w, k)
+        if beside is not None:
+            beside(i)
     for copy in copies:
         copy.wait_send()
     for k in range(subs if shared else 0):
         for w, (near, far) in enumerate(ways):
             third[k][w][near - 1].wait_recv()
-    for copy in fourth:
+            landed(near, w, k)
+    for at, copy in enumerate(fourth):
         copy.wait_recv()
+        landed(3, at % 2, at // 2)
 
 
 def forward_relay_kernel(unit, subs, p_ref, x_ref, gain_ref, o_ref, resid_ref, got1, pass2, got2, ordered, *sems):
@@ -647,12 +656,12 @@
     return middle
 
 
-def backward_relay_kernel(unit, subs, parts, p_ref, resid_ref, cot_ref, gain_ref, *refs):
-    hidden_hbm, (branch_hbm, down_hbm, o_ref, d_resid_ref, g_gain_ref, g_down_hbm, kept_hbm, one_hbm, two_hbm, *refs) = refs[:parts], refs[parts:]
+def backward_relay_kernel(unit, subs, parts, p_hbm, resid_hbm, cot_hbm, gain_ref, *refs):
+    hidden_hbm, (branch_hbm, down_hbm, o_hbm, d_resid_hbm, g_gain_ref, g_down_hbm, kept_hbm, one_hbm, two_hbm, *refs) = refs[:parts], refs[parts:]
     (got1, pass2, got2, ordered, send_sem, recv_sem, hidden, branch, down, g_down, g_other, terms,
-     in_sem, out_sem, core_send, core_recv) = refs
+     in_sem, out_sem, core_send, core_recv, p_ref, resid_ref, cot_ref, o_ref, d_resid_ref, block_sem, resid_sem) = refs
     z, t, c = (lax.axis_index(a) for a in ALL)
-    loads, at = [], 0
+    loads, at = [(p_hbm, p_ref), (resid_hbm, resid_ref), (cot_hbm, cot_ref)], 0
     for source in hidden_hbm:
         loads.append((source, hidden.at[:, at:at + source.shape[1]]))
         at += source.shape[1]
@@ -666,7 +675,7 @@
 
     def beside(i):
         if i == 0:
-            for copy in loads:
+            for copy in loads[1:]:
                 copy.wait()
         cols = slice(i * width, (i + 1) * width)
         if i < subs:
@@ -701,7 +710,18 @@
         return d.astype(BF16)
 
     middle = norm_backward(unit, resid_ref, gain_ref, g_gain_ref, ordered, finish)
-    relay(p_ref, o_ref, got1, pass2, got2, (send_sem, recv_sem), subs, middle, beside=beside, cores=True)
+    part = o_ref.shape[1] // (2 * subs)
+
+    def landed(block, w, i):
+        rows = pl.ds((w * subs + i) * part, part)
+        stores.append(pltpu.make_async_copy(o_ref.at[block, rows], o_hbm.at[block, rows], block_sem.at[block, w, i]))
+        stores[-1].start()
+        if block == 0:
+            stores.append(pltpu.make_async_copy(d_resid_ref.at[rows], d_resid_hbm.at[rows], resid_sem.at[w, i]))
+            stores[-1].start()
+
+    relay(p_ref, o_ref, got1, pass2, got2, (send_sem, recv_sem), subs, middle, beside=beside, cores=True,
+          source=p_hbm, ready=loads[0].wait, landed=landed)
     for copy in stores:
         copy.wait()
 
@@ -818,8 +838,8 @@
             jax.ShapeDtypeStruct((1, D), F32),
             jax.ShapeDtypeStruct((zs, each, D), BF16),
         ) + tuple(jax.ShapeDtypeStruct((rows, D), BF16) for rows in (tokens // 2, tokens // 4, tokens // 4)),
-        in_specs=[fast] * 4 + [anywhere] * (len(hidden) + 2),
-        out_specs=(fast,) * 3 + (anywhere,) * 4,
+        in_specs=[anywhere] * 3 + [fast] + [anywhere] * (len(hidden) + 2),
+        out_specs=(anywhere,) * 2 + (fast,) + (anywhere,) * 4,
         scratch_shapes=relay_scratch(count, D, SUBS) + [
             pltpu.VMEM((tokens, units), BF16),
             pltpu.VMEM(branch.shape, BF16),
@@ -827,10 +847,17 @@
             pltpu.VMEM((SUBS, zs, cs, each, width), BF16),
             pltpu.VMEM((SUBS, zs, each, width), BF16),
             pltpu.VMEM((SUBS, tokens, width), BF16),
-            pltpu.SemaphoreType.DMA((len(hidden) + 2,)),
+            pltpu.SemaphoreType.DMA((len(hidden) + 5,)),
             pltpu.SemaphoreType.DMA((8, SUBS)),
             pltpu.SemaphoreType.DMA((SUBS,)),
             pltpu.SemaphoreType.DMA((SUBS,)),
+            pltpu.VMEM(p.shape, BF16),
+            pltpu.VMEM(resid.shape, F32),
+            pltpu.VMEM(cot.shape, BF16),
+            pltpu.VMEM(p.shape, BF16),
+            pltpu.VMEM(resid.shape, F32),
+            pltpu.SemaphoreType.DMA((TP, 2, SUBS)),
+            pltpu.SemaphoreType.DMA((2, SUBS)),
         ],
         compiler_params=pltpu.CompilerParams(collective_id=ident, has_side_effects=True, vmem_limit_bytes=60 << 20),
         name="relay_backward",
@@ -1102,7 +1129,7 @@
     small = share(small, n, cs, 9)
     piece = cs * ff_rows
     units = zs * piece
-    middle = (units // LANES + 1) // 2 * 2 * LANES
+    middle = units // LANES // 2 * 2 * LANES
     parts = ((0, middle), (middle, 2 * units))
     w_gate, small = after(w_gate, small)
     gus = spread_ff(w_gate, w_up, piece, parts, 2)
@@ -1168,7 +1195,7 @@
     d_attn, g_gus[0] = after(d_attn, g_gus[0])
     d_attn, g_gus[1] = after(d_attn, g_gus[1])
     first = send_t(branch[1], 1), send_t(branch[2], 2)
-    d_act = dot_nt(d_attn, wo)
+    d_act = dot_nt(d_attn, wo).astype(BF16)
     count = TP * seqs
     ahead = count * 5 // 8
     *begun, g_norm_head = slots_backward(pre, f_low, wfu, gain_head, docs, d_act, 0, ahead)

time: 604 us -> 602 us (level)
  transfers between devices with their start and end apart: 26 -> 26, of which waited for: 8 -> 8; matrix products, arithmetic and copies ran while one was open for 21% -> 21% of each run, Pallas kernels for 62% -> 61%
where the time goes in v3:
time: 602 us; the launch traced here: 596 us
  Pallas kernels  366 us (61%)
  matrix products  67.6 us (11%)
  local copies, waits for them, and re-layouts  58.7 us (10%)
  waiting for transfers between devices  54.7 us (9%)
  starting transfers between devices  17.4 us (3%)
  other arithmetic  16.8 us (3%)
  between operations  14.9 us (2%)
    pallas_call x1, Pallas kernels, relay_backward(): pl.pallas_call(functools.partial(backward_relay_kernel, unit, SUBS, len(h...  74.4 us
    pallas_call x1, Pallas kernels, relay_forward(): pl.pallas_call(functools.partial(forward_relay_kernel, unit, SUBS), out_s...  72 us
    dot_general x11, matrix products, mm(): return lax.dot_general(a, b, (dims, ((), ())), preferred_element_type=F32)  67.6 us
    pallas_call x1, Pallas kernels, settle(): pl.pallas_call(functools.partial(settle_kernel, unit, SUBS), out_shape=(j...  53.2 us
    ppermute x15, waiting for transfers between devices, send_t(): return lax.ppermute(x, 't', [(i, i ^ step) for i in range(TP)])  44.4 us
    unnamed x87, local copies, waits for them, and re-layouts  29.9 us
    pallas_call x2, Pallas kernels, slots_backward(): pl.pallas_call(backward_kernel, out_shape=(jax.ShapeDtypeStruct((count *...  23.4 us
    pallas_call x2, Pallas kernels, ff_forward(): pl.pallas_call(functools.partial(ff_kernel, 256), out_shape=(jax.ShapeDty...  22.9 us
  transfers between devices with their start and end apart: 26, of which 8 were waited for; matrix products, arithmetic and copies ran while one was open for 21% of the time, Pallas kernels for 61%

profile of v3, /device:TPU:0, one launch (start us, length us, event | category | flops | bytes accessed | tf_op | source)
XLA Modules:
  0.0 595.6 jit_solution(15266649684517574691)
XLA Ops:
  12.4 16.7 %spread.1 = bf16[4,64,2048]{2,1,0:T(8,128)(2,1)} custom-call(bf16[64,2048]{1,0:T(8,128)(2,1)} %refs_0_.1, bf16[64,2048]{1,0:T(8,128)(2,1)} %refs_1_.1, bf16[64,2048]{1,0:T(8,128)(2,1)} %refs_2_.1, bf16[64,2048]{1,0:T(8,128)(2,1)} %refs_3_.1), custom_call_target="tpu_custom_call" | custom-call | tf_op jit(solution)/shard_map/spread/pallas_call | solution.py:371
  29.4 10.4 %share_small.1 = bf16[32,16,128]{2,1,0:T(8,128)(2,1)S(1)} custom-call(bf16[16,128]{1,0:T(8,128)(2,1)S(1)} %pad_bitcast_fusion.x_ref), custom_call_target="tpu_custom_call" | custom-call | tf_op jit(solution)/shard_map/share_small/pallas_call | solution.py:330
  39.9 22.3 %spread_ff.1 = (bf16[4,64,1280]{2,1,0:T(8,128)(2,1)}, bf16[4,64,1536]{2,1,0:T(8,128)(2,1)}) custom-call(bf16[64,5632]{1,0:T(8,128)(2,1)S(1)} %copy-done.19, bf16[64,5632]{1,0:T(8,128)(2,1)S(1)} %copy-done.20), custom_call_target="tpu_custom_call" | custom-call | tf_op jit(solution)/shard_map/spread_ff/pallas_call | solution.py:433
  81.1 7.6 %collective-permute-done.5 = bf16[256,2048]{1,0:T(8,128)(2,1)} collective-permute-done((bf16[256,2048]{1,0:T(8,128)(2,1)}, bf16[256,2048]{1,0:T(8,128)(2,1)}, u32[]{:S(2)}, u32[]{:S(2)}) %collective-permute-start.5) | collective-permute-done | bytes 1048608 | tf_op jit(solution)/shard_map/ppermute | solution.py:1025
  93.0 18.2 %collective-permute-done.1 = bf16[256,2048]{1,0:T(8,128)(2,1)} collective-permute-done((bf16[256,2048]{1,0:T(8,128)(2,1)}, bf16[256,2048]{1,0:T(8,128)(2,1)}, u32[]{:S(2)}, u32[]{:S(2)}) %collective-permute-start.1) | collective-permute-done | bytes 1048608 | tf_op jit(solution)/shard_map/ppermute | solution.py:1025
  124.8 8.2 %collective-permute-done.2 = bf16[128,2048]{1,0:T(8,128)(2,1)S(1)} collective-permute-done((bf16[128,2048]{1,0:T(8,128)(2,1)S(1)}, bf16[128,2048]{1,0:T(8,128)(2,1)S(1)}, u32[]{:S(2)}, u32[]{:S(2)}) %collective-permute-start.2) | collective-permute-done | bytes 524320 | tf_op jit(solution)/shard_map/ppermute | solution.py:1025
  145.0 10.4 %fusion.21.d_hidden_ref = f32[1024,1408]{1,0:T(8,128)} fusion(bf16[1024,2048]{1,0:T(8,128)(2,1)} %constant_dynamic-update-slice_fusion.5.refs_2_, bf16[1408,2048]{1,0:T(8,128)(2,1)S(1)} %bitcast.98), kind=kOutput, calls=%fused_computation.72 | convolution fusion | flops 5905580032 | bytes 15728640 | tf_op jit(solution)/shard_map/dot_general | solution.py:21
  157.3 8.3 %collective-permute-done.9 = bf16[2,64,2048]{2,1,0:T(8,128)(2,1)S(1)} collective-permute-done((bf16[2,64,2048]{2,1,0:T(8,128)(2,1)S(1)}, bf16[2,64,2048]{2,1,0:T(8,128)(2,1)S(1)}, u32[]{:S(2)}, u32[]{:S(2)}) %collective-permute-start.9) | collective-permute-done | bytes 524320 | tf_op jit(solution)/shard_map/ppermute | solution.py:1025
  167.6 4.6 constant_dynamic-slice_fusion.5
  172.3 3.4 convolution_convert_fusion.4.f_low_ref
  175.7 12.5 %fusion.22.pre_ref = f32[1024,2048]{1,0:T(8,128)S(1)} fusion(bf16[1024,2048]{1,0:T(8,128)(2,1)} %constant_dynamic-update-slice_fusion.h_hbm, bf16[2048,2048]{1,0:T(8,128)(2,1)} %all-gather.7.cloned.1.call-done), kind=kOutput, calls=%fused_computation.73 | convolution fusion | flops 8589934592 | bytes 20971520 | tf_op jit(solution)/shard_map/dot_general | solution.py:21
  188.3 10.7 %slots_forward.1.act_hbm = bf16[1024,512]{1,0:T(8,128)(2,1)S(1)} custom-call(f32[1024,2048]{1,0:T(8,128)S(1)} %fusion.22.pre_ref, bf16[1024,16]{1,0:T(8,128)(2,1)S(1)} %convolution_convert_fusion.4.f_low_ref, bf16[16,64]{1,0:T(8,128)(2,1)S(1)} %copy.58.wfu_ref, f32[1,512]{1,0:T(1,128)S(1)} %reshape.264.gain_ref, f32[8,128,1]{2,1,0:T(8,128)S(1)} %reshape.269.doc_col_ref, ...), custom_call_target="tpu_custom_call" | custom-call | tf_op jit(solution)/shard_map/slots_forward/pallas_call | solution.py:252
  201.4 72.0 %relay_forward.1 = (bf16[4,256,2048]{2,1,0:T(8,128)(2,1)S(1)}, f32[256,2048]{1,0:T(8,128)S(1)}) custom-call(bf16[4,256,2048]{2,1,0:T(8,128)(2,1)S(1)} %bitcast.95, bf16[256,2048]{1,0:T(8,128)(2,1)S(1)} %bitcast.94, f32[1,2048]{1,0:T(1,128)S(1)} %reshape.267.gain_ref), custom_call_target="tpu_custom_call" | custom-call | tf_op jit(solution)/shard_map/relay_forward/pallas_call | solution.py:814
  276.7 10.5 %feed_forward.2 = (bf16[1024,640]{1,0:T(8,128)(2,1)S(1)}, bf16[1024,1280]{1,0:T(8,128)(2,1)S(1)}) custom-call(bf16[1024,2048]{1,0:T(8,128)(2,1)} %bitcast.87, bf16[2048,1280]{1,0:T(8,128)(2,1)} %all-gather.9.cloned.1.call-done.gu_ref.refs_2_, f32[1024,1408]{1,0:T(8,128)} %fusion.21.d_hidden_ref), custom_call_target="tpu_custom_call" | custom-call | tf_op jit(solution)/shard_map/feed_forward/pallas_call | solution.py:918
  290.5 5.2 collective-permute-done.11
  295.7 4.2 add_convert_fusion.2
  300.0 12.4 %feed_forward.3 = (bf16[1024,768]{1,0:T(8,128)(2,1)S(1)}, bf16[1024,1536]{1,0:T(8,128)(2,1)S(1)}) custom-call(bf16[1024,2048]{1,0:T(8,128)(2,1)} %bitcast.88, bf16[2048,1536]{1,0:T(8,128)(2,1)} %all-gather.11.cloned.1.call-done.gu_ref.refs_3_, f32[1024,1408]{1,0:T(8,128)} %fusion.21.d_hidden_ref), custom_call_target="tpu_custom_call" | custom-call | tf_op jit(solution)/shard_map/feed_forward/pallas_call | solution.py:918
  313.6 4.9 convolution_convert_fusion.1
  318.6 15.8 %d_hm.1 = bf16[1024,2048]{1,0:T(8,128)(2,1)} custom-call(bf16[1024,1280]{1,0:T(8,128)(2,1)S(1)} %copy-done.12, bf16[1024,1536]{1,0:T(8,128)(2,1)S(1)} %get-tuple-element.120.refs_1_, bf16[2048,1280]{1,0:T(8,128)(2,1)} %all-gather.9.cloned.1.call-done.gu_ref.refs_2_, bf16[2048,1536]{1,0:T(8,128)(2,1)} %all-gather.11.cloned.1.call-done.gu_ref.refs_3_), custom_call_target="tpu_custom_call" | custom-call | tf_op jit(solution)/shard_map/d_hm/pallas_call | solution.py:943
  334.4 4.8 add_convert_fusion.1
  339.7 74.4 %relay_backward.1 = (bf16[4,256,2048]{2,1,0:T(8,128)(2,1)}, f32[256,2048]{1,0:T(8,128)}, f32[1,2048]{1,0:T(1,128)}, bf16[4,176,2048]{2,1,0:T(8,128)(2,1)}, bf16[...) custom-call(bf16[4,256,2048]{2,1,0:T(8,128)(2,1)} %bitcast.101, f32[256,2048]{1,0:T(8,128)} %copy-done.7, ...), custom_call_target="tpu_custom_call" | custom-call | tf_op jit(solution)/shard_map/relay_backward/pallas_call | solution.py:833
  416.3 5.2 convolution_convert_fusion.3.d_act_ref
  421.5 3.4 copy-done.1
  424.9 14.5 %slots_backward.2 = (bf16[1024,2048]{1,0:T(8,128)(2,1)S(1)}, bf16[1024,64]{1,0:T(8,128)(2,1)S(1)}, bf16[1024,16]{1,0:T(8,128)(2,1)S(1)}, f32[1,512]{1,0:T(1,128)S(1)}) custom-call(f32[1024,2048]{1,0:T(8,128)S(1)} %copy-done.1, bf16[1024,16]{1,0:T(8,128)(2,1)S(1)} %convolution_convert_fusion.4.f_low_ref, bf16[16,64]{1,0:T(8,128)(2,1)S(1)} %copy.58.wfu_ref, ...), custom_call_target="tpu_custom_call" | custom-call | tf_op jit(solution)/shard_map/slots_backward/pallas_call | solution.py:270
  439.4 3.2 convert_add_fusion.1
  445.1 8.9 %slots_backward.3 = (bf16[1024,2048]{1,0:T(8,128)(2,1)S(1)}, bf16[1024,64]{1,0:T(8,128)(2,1)S(1)}, bf16[1024,16]{1,0:T(8,128)(2,1)S(1)}, f32[1,512]{1,0:T(1,128)S(1)}) custom-call(f32[1024,2048]{1,0:T(8,128)S(1)} %copy-done.1, bf16[1024,16]{1,0:T(8,128)(2,1)S(1)} %convolution_convert_fusion.4.f_low_ref, ...), custom_call_target="tpu_custom_call", output_to_operand_aliasing={{0}: (7, {}), {1}: (8, {}), {2}: (9, {})} | custom-call | tf_op jit(solution)/shard_map/slots_backward/pallas_call | solution.py:270
  456.3 19.1 %heads_gradient.1 = (bf16[1024,2048]{1,0:T(8,128)(2,1)}, bf16[4,64,1280]{2,1,0:T(8,128)(2,1)}, bf16[4,64,1536]{2,1,0:T(8,128)(2,1)}) custom-call(bf16[1024,1024]{1,0:T(8,128)(2,1)} %get-tuple-element.107.own_hbm, bf16[1024,1024]{1,0:T(8,128)(2,1)} %get-tuple-element.108.other_hbm, bf16[1024,2048]{1,0:T(8,128)(2,1)} %copy-done.2, ...), custom_call_target="tpu_custom_call" | custom-call | tf_op jit(solution)/shard_map/heads_gradient/pallas_call | solution.py:1001
  476.7 13.2 %fusion.23 = f32[1024,2048]{1,0:T(8,128)S(1)} fusion(bf16[1024,2048]{1,0:T(8,128)(2,1)} %copy-done.2, bf16[2048,2048]{1,0:T(8,128)(2,1)} %all-gather.7.cloned.1.call-done), kind=kOutput, calls=%fused_computation.74 | convolution fusion | flops 8589934592 | bytes 20971520 | tf_op jit(solution)/shard_map/dot_general | solution.py:21
  490.0 3.2 add_convert_fusion
  493.2 53.2 %settle.1 = (bf16[256,2048]{1,0:T(8,128)(2,1)}, f32[32,24,128]{2,1,0:T(8,128)}, bf16[4,1,64,2048]{3,2,1,0:T(8,128)(2,1)}) custom-call(bf16[4,256,2048]{2,1,0:T(8,128)(2,1)} %bitcast.100, bf16[256,2048]{1,0:T(8,128)(2,1)} %bitcast.93, f32[256,2048]{1,0:T(8,128)} %get-tuple-element.156.d_resid_ref, f32[1,2048]{1,0:T(1,128)} %reshape.268.gain_ref, ...), custom_call_target="tpu_custom_call" | custom-call | tf_op jit(solution)/shard_map/settle/pallas_call | solution.py:873
  556.0 21.2 %finish.1 = (f32[24,128]{1,0:T(8,128)S(1)}, bf16[4,64,2048]{2,1,0:T(8,128)(2,1)S(1)}) custom-call(f32[32,24,128]{2,1,0:T(8,128)S(1)} %copy-done.22, bf16[4,64,2048]{2,1,0:T(8,128)(2,1)S(1)} %bitcast.96), custom_call_target="tpu_custom_call" | custom-call | tf_op jit(solution)/shard_map/finish/pallas_call | solution.py:517
  581.1 5.0 reduce-scatter.14.cloned.1.call-done
  (197 shorter events, 92.9 us)
Async XLA Ops:
  7.2 57.1 %copy-start.6 = (bf16[2,128,2048]{2,1,0:T(8,128)(2,1)S(1)}, bf16[2,128,2048]{2,1,0:T(8,128)(2,1)}, u32[]{:S(2)}) copy-start(bf16[2,128,2048]{2,1,0:T(8,128)(2,1)} %param.16) | copy-start | bytes 3145732
  7.2 129.1 %all-gather.5.cloned.1.call-start = ((), (), s32[]{:S(2)}) async-start(), calls=%async_computation.5 | async-start | bytes 8847360 | tf_op jit(solution)/shard_map/all_gather | solution.py:1124
  9.7 166.0 %all-gather.7.cloned.1.call-start = ((), (), s32[]{:S(2)}) async-start(), calls=%async_computation.6 | async-start | bytes 9437184 | tf_op jit(solution)/shard_map/all_gather | solution.py:1150
  29.3 247.3 %all-gather.9.cloned.1.call-start = ((), (), s32[]{:S(2)}) async-start(), calls=%async_computation.7 | async-start | bytes 5898240 | tf_op jit(solution)/shard_map/all_gather | solution.py:1150
  62.2 237.8 %all-gather.11.cloned.1.call-start = ((), (), s32[]{:S(2)}) async-start(), calls=%async_computation.8 | async-start | bytes 7077888 | tf_op jit(solution)/shard_map/all_gather | solution.py:1150
  62.2 26.5 %collective-permute-start.5 = (bf16[256,2048]{1,0:T(8,128)(2,1)}, bf16[256,2048]{1,0:T(8,128)(2,1)}, u32[]{:S(2)}, u32[]{:S(2)}) collective-permute-start(bf16[256,2048]{1,0:T(8,128)(2,1)} %bitcast.104), channel_id=1, source_target_pairs={{0,4},{2,6},{4,0},{6,2},{1,5},{3,7},{5,1},{7,3},{8,12},{10,14},{12... | collective-permute-start | bytes 3145736 | tf_op jit(solution)/shard_map/ppermute | solution.py:1025
  63.3 27.6 %collective-permute-start.4 = (bf16[256,2048]{1,0:T(8,128)(2,1)}, bf16[256,2048]{1,0:T(8,128)(2,1)}, u32[]{:S(2)}, u32[]{:S(2)}) collective-permute-start(bf16[256,2048]{1,0:T(8,128)(2,1)} %bitcast.105), channel_id=1, source_target_pairs={{0,2},{2,0},{4,6},{6,4},{1,3},{3,1},{5,7},{7,5},{8,10},{10,8},{12,... | collective-permute-start | bytes 3145736 | tf_op jit(solution)/shard_map/ppermute | solution.py:1025
  73.5 37.6 %collective-permute-start.1 = (bf16[256,2048]{1,0:T(8,128)(2,1)}, bf16[256,2048]{1,0:T(8,128)(2,1)}, u32[]{:S(2)}, u32[]{:S(2)}) collective-permute-start(bf16[256,2048]{1,0:T(8,128)(2,1)} %copy.46), channel_id=1, source_target_pairs={{0,4},{2,6},{4,0},{6,2},{1,5},{3,7},{5,1},{7,3},{8,12},{10,14},{12... | collective-permute-start | bytes 3145736 | tf_op jit(solution)/shard_map/ppermute | solution.py:1025
  74.6 38.8 %collective-permute-start = (bf16[256,2048]{1,0:T(8,128)(2,1)}, bf16[256,2048]{1,0:T(8,128)(2,1)}, u32[]{:S(2)}, u32[]{:S(2)}) collective-permute-start(bf16[256,2048]{1,0:T(8,128)(2,1)} %copy.46), channel_id=1, source_target_pairs={{0,2},{2,0},{4,6},{6,4},{1,3},{3,1},{5,7},{7,5},{8,10},{10,8},{12,... | collective-permute-start | bytes 3145736 | tf_op jit(solution)/shard_map/ppermute | solution.py:1025
  75.6 340.7 %reduce-scatter.6.cloned.1.call-start = ((), (), s32[]{:S(2)}) async-start(), calls=%async_computation.9 | async-start | bytes 3276800 | tf_op jit(solution)/shard_map/reduce_scatter | solution.py:1109
  76.8 124.5 %copy-start.23 = (f32[1,2048]{1,0:T(1,128)}, f32[1,2048]{1,0:T(1,128)S(1)}, u32[]{:S(2)}) copy-start(f32[1,2048]{1,0:T(1,128)S(1)} %reshape.267.gain_ref) | copy-start | bytes 24580
  89.8 44.9 %collective-permute-start.6 = (bf16[128,2048]{1,0:T(8,128)(2,1)S(1)}, bf16[128,2048]{1,0:T(8,128)(2,1)S(1)}, u32[]{:S(2)}, u32[]{:S(2)}) collective-permute-start(bf16[128,2048]{1,0:T(8,128)(2,1)S(1)} %slice.103), channel_id=1, source_target_pairs={{0,2},{2,0},{4,6},{6,4},{1,3},{3,1},{5,7},{7,5},{8,10},{10,8},{12,... | collective-permute-start | bytes 1572872 | tf_op jit(solution)/shard_map/ppermute | solution.py:1025
  92.0 43.5 %collective-permute-start.7 = (bf16[128,2048]{1,0:T(8,128)(2,1)S(1)}, bf16[128,2048]{1,0:T(8,128)(2,1)S(1)}, u32[]{:S(2)}, u32[]{:S(2)}) collective-permute-start(bf16[128,2048]{1,0:T(8,128)(2,1)S(1)} %slice.104), channel_id=1, source_target_pairs={{0,4},{2,6},{4,0},{6,2},{1,5},{3,7},{5,1},{7,3},{8,12},{10,14},{12... | collective-permute-start | bytes 1572872 | tf_op jit(solution)/shard_map/ppermute | solution.py:1025
  112.2 20.7 %collective-permute-start.2 = (bf16[128,2048]{1,0:T(8,128)(2,1)S(1)}, bf16[128,2048]{1,0:T(8,128)(2,1)S(1)}, u32[]{:S(2)}, u32[]{:S(2)}) collective-permute-start(bf16[128,2048]{1,0:T(8,128)(2,1)S(1)} %slice.101), channel_id=1, source_target_pairs={{0,2},{2,0},{4,6},{6,4},{1,3},{3,1},{5,7},{7,5},{8,10},{10,8},{12,... | collective-permute-start | bytes 1572872 | tf_op jit(solution)/shard_map/ppermute | solution.py:1025
  114.5 19.3 %collective-permute-start.3 = (bf16[128,2048]{1,0:T(8,128)(2,1)S(1)}, bf16[128,2048]{1,0:T(8,128)(2,1)S(1)}, u32[]{:S(2)}, u32[]{:S(2)}) collective-permute-start(bf16[128,2048]{1,0:T(8,128)(2,1)S(1)} %slice.102), channel_id=1, source_target_pairs={{0,4},{2,6},{4,0},{6,2},{1,5},{3,7},{5,1},{7,3},{8,12},{10,14},{12... | collective-permute-start | bytes 1572872 | tf_op jit(solution)/shard_map/ppermute | solution.py:1025
  141.5 15.8 %collective-permute-start.10 = (bf16[2,64,2048]{2,1,0:T(8,128)(2,1)S(1)}, bf16[2,64,2048]{2,1,0:T(8,128)(2,1)S(1)}, u32[]{:S(2)}, u32[]{:S(2)}) collective-permute-start(bf16[2,64,2048]{2,1,0:T(8,128)(2,1)S(1)} %get-tuple-element.232), channel_id=1, source_target_pairs={{0,6},{2,4},{4,2},{6,0},{1,7},{3,5},{5,3},{7,1},{8,14},{10,12},{12... | collective-permute-start | bytes 1572872 | tf_op jit(solution)/shard_map/ppermute | solution.py:1025
  142.7 22.9 %collective-permute-start.9 = (bf16[2,64,2048]{2,1,0:T(8,128)(2,1)S(1)}, bf16[2,64,2048]{2,1,0:T(8,128)(2,1)S(1)}, u32[]{:S(2)}, u32[]{:S(2)}) collective-permute-start(bf16[2,64,2048]{2,1,0:T(8,128)(2,1)S(1)} %get-tuple-element.233), channel_id=1, source_target_pairs={{0,4},{2,6},{4,0},{6,2},{1,5},{3,7},{5,1},{7,3},{8,12},{10,14},{12... | collective-permute-start | bytes 1572872 | tf_op jit(solution)/shard_map/ppermute | solution.py:1025
  143.8 21.8 %collective-permute-start.8 = (bf16[2,64,2048]{2,1,0:T(8,128)(2,1)S(1)}, bf16[2,64,2048]{2,1,0:T(8,128)(2,1)S(1)}, u32[]{:S(2)}, u32[]{:S(2)}) collective-permute-start(bf16[2,64,2048]{2,1,0:T(8,128)(2,1)S(1)} %get-tuple-element.234), channel_id=1, source_target_pairs={{0,2},{2,0},{4,6},{6,4},{1,3},{3,1},{5,7},{7,5},{8,10},{10,8},{12,... | collective-permute-start | bytes 1572872 | tf_op jit(solution)/shard_map/ppermute | solution.py:1025
  175.7 269.4 %copy-start.9 = (bf16[1024,16]{1,0:T(8,128)(2,1)}, bf16[1024,16]{1,0:T(8,128)(2,1)S(1)}, u32[]{:S(2)}) copy-start(bf16[1024,16]{1,0:T(8,128)(2,1)S(1)} %convolution_convert_fusion.4.f_low_ref) | copy-start | bytes 98308
  290.4 5.3 collective-permute-start.11
  299.9 116.4 %reduce-scatter.8.cloned.1.call-start = ((), (), s32[]{:S(2)}) async-start(), calls=%async_computation.10 | async-start | bytes 3932160 | tf_op jit(solution)/shard_map/reduce_scatter | solution.py:1109
  318.5 15.9 %collective-permute-start.12 = (bf16[1024,1536]{1,0:T(8,128)(2,1)}, bf16[1024,1536]{1,0:T(8,128)(2,1)S(1)}, u32[]{:S(2)}, u32[]{:S(2)}) collective-permute-start(bf16[1024,1536]{1,0:T(8,128)(2,1)} %convolution_convert_fusion.1), channel_id=1, source_target_pairs={{0,1},{1,0},{2,3},{3,2},{4,5},{5,4},{6,7},{7,6},{8,9},{9,8},{10,11... | collective-permute-start | bytes 9437192 | tf_op jit(solution)/shard_map/ppermute | solution.py:1029
  339.2 137.5 %reduce-scatter.12.cloned.1.call-start = ((), (), s32[]{:S(2)}) async-start(), calls=%async_computation.12 | async-start | bytes 3604480 | tf_op jit(solution)/shard_map/reduce_scatter | solution.py:1109
  414.1 139.7 %reduce-scatter.10.cloned.1.call-start = ((), (), s32[]{:S(2)}) async-start(), calls=%async_computation.11 | async-start | bytes 5242880 | tf_op jit(solution)/shard_map/reduce_scatter | solution.py:1109
  414.2 25.2 %collective-permute-start.13 = (bf16[256,2048]{1,0:T(8,128)(2,1)}, bf16[256,2048]{1,0:T(8,128)(2,1)S(1)}, u32[]{:S(2)}, u32[]{:S(2)}) collective-permute-start(bf16[256,2048]{1,0:T(8,128)(2,1)} %get-tuple-element.132), channel_id=1, source_target_pairs={{0,2},{2,0},{4,6},{6,4},{1,3},{3,1},{5,7},{7,5},{8,10},{10,8},{12,... | collective-permute-start | bytes 3145736 | tf_op jit(solution)/shard_map/ppermute | solution.py:1025
  414.7 24.8 %collective-permute-start.14 = (bf16[256,2048]{1,0:T(8,128)(2,1)}, bf16[256,2048]{1,0:T(8,128)(2,1)}, u32[]{:S(2)}, u32[]{:S(2)}) collective-permute-start(bf16[256,2048]{1,0:T(8,128)(2,1)} %get-tuple-element.133), channel_id=1, source_target_pairs={{0,4},{2,6},{4,0},{6,2},{1,5},{3,7},{5,1},{7,3},{8,12},{10,14},{12... | collective-permute-start | bytes 3145736 | tf_op jit(solution)/shard_map/ppermute | solution.py:1025
  442.7 13.3 %collective-permute-start.15 = (bf16[128,2048]{1,0:T(8,128)(2,1)S(1)}, bf16[128,2048]{1,0:T(8,128)(2,1)S(1)}, u32[]{:S(2)}, u32[]{:S(2)}) collective-permute-start(bf16[128,2048]{1,0:T(8,128)(2,1)S(1)} %get-tuple-element.144), channel_id=1, source_target_pairs={{0,4},{2,6},{4,0},{6,2},{1,5},{3,7},{5,1},{7,3},{8,12},{10,14},{12... | collective-permute-start | bytes 1572872 | tf_op jit(solution)/shard_map/ppermute | solution.py:1025
  444.3 12.0 %collective-permute-start.16 = (bf16[128,2048]{1,0:T(8,128)(2,1)S(1)}, bf16[128,2048]{1,0:T(8,128)(2,1)S(1)}, u32[]{:S(2)}, u32[]{:S(2)}) collective-permute-start(bf16[128,2048]{1,0:T(8,128)(2,1)S(1)} %get-tuple-element.145), channel_id=1, source_target_pairs={{0,2},{2,0},{4,6},{6,4},{1,3},{3,1},{5,7},{7,5},{8,10},{10,8},{12,... | collective-permute-start | bytes 1572872 | tf_op jit(solution)/shard_map/ppermute | solution.py:1025
  475.4 110.6 %reduce-scatter.14.cloned.1.call-start = ((), (), s32[]{:S(2)}) async-start(), calls=%async_computation.13 | async-start | bytes 1310720 | tf_op jit(solution)/shard_map/reduce_scatter | solution.py:1109
  493.2 55.8 %copy-start.18 = (bf16[4,64,1536]{2,1,0:T(8,128)(2,1)S(1)}, bf16[4,64,1536]{2,1,0:T(8,128)(2,1)}, u32[]{:S(2)}) copy-start(bf16[4,64,1536]{2,1,0:T(8,128)(2,1)} %get-tuple-element.166.refs_1_) | copy-start | bytes 2359300
  493.2 55.8 %copy-start.21 = (bf16[4,64,1280]{2,1,0:T(8,128)(2,1)S(1)}, bf16[4,64,1280]{2,1,0:T(8,128)(2,1)}, u32[]{:S(2)}) copy-start(bf16[4,64,1280]{2,1,0:T(8,128)(2,1)} %get-tuple-element.165.refs_0_) | copy-start | bytes 1966084
  551.1 36.8 %copy-start.30 = (bf16[256,2048]{1,0:T(8,128)(2,1)S(1)}, bf16[256,2048]{1,0:T(8,128)(2,1)}, u32[]{:S(2)}) copy-start(bf16[256,2048]{1,0:T(8,128)(2,1)} %get-tuple-element.171) | copy-start | bytes 3145732
  (30 other events, 351.2 us)
Sparse Core Ops, SparseCore 0:
  10.3 83.1 all-gather.4
  95.1 80.5 all-gather.6
  177.3 54.5 all-gather.8
  233.3 63.5 all-gather.10
  300.0 50.4 reduce-scatter.5
  352.7 59.9 reduce-scatter.7
  414.9 56.1 reduce-scatter.11
  475.5 75.1 reduce-scatter.9
  553.2 32.8 reduce-scatter.13

commit v4 on v3

--- a/solution.py
+++ b/solution.py
@@ -916,7 +916,7 @@
     columns = gu.shape[1]
     wide = pl.BlockSpec((tokens, 2 * LANES), lambda j: (0, j))
     return pl.pallas_call(
-        functools.partial(ff_kernel, 256),
+        functools.partial(ff_kernel, 1024),
         out_shape=(jax.ShapeDtypeStruct((tokens, columns // 2), BF16), jax.ShapeDtypeStruct((tokens, columns), BF16)),
         grid=(columns // (2 * LANES),),
         in_specs=[
@@ -941,7 +941,7 @@
     tokens, D = grads[0].shape[0], weights[0].shape[0]
     width = 256
     return pl.pallas_call(
-        functools.partial(d_hm_kernel, 256, len(grads)),
+        functools.partial(d_hm_kernel, 1024, len(grads)),
         out_shape=jax.ShapeDtypeStruct((tokens, D), BF16),
         grid=(D // width,),
         in_specs=[pl.BlockSpec(g.shape, lambda j: (0, 0)) for g in grads]

time: 602 us -> 601 us (level)
  no operation moved by 1% of the time
where the time goes in v4:
time: 601 us; the launch traced here: 594 us
  Pallas kernels  364 us (61%)
  matrix products  67.2 us (11%)
  local copies, waits for them, and re-layouts  58.9 us (10%)
  waiting for transfers between devices  54.3 us (9%)
  starting transfers between devices  17.4 us (3%)
  other arithmetic  16.8 us (3%)
  between operations  14.9 us (2%)
    pallas_call x1, Pallas kernels, relay_backward(): pl.pallas_call(functools.partial(backward_relay_kernel, unit, SUBS, len(h...  74.4 us
    pallas_call x1, Pallas kernels, relay_forward(): pl.pallas_call(functools.partial(forward_relay_kernel, unit, SUBS), out_s...  72 us
    dot_general x11, matrix products, mm(): return lax.dot_general(a, b, (dims, ((), ())), preferred_element_type=F32)  67.2 us
    pallas_call x1, Pallas kernels, settle(): pl.pallas_call(functools.partial(settle_kernel, unit, SUBS), out_shape=(j...  53.6 us
    ppermute x15, waiting for transfers between devices, send_t(): return lax.ppermute(x, 't', [(i, i ^ step) for i in range(TP)])  44.3 us
    unnamed x87, local copies, waits for them, and re-layouts  30.1 us
    pallas_call x2, Pallas kernels, slots_backward(): pl.pallas_call(backward_kernel, out_shape=(jax.ShapeDtypeStruct((count *...  23.4 us
    pallas_call x1, Pallas kernels, spread_ff(): pl.pallas_call(functools.partial(spread_ff_kernel, piece, parts), out_sha...  22.3 us
  transfers between devices with their start and end apart: 26, of which 8 were waited for; matrix products, arithmetic and copies ran while one was open for 21% of the time, Pallas kernels for 61%

profile of v4, /device:TPU:0, one launch (start us, length us, event | category | flops | bytes accessed | tf_op | source)
XLA Modules:
  0.0 594.0 jit_solution(10068045412811060659)
XLA Ops:
  12.4 16.7 %spread.1 = bf16[4,64,2048]{2,1,0:T(8,128)(2,1)} custom-call(bf16[64,2048]{1,0:T(8,128)(2,1)} %refs_0_.1, bf16[64,2048]{1,0:T(8,128)(2,1)} %refs_1_.1, bf16[64,2048]{1,0:T(8,128)(2,1)} %refs_2_.1, bf16[64,2048]{1,0:T(8,128)(2,1)} %refs_3_.1), custom_call_target="tpu_custom_call" | custom-call | tf_op jit(solution)/shard_map/spread/pallas_call | solution.py:371
  29.4 10.4 %share_small.1 = bf16[32,16,128]{2,1,0:T(8,128)(2,1)S(1)} custom-call(bf16[16,128]{1,0:T(8,128)(2,1)S(1)} %pad_bitcast_fusion.x_ref), custom_call_target="tpu_custom_call" | custom-call | tf_op jit(solution)/shard_map/share_small/pallas_call | solution.py:330
  39.9 22.3 %spread_ff.1 = (bf16[4,64,1280]{2,1,0:T(8,128)(2,1)}, bf16[4,64,1536]{2,1,0:T(8,128)(2,1)}) custom-call(bf16[64,5632]{1,0:T(8,128)(2,1)S(1)} %copy-done.19, bf16[64,5632]{1,0:T(8,128)(2,1)S(1)} %copy-done.20), custom_call_target="tpu_custom_call" | custom-call | tf_op jit(solution)/shard_map/spread_ff/pallas_call | solution.py:433
  81.1 7.6 %collective-permute-done.5 = bf16[256,2048]{1,0:T(8,128)(2,1)} collective-permute-done((bf16[256,2048]{1,0:T(8,128)(2,1)}, bf16[256,2048]{1,0:T(8,128)(2,1)}, u32[]{:S(2)}, u32[]{:S(2)}) %collective-permute-start.5) | collective-permute-done | bytes 1048608 | tf_op jit(solution)/shard_map/ppermute | solution.py:1025
  93.0 18.2 %collective-permute-done.1 = bf16[256,2048]{1,0:T(8,128)(2,1)} collective-permute-done((bf16[256,2048]{1,0:T(8,128)(2,1)}, bf16[256,2048]{1,0:T(8,128)(2,1)}, u32[]{:S(2)}, u32[]{:S(2)}) %collective-permute-start.1) | collective-permute-done | bytes 1048608 | tf_op jit(solution)/shard_map/ppermute | solution.py:1025
  124.8 8.2 %collective-permute-done.2 = bf16[128,2048]{1,0:T(8,128)(2,1)S(1)} collective-permute-done((bf16[128,2048]{1,0:T(8,128)(2,1)S(1)}, bf16[128,2048]{1,0:T(8,128)(2,1)S(1)}, u32[]{:S(2)}, u32[]{:S(2)}) %collective-permute-start.2) | collective-permute-done | bytes 524320 | tf_op jit(solution)/shard_map/ppermute | solution.py:1025
  145.0 10.4 %fusion.21.d_hidden_ref = f32[1024,1408]{1,0:T(8,128)} fusion(bf16[1024,2048]{1,0:T(8,128)(2,1)} %constant_dynamic-update-slice_fusion.5.refs_2_, bf16[1408,2048]{1,0:T(8,128)(2,1)S(1)} %bitcast.98), kind=kOutput, calls=%fused_computation.72 | convolution fusion | flops 5905580032 | bytes 15728640 | tf_op jit(solution)/shard_map/dot_general | solution.py:21
  157.3 8.3 %collective-permute-done.9 = bf16[2,64,2048]{2,1,0:T(8,128)(2,1)S(1)} collective-permute-done((bf16[2,64,2048]{2,1,0:T(8,128)(2,1)S(1)}, bf16[2,64,2048]{2,1,0:T(8,128)(2,1)S(1)}, u32[]{:S(2)}, u32[]{:S(2)}) %collective-permute-start.9) | collective-permute-done | bytes 524320 | tf_op jit(solution)/shard_map/ppermute | solution.py:1025
  167.6 4.6 constant_dynamic-slice_fusion.5
  172.3 3.4 convolution_convert_fusion.4.f_low_ref
  175.7 12.5 %fusion.22.pre_ref = f32[1024,2048]{1,0:T(8,128)S(1)} fusion(bf16[1024,2048]{1,0:T(8,128)(2,1)} %constant_dynamic-update-slice_fusion.h_hbm, bf16[2048,2048]{1,0:T(8,128)(2,1)} %all-gather.7.cloned.1.call-done), kind=kOutput, calls=%fused_computation.73 | convolution fusion | flops 8589934592 | bytes 20971520 | tf_op jit(solution)/shard_map/dot_general | solution.py:21
  188.3 10.7 %slots_forward.1.act_hbm = bf16[1024,512]{1,0:T(8,128)(2,1)S(1)} custom-call(f32[1024,2048]{1,0:T(8,128)S(1)} %fusion.22.pre_ref, bf16[1024,16]{1,0:T(8,128)(2,1)S(1)} %convolution_convert_fusion.4.f_low_ref, bf16[16,64]{1,0:T(8,128)(2,1)S(1)} %copy.58.wfu_ref, f32[1,512]{1,0:T(1,128)S(1)} %reshape.264.gain_ref, f32[8,128,1]{2,1,0:T(8,128)S(1)} %reshape.269.doc_col_ref, ...), custom_call_target="tpu_custom_call" | custom-call | tf_op jit(solution)/shard_map/slots_forward/pallas_call | solution.py:252
  201.4 72.0 %relay_forward.1 = (bf16[4,256,2048]{2,1,0:T(8,128)(2,1)S(1)}, f32[256,2048]{1,0:T(8,128)S(1)}) custom-call(bf16[4,256,2048]{2,1,0:T(8,128)(2,1)S(1)} %bitcast.95, bf16[256,2048]{1,0:T(8,128)(2,1)S(1)} %bitcast.94, f32[1,2048]{1,0:T(1,128)S(1)} %reshape.267.gain_ref), custom_call_target="tpu_custom_call" | custom-call | tf_op jit(solution)/shard_map/relay_forward/pallas_call | solution.py:814
  276.7 9.8 %feed_forward.2 = (bf16[1024,640]{1,0:T(8,128)(2,1)S(1)}, bf16[1024,1280]{1,0:T(8,128)(2,1)S(1)}) custom-call(bf16[1024,2048]{1,0:T(8,128)(2,1)} %bitcast.87, bf16[2048,1280]{1,0:T(8,128)(2,1)} %all-gather.9.cloned.1.call-done.gu_ref.refs_2_, f32[1024,1408]{1,0:T(8,128)} %fusion.21.d_hidden_ref), custom_call_target="tpu_custom_call" | custom-call | tf_op jit(solution)/shard_map/feed_forward/pallas_call | solution.py:918
  289.8 4.9 collective-permute-done.11
  294.7 4.2 add_convert_fusion.2
  299.1 11.7 %feed_forward.3 = (bf16[1024,768]{1,0:T(8,128)(2,1)S(1)}, bf16[1024,1536]{1,0:T(8,128)(2,1)S(1)}) custom-call(bf16[1024,2048]{1,0:T(8,128)(2,1)} %bitcast.88, bf16[2048,1536]{1,0:T(8,128)(2,1)} %all-gather.11.cloned.1.call-done.gu_ref.refs_3_, f32[1024,1408]{1,0:T(8,128)} %fusion.21.d_hidden_ref), custom_call_target="tpu_custom_call" | custom-call | tf_op jit(solution)/shard_map/feed_forward/pallas_call | solution.py:918
  312.0 4.9 convolution_convert_fusion.1
  317.1 15.8 %d_hm.1 = bf16[1024,2048]{1,0:T(8,128)(2,1)} custom-call(bf16[1024,1280]{1,0:T(8,128)(2,1)S(1)} %copy-done.12, bf16[1024,1536]{1,0:T(8,128)(2,1)S(1)} %get-tuple-element.120.refs_1_, bf16[2048,1280]{1,0:T(8,128)(2,1)} %all-gather.9.cloned.1.call-done.gu_ref.refs_2_, bf16[2048,1536]{1,0:T(8,128)(2,1)} %all-gather.11.cloned.1.call-done.gu_ref.refs_3_), custom_call_target="tpu_custom_call" | custom-call | tf_op jit(solution)/shard_map/d_hm/pallas_call | solution.py:943
  332.9 4.8 add_convert_fusion.1
  338.2 74.4 %relay_backward.1 = (bf16[4,256,2048]{2,1,0:T(8,128)(2,1)}, f32[256,2048]{1,0:T(8,128)}, f32[1,2048]{1,0:T(1,128)}, bf16[4,176,2048]{2,1,0:T(8,128)(2,1)}, bf16[...) custom-call(bf16[4,256,2048]{2,1,0:T(8,128)(2,1)} %bitcast.101, f32[256,2048]{1,0:T(8,128)} %copy-done.7, ...), custom_call_target="tpu_custom_call" | custom-call | tf_op jit(solution)/shard_map/relay_backward/pallas_call | solution.py:833
  414.7 5.2 convolution_convert_fusion.3.d_act_ref
  420.0 3.6 copy-done.1
  423.6 14.5 %slots_backward.2 = (bf16[1024,2048]{1,0:T(8,128)(2,1)S(1)}, bf16[1024,64]{1,0:T(8,128)(2,1)S(1)}, bf16[1024,16]{1,0:T(8,128)(2,1)S(1)}, f32[1,512]{1,0:T(1,128)S(1)}) custom-call(f32[1024,2048]{1,0:T(8,128)S(1)} %copy-done.1, bf16[1024,16]{1,0:T(8,128)(2,1)S(1)} %convolution_convert_fusion.4.f_low_ref, bf16[16,64]{1,0:T(8,128)(2,1)S(1)} %copy.58.wfu_ref, ...), custom_call_target="tpu_custom_call" | custom-call | tf_op jit(solution)/shard_map/slots_backward/pallas_call | solution.py:270
  438.1 3.2 convert_add_fusion.1
  443.7 8.9 %slots_backward.3 = (bf16[1024,2048]{1,0:T(8,128)(2,1)S(1)}, bf16[1024,64]{1,0:T(8,128)(2,1)S(1)}, bf16[1024,16]{1,0:T(8,128)(2,1)S(1)}, f32[1,512]{1,0:T(1,128)S(1)}) custom-call(f32[1024,2048]{1,0:T(8,128)S(1)} %copy-done.1, bf16[1024,16]{1,0:T(8,128)(2,1)S(1)} %convolution_convert_fusion.4.f_low_ref, ...), custom_call_target="tpu_custom_call", output_to_operand_aliasing={{0}: (7, {}), {1}: (8, {}), {2}: (9, {})} | custom-call | tf_op jit(solution)/shard_map/slots_backward/pallas_call | solution.py:270
  454.7 19.0 %heads_gradient.1 = (bf16[1024,2048]{1,0:T(8,128)(2,1)}, bf16[4,64,1280]{2,1,0:T(8,128)(2,1)}, bf16[4,64,1536]{2,1,0:T(8,128)(2,1)}) custom-call(bf16[1024,1024]{1,0:T(8,128)(2,1)} %get-tuple-element.107.own_hbm, bf16[1024,1024]{1,0:T(8,128)(2,1)} %get-tuple-element.108.other_hbm, bf16[1024,2048]{1,0:T(8,128)(2,1)} %copy-done.2, ...), custom_call_target="tpu_custom_call" | custom-call | tf_op jit(solution)/shard_map/heads_gradient/pallas_call | solution.py:1001
  475.1 12.9 %fusion.23 = f32[1024,2048]{1,0:T(8,128)S(1)} fusion(bf16[1024,2048]{1,0:T(8,128)(2,1)} %copy-done.2, bf16[2048,2048]{1,0:T(8,128)(2,1)} %all-gather.7.cloned.1.call-done), kind=kOutput, calls=%fused_computation.74 | convolution fusion | flops 8589934592 | bytes 20971520 | tf_op jit(solution)/shard_map/dot_general | solution.py:21
  488.1 3.2 add_convert_fusion
  491.3 53.6 %settle.1 = (bf16[256,2048]{1,0:T(8,128)(2,1)}, f32[32,24,128]{2,1,0:T(8,128)}, bf16[4,1,64,2048]{3,2,1,0:T(8,128)(2,1)}) custom-call(bf16[4,256,2048]{2,1,0:T(8,128)(2,1)} %bitcast.100, bf16[256,2048]{1,0:T(8,128)(2,1)} %bitcast.93, f32[256,2048]{1,0:T(8,128)} %get-tuple-element.156.d_resid_ref, f32[1,2048]{1,0:T(1,128)} %reshape.268.gain_ref, ...), custom_call_target="tpu_custom_call" | custom-call | tf_op jit(solution)/shard_map/settle/pallas_call | solution.py:873
  554.5 21.2 %finish.1 = (f32[24,128]{1,0:T(8,128)S(1)}, bf16[4,64,2048]{2,1,0:T(8,128)(2,1)S(1)}) custom-call(f32[32,24,128]{2,1,0:T(8,128)S(1)} %copy-done.22, bf16[4,64,2048]{2,1,0:T(8,128)(2,1)S(1)} %bitcast.96), custom_call_target="tpu_custom_call" | custom-call | tf_op jit(solution)/shard_map/finish/pallas_call | solution.py:517
  579.5 5.0 reduce-scatter.14.cloned.1.call-done
  (197 shorter events, 92.8 us)
Async XLA Ops:
  7.2 57.1 %copy-start.6 = (bf16[2,128,2048]{2,1,0:T(8,128)(2,1)S(1)}, bf16[2,128,2048]{2,1,0:T(8,128)(2,1)}, u32[]{:S(2)}) copy-start(bf16[2,128,2048]{2,1,0:T(8,128)(2,1)} %param.16) | copy-start | bytes 3145732
  7.2 129.1 %all-gather.5.cloned.1.call-start = ((), (), s32[]{:S(2)}) async-start(), calls=%async_computation.5 | async-start | bytes 8847360 | tf_op jit(solution)/shard_map/all_gather | solution.py:1124
  9.7 166.0 %all-gather.7.cloned.1.call-start = ((), (), s32[]{:S(2)}) async-start(), calls=%async_computation.6 | async-start | bytes 9437184 | tf_op jit(solution)/shard_map/all_gather | solution.py:1150
  29.3 247.3 %all-gather.9.cloned.1.call-start = ((), (), s32[]{:S(2)}) async-start(), calls=%async_computation.7 | async-start | bytes 5898240 | tf_op jit(solution)/shard_map/all_gather | solution.py:1150
  62.2 236.9 %all-gather.11.cloned.1.call-start = ((), (), s32[]{:S(2)}) async-start(), calls=%async_computation.8 | async-start | bytes 7077888 | tf_op jit(solution)/shard_map/all_gather | solution.py:1150
  62.2 26.5 %collective-permute-start.5 = (bf16[256,2048]{1,0:T(8,128)(2,1)}, bf16[256,2048]{1,0:T(8,128)(2,1)}, u32[]{:S(2)}, u32[]{:S(2)}) collective-permute-start(bf16[256,2048]{1,0:T(8,128)(2,1)} %bitcast.104), channel_id=1, source_target_pairs={{0,4},{2,6},{4,0},{6,2},{1,5},{3,7},{5,1},{7,3},{8,12},{10,14},{12... | collective-permute-start | bytes 3145736 | tf_op jit(solution)/shard_map/ppermute | solution.py:1025
  63.3 27.6 %collective-permute-start.4 = (bf16[256,2048]{1,0:T(8,128)(2,1)}, bf16[256,2048]{1,0:T(8,128)(2,1)}, u32[]{:S(2)}, u32[]{:S(2)}) collective-permute-start(bf16[256,2048]{1,0:T(8,128)(2,1)} %bitcast.105), channel_id=1, source_target_pairs={{0,2},{2,0},{4,6},{6,4},{1,3},{3,1},{5,7},{7,5},{8,10},{10,8},{12,... | collective-permute-start | bytes 3145736 | tf_op jit(solution)/shard_map/ppermute | solution.py:1025
  73.5 37.6 %collective-permute-start.1 = (bf16[256,2048]{1,0:T(8,128)(2,1)}, bf16[256,2048]{1,0:T(8,128)(2,1)}, u32[]{:S(2)}, u32[]{:S(2)}) collective-permute-start(bf16[256,2048]{1,0:T(8,128)(2,1)} %copy.46), channel_id=1, source_target_pairs={{0,4},{2,6},{4,0},{6,2},{1,5},{3,7},{5,1},{7,3},{8,12},{10,14},{12... | collective-permute-start | bytes 3145736 | tf_op jit(solution)/shard_map/ppermute | solution.py:1025
  74.6 38.8 %collective-permute-start = (bf16[256,2048]{1,0:T(8,128)(2,1)}, bf16[256,2048]{1,0:T(8,128)(2,1)}, u32[]{:S(2)}, u32[]{:S(2)}) collective-permute-start(bf16[256,2048]{1,0:T(8,128)(2,1)} %copy.46), channel_id=1, source_target_pairs={{0,2},{2,0},{4,6},{6,4},{1,3},{3,1},{5,7},{7,5},{8,10},{10,8},{12,... | collective-permute-start | bytes 3145736 | tf_op jit(solution)/shard_map/ppermute | solution.py:1025
  75.6 339.1 %reduce-scatter.6.cloned.1.call-start = ((), (), s32[]{:S(2)}) async-start(), calls=%async_computation.9 | async-start | bytes 3276800 | tf_op jit(solution)/shard_map/reduce_scatter | solution.py:1109
  76.8 124.5 %copy-start.23 = (f32[1,2048]{1,0:T(1,128)}, f32[1,2048]{1,0:T(1,128)S(1)}, u32[]{:S(2)}) copy-start(f32[1,2048]{1,0:T(1,128)S(1)} %reshape.267.gain_ref) | copy-start | bytes 24580
  89.8 44.9 %collective-permute-start.6 = (bf16[128,2048]{1,0:T(8,128)(2,1)S(1)}, bf16[128,2048]{1,0:T(8,128)(2,1)S(1)}, u32[]{:S(2)}, u32[]{:S(2)}) collective-permute-start(bf16[128,2048]{1,0:T(8,128)(2,1)S(1)} %slice.103), channel_id=1, source_target_pairs={{0,2},{2,0},{4,6},{6,4},{1,3},{3,1},{5,7},{7,5},{8,10},{10,8},{12,... | collective-permute-start | bytes 1572872 | tf_op jit(solution)/shard_map/ppermute | solution.py:1025
  92.0 43.5 %collective-permute-start.7 = (bf16[128,2048]{1,0:T(8,128)(2,1)S(1)}, bf16[128,2048]{1,0:T(8,128)(2,1)S(1)}, u32[]{:S(2)}, u32[]{:S(2)}) collective-permute-start(bf16[128,2048]{1,0:T(8,128)(2,1)S(1)} %slice.104), channel_id=1, source_target_pairs={{0,4},{2,6},{4,0},{6,2},{1,5},{3,7},{5,1},{7,3},{8,12},{10,14},{12... | collective-permute-start | bytes 1572872 | tf_op jit(solution)/shard_map/ppermute | solution.py:1025
  112.2 20.7 %collective-permute-start.2 = (bf16[128,2048]{1,0:T(8,128)(2,1)S(1)}, bf16[128,2048]{1,0:T(8,128)(2,1)S(1)}, u32[]{:S(2)}, u32[]{:S(2)}) collective-permute-start(bf16[128,2048]{1,0:T(8,128)(2,1)S(1)} %slice.101), channel_id=1, source_target_pairs={{0,2},{2,0},{4,6},{6,4},{1,3},{3,1},{5,7},{7,5},{8,10},{10,8},{12,... | collective-permute-start | bytes 1572872 | tf_op jit(solution)/shard_map/ppermute | solution.py:1025
  114.5 19.3 %collective-permute-start.3 = (bf16[128,2048]{1,0:T(8,128)(2,1)S(1)}, bf16[128,2048]{1,0:T(8,128)(2,1)S(1)}, u32[]{:S(2)}, u32[]{:S(2)}) collective-permute-start(bf16[128,2048]{1,0:T(8,128)(2,1)S(1)} %slice.102), channel_id=1, source_target_pairs={{0,4},{2,6},{4,0},{6,2},{1,5},{3,7},{5,1},{7,3},{8,12},{10,14},{12... | collective-permute-start | bytes 1572872 | tf_op jit(solution)/shard_map/ppermute | solution.py:1025
  141.5 15.8 %collective-permute-start.10 = (bf16[2,64,2048]{2,1,0:T(8,128)(2,1)S(1)}, bf16[2,64,2048]{2,1,0:T(8,128)(2,1)S(1)}, u32[]{:S(2)}, u32[]{:S(2)}) collective-permute-start(bf16[2,64,2048]{2,1,0:T(8,128)(2,1)S(1)} %get-tuple-element.232), channel_id=1, source_target_pairs={{0,6},{2,4},{4,2},{6,0},{1,7},{3,5},{5,3},{7,1},{8,14},{10,12},{12... | collective-permute-start | bytes 1572872 | tf_op jit(solution)/shard_map/ppermute | solution.py:1025
  142.7 22.9 %collective-permute-start.9 = (bf16[2,64,2048]{2,1,0:T(8,128)(2,1)S(1)}, bf16[2,64,2048]{2,1,0:T(8,128)(2,1)S(1)}, u32[]{:S(2)}, u32[]{:S(2)}) collective-permute-start(bf16[2,64,2048]{2,1,0:T(8,128)(2,1)S(1)} %get-tuple-element.233), channel_id=1, source_target_pairs={{0,4},{2,6},{4,0},{6,2},{1,5},{3,7},{5,1},{7,3},{8,12},{10,14},{12... | collective-permute-start | bytes 1572872 | tf_op jit(solution)/shard_map/ppermute | solution.py:1025
  143.8 21.8 %collective-permute-start.8 = (bf16[2,64,2048]{2,1,0:T(8,128)(2,1)S(1)}, bf16[2,64,2048]{2,1,0:T(8,128)(2,1)S(1)}, u32[]{:S(2)}, u32[]{:S(2)}) collective-permute-start(bf16[2,64,2048]{2,1,0:T(8,128)(2,1)S(1)} %get-tuple-element.234), channel_id=1, source_target_pairs={{0,2},{2,0},{4,6},{6,4},{1,3},{3,1},{5,7},{7,5},{8,10},{10,8},{12,... | collective-permute-start | bytes 1572872 | tf_op jit(solution)/shard_map/ppermute | solution.py:1025
  175.7 268.0 %copy-start.9 = (bf16[1024,16]{1,0:T(8,128)(2,1)}, bf16[1024,16]{1,0:T(8,128)(2,1)S(1)}, u32[]{:S(2)}) copy-start(bf16[1024,16]{1,0:T(8,128)(2,1)S(1)} %convolution_convert_fusion.4.f_low_ref) | copy-start | bytes 98308
  289.8 5.0 collective-permute-start.11
  299.0 115.7 %reduce-scatter.8.cloned.1.call-start = ((), (), s32[]{:S(2)}) async-start(), calls=%async_computation.10 | async-start | bytes 3932160 | tf_op jit(solution)/shard_map/reduce_scatter | solution.py:1109
  316.8 16.0 %collective-permute-start.12 = (bf16[1024,1536]{1,0:T(8,128)(2,1)}, bf16[1024,1536]{1,0:T(8,128)(2,1)S(1)}, u32[]{:S(2)}, u32[]{:S(2)}) collective-permute-start(bf16[1024,1536]{1,0:T(8,128)(2,1)} %convolution_convert_fusion.1), channel_id=1, source_target_pairs={{0,1},{1,0},{2,3},{3,2},{4,5},{5,4},{6,7},{7,6},{8,9},{9,8},{10,11... | collective-permute-start | bytes 9437192 | tf_op jit(solution)/shard_map/ppermute | solution.py:1029
  337.7 137.4 %reduce-scatter.12.cloned.1.call-start = ((), (), s32[]{:S(2)}) async-start(), calls=%async_computation.12 | async-start | bytes 3604480 | tf_op jit(solution)/shard_map/reduce_scatter | solution.py:1109
  412.6 139.7 %reduce-scatter.10.cloned.1.call-start = ((), (), s32[]{:S(2)}) async-start(), calls=%async_computation.11 | async-start | bytes 5242880 | tf_op jit(solution)/shard_map/reduce_scatter | solution.py:1109
  412.6 25.5 %collective-permute-start.13 = (bf16[256,2048]{1,0:T(8,128)(2,1)}, bf16[256,2048]{1,0:T(8,128)(2,1)S(1)}, u32[]{:S(2)}, u32[]{:S(2)}) collective-permute-start(bf16[256,2048]{1,0:T(8,128)(2,1)} %get-tuple-element.132), channel_id=1, source_target_pairs={{0,2},{2,0},{4,6},{6,4},{1,3},{3,1},{5,7},{7,5},{8,10},{10,8},{12,... | collective-permute-start | bytes 3145736 | tf_op jit(solution)/shard_map/ppermute | solution.py:1025
  413.3 24.9 %collective-permute-start.14 = (bf16[256,2048]{1,0:T(8,128)(2,1)}, bf16[256,2048]{1,0:T(8,128)(2,1)}, u32[]{:S(2)}, u32[]{:S(2)}) collective-permute-start(bf16[256,2048]{1,0:T(8,128)(2,1)} %get-tuple-element.133), channel_id=1, source_target_pairs={{0,4},{2,6},{4,0},{6,2},{1,5},{3,7},{5,1},{7,3},{8,12},{10,14},{12... | collective-permute-start | bytes 3145736 | tf_op jit(solution)/shard_map/ppermute | solution.py:1025
  441.4 13.2 %collective-permute-start.15 = (bf16[128,2048]{1,0:T(8,128)(2,1)S(1)}, bf16[128,2048]{1,0:T(8,128)(2,1)S(1)}, u32[]{:S(2)}, u32[]{:S(2)}) collective-permute-start(bf16[128,2048]{1,0:T(8,128)(2,1)S(1)} %get-tuple-element.144), channel_id=1, source_target_pairs={{0,4},{2,6},{4,0},{6,2},{1,5},{3,7},{5,1},{7,3},{8,12},{10,14},{12... | collective-permute-start | bytes 1572872 | tf_op jit(solution)/shard_map/ppermute | solution.py:1025
  442.7 12.0 %collective-permute-start.16 = (bf16[128,2048]{1,0:T(8,128)(2,1)S(1)}, bf16[128,2048]{1,0:T(8,128)(2,1)S(1)}, u32[]{:S(2)}, u32[]{:S(2)}) collective-permute-start(bf16[128,2048]{1,0:T(8,128)(2,1)S(1)} %get-tuple-element.145), channel_id=1, source_target_pairs={{0,2},{2,0},{4,6},{6,4},{1,3},{3,1},{5,7},{7,5},{8,10},{10,8},{12,... | collective-permute-start | bytes 1572872 | tf_op jit(solution)/shard_map/ppermute | solution.py:1025
  473.8 110.7 %reduce-scatter.14.cloned.1.call-start = ((), (), s32[]{:S(2)}) async-start(), calls=%async_computation.13 | async-start | bytes 1310720 | tf_op jit(solution)/shard_map/reduce_scatter | solution.py:1109
  491.3 56.2 %copy-start.18 = (bf16[4,64,1536]{2,1,0:T(8,128)(2,1)S(1)}, bf16[4,64,1536]{2,1,0:T(8,128)(2,1)}, u32[]{:S(2)}) copy-start(bf16[4,64,1536]{2,1,0:T(8,128)(2,1)} %get-tuple-element.166.refs_1_) | copy-start | bytes 2359300
  491.3 56.2 %copy-start.21 = (bf16[4,64,1280]{2,1,0:T(8,128)(2,1)S(1)}, bf16[4,64,1280]{2,1,0:T(8,128)(2,1)}, u32[]{:S(2)}) copy-start(bf16[4,64,1280]{2,1,0:T(8,128)(2,1)} %get-tuple-element.165.refs_0_) | copy-start | bytes 1966084
  549.5 36.8 %copy-start.30 = (bf16[256,2048]{1,0:T(8,128)(2,1)S(1)}, bf16[256,2048]{1,0:T(8,128)(2,1)}, u32[]{:S(2)}) copy-start(bf16[256,2048]{1,0:T(8,128)(2,1)} %get-tuple-element.171) | copy-start | bytes 3145732
  (30 other events, 349.0 us)
Sparse Core Ops, SparseCore 0:
  10.3 83.1 all-gather.4
  95.1 80.5 all-gather.6
  177.3 54.5 all-gather.8
  233.3 63.5 all-gather.10
  299.1 50.6 reduce-scatter.5
  352.0 59.9 reduce-scatter.7
  414.3 56.1 reduce-scatter.11
  473.9 75.4 reduce-scatter.9
  551.9 32.5 reduce-scatter.13
